TPU v7x, 128 devices: a whole 4x4x4 slice. The times are simulated.
128 devices in a mesh: dp: 16 (over z_hi, y, core), tensor: 8 (over z_lo, x).
Axes of the slice: x: 4, y: 4, z: 4 (z_hi: 2, z_lo: 2; z = z_hi * 2 + z_lo), core: 2. Of those that a mesh axis runs over, the one named last changes fastest.
Arguments:
- x_in: bfloat16 [18688, 1024], P(('dp', 'tensor')), may hold values from -6 to 6
- valid_len: int32 [32], P('dp'), may hold values from 480 to 577, as said below
- w_qkv: bfloat16 [2, 1024, 3, 1024], P(None, 'dp', None, 'tensor'), may hold values from -0.1875 to 0.1875
- w_out: bfloat16 [2, 1024, 1024], P(None, 'tensor', 'dp'), may hold values from -0.75 to 0.75
- w_up: bfloat16 [2, 1024, 4096], P(None, 'dp', 'tensor'), may hold values from -0.1875 to 0.1875
- w_down: bfloat16 [2, 4096, 1024], P(None, 'tensor', 'dp'), may hold values from -0.09375 to 0.09375
- norm_gain: float32 [2, 2, 1024], replicated, may hold values from 0.1 to 1.9
- norm_shift: float32 [2, 2, 1024], replicated, may hold values from -3 to 3
- bias: float32 [2, 4, 1024], replicated, may hold values from -3 to 3
- up_bias: float32 [2, 4096], replicated, may hold values from -3 to 3
- cotangent: bfloat16 [18688, 1024], P(('dp', 'tensor')), may hold values from -6 to 6
Outputs:
- out_rows: bfloat16 [18688, 1024], P(('dp', 'tensor'))
- grad_input: float32 [18688, 1024], P(('dp', 'tensor'))
- grad_qkv: float32 [2, 1024, 3, 1024], P(None, 'dp', None, 'tensor')
- grad_out: float32 [2, 1024, 1024], P(None, 'tensor', 'dp')
- grad_up: float32 [2, 1024, 4096], P(None, 'dp', 'tensor')
- grad_down: float32 [2, 4096, 1024], P(None, 'tensor', 'dp')
- grad_gain: float32 [2, 2, 1024], replicated
- grad_shift: float32 [2, 2, 1024], replicated
- grad_bias: float32 [2, 4, 1024], replicated
- grad_up_bias: float32 [2, 4096], replicated
Inputs may be any that keep to these rules, and one draw needn't show every extreme that they name: `valid_len`: the number of valid leading positions of each image; padding follows them; some image has 577 and some has 480.
All inputs are finite; a program needn't handle non-finite values.
Results may differ from a plain program's by a relative error of at most 0.02.
Values may be sent and summed in bfloat16 or wider, within the bound.
A program may use at most 128 MiB of HBM per device.

v0:
```python
import jax
import jax.numpy as jnp
from jax import lax
from jax.sharding import PartitionSpec as P

HEADS = 16
HEAD_DIM = 64
SEQ = 584


EPSILON = 1e-06
NEG_FILL = -1e30


def layer_norm(inputs, gains, offset):
    row_mean = jnp.mean(inputs, axis=-1, keepdims=True)
    centred = inputs - row_mean
    spread = jnp.mean(centred * centred, axis=-1, keepdims=True)
    return centred * lax.rsqrt(spread + EPSILON) * gains + offset


def gelu_exact(values):
    return jax.nn.gelu(values, approximate=False)


def masked_scores(queries, key_rows, length):
    scores = jnp.einsum("qhc,khc->hqk", queries, key_rows, preferred_element_type=jnp.float32)
    scores = scores * HEAD_DIM ** (-0.5)
    key_valid = jnp.arange(key_rows.shape[0]) < length
    return jnp.where(key_valid[None, None, :], scores, NEG_FILL)


def attend_image(packed):
    queries, key_rows, value_rows, length = packed
    scores = masked_scores(queries, key_rows, length)
    row_max = jnp.max(scores, axis=-1, keepdims=True)
    exponent = jnp.exp(scores - row_max)
    row_total = jnp.sum(exponent, axis=-1, keepdims=True)
    weights = (exponent / row_total).astype(jnp.bfloat16)
    attended = jnp.einsum("hqk,khc->qhc", weights, value_rows, preferred_element_type=jnp.float32)
    return (attended.astype(jnp.bfloat16), row_max + jnp.log(row_total))


def attend_back(packed):
    queries, key_rows, value_rows, length, log_total, grad_mixed = packed
    scores = masked_scores(queries, key_rows, length)
    probability = jnp.exp(scores - log_total)
    grad_value = jnp.einsum(
        "hqk,qhc->khc",
        probability.astype(jnp.bfloat16),
        grad_mixed,
        preferred_element_type=jnp.float32,
    )
    grad_prob = jnp.einsum(
        "qhc,khc->hqk", grad_mixed, value_rows, preferred_element_type=jnp.float32
    )
    row_inner = jnp.sum(grad_prob * probability, axis=-1, keepdims=True)
    grad_scores = (probability * (grad_prob - row_inner)).astype(jnp.bfloat16)
    score_scale = HEAD_DIM ** (-0.5)
    grad_query = (
        jnp.einsum("hqk,khc->qhc", grad_scores, key_rows, preferred_element_type=jnp.float32)
        * score_scale
    )
    grad_key = (
        jnp.einsum("hqk,qhc->khc", grad_scores, queries, preferred_element_type=jnp.float32)
        * score_scale
    )
    return (
        grad_query.astype(jnp.bfloat16),
        grad_key.astype(jnp.bfloat16),
        grad_value.astype(jnp.bfloat16),
    )


def spread_rows(rows_local):
    return lax.all_gather(rows_local, "tensor", axis=0, tiled=True)


def sum_rows(partial_rows):
    return lax.psum_scatter(
        partial_rows.astype(jnp.bfloat16), "tensor", scatter_dimension=0, tiled=True
    ).astype(jnp.float32)


def spread_grads(rows_local):
    return lax.all_gather(rows_local, "tensor", axis=0, tiled=True)


def sum_grads(partial_rows):
    return lax.psum_scatter(
        partial_rows.astype(jnp.bfloat16), "tensor", scatter_dimension=0, tiled=True
    ).astype(jnp.float32)


def per_device(
    x_in, valid_len, w_qkv, w_out, w_up, w_down, norm_gain, norm_shift, bias, up_bias, cotangent
):
    tensor_size = lax.axis_size("tensor")
    tensor_rank = lax.axis_index("tensor")
    layers = w_qkv.shape[0]
    width = x_in.shape[1]
    part_cols = w_qkv.shape[3]
    part_hidden = w_up.shape[2]
    full_hidden = up_bias.shape[1]
    heads_here = HEADS // tensor_size
    images = valid_len.shape[0]
    col_start = tensor_rank * part_cols
    hid_start = tensor_rank * part_hidden
    head_shape = (images, SEQ, heads_here, HEAD_DIM)
    state = x_in.astype(jnp.float32)
    saved = []
    for layer in range(layers):
        w_q, w_o, w_u, w_d = (
            lax.all_gather(w_qkv[layer], "dp", axis=0, tiled=True),
            lax.all_gather(w_out[layer], "dp", axis=1, tiled=True),
            lax.all_gather(w_up[layer], "dp", axis=0, tiled=True),
            lax.all_gather(w_down[layer], "dp", axis=1, tiled=True),
        )
        bias_rows = bias[layer]
        normed_one = spread_rows(
            layer_norm(state, norm_gain[layer, 0], norm_shift[layer, 0]).astype(jnp.bfloat16)
        )
        projected = jnp.einsum("rd,dkc->rkc", normed_one, w_q, preferred_element_type=jnp.float32)
        queries = (
            projected[:, 0] + lax.dynamic_slice_in_dim(bias_rows[0], col_start, part_cols)
        ).astype(jnp.bfloat16)
        key_rows = projected[:, 1].astype(jnp.bfloat16)
        value_rows = (
            projected[:, 2] + lax.dynamic_slice_in_dim(bias_rows[1], col_start, part_cols)
        ).astype(jnp.bfloat16)
        queries = queries.reshape(head_shape)
        key_rows = key_rows.reshape(head_shape)
        value_rows = value_rows.reshape(head_shape)
        attended, log_total = lax.map(attend_image, (queries, key_rows, value_rows, valid_len))
        attended = attended.reshape(-1, part_cols)
        branch = sum_rows(jnp.dot(attended, w_o, preferred_element_type=jnp.float32))
        middle = state + (branch + bias_rows[2])
        normed_two = spread_rows(
            layer_norm(middle, norm_gain[layer, 1], norm_shift[layer, 1]).astype(jnp.bfloat16)
        )
        hidden = jnp.dot(normed_two, w_u, preferred_element_type=jnp.float32)
        hidden = hidden + lax.dynamic_slice_in_dim(up_bias[layer], hid_start, part_hidden)
        activated = gelu_exact(hidden).astype(jnp.bfloat16)
        new_state = middle + (
            sum_rows(jnp.dot(activated, w_d, preferred_element_type=jnp.float32)) + bias_rows[3]
        )
        kept_weights = None
        saved.append(
            (
                state,
                normed_one,
                queries,
                key_rows,
                value_rows,
                log_total,
                attended,
                middle,
                normed_two,
                hidden,
                activated,
                kept_weights,
            )
        )
        state = new_state
    gradient = cotangent.astype(jnp.float32)
    summed_grads = [None] * layers
    gain_grads = [None] * layers
    shift_grads = [None] * layers
    bias_grads = [None] * layers
    hidden_bias_grads = [None] * layers
    for layer in reversed(range(layers)):
        (
            layer_in,
            normed_one,
            queries,
            key_rows,
            value_rows,
            log_total,
            attended,
            middle,
            normed_two,
            hidden,
            activated,
            kept_weights,
        ) = saved[layer]
        w_q, w_o, w_u, w_d = (
            lax.all_gather(w_qkv[layer], "dp", axis=0, tiled=True),
            lax.all_gather(w_out[layer], "dp", axis=1, tiled=True),
            lax.all_gather(w_up[layer], "dp", axis=0, tiled=True),
            lax.all_gather(w_down[layer], "dp", axis=1, tiled=True),
        )
        down_bias_grad = jnp.sum(gradient, axis=0)
        grad_down_rows = spread_grads(gradient.astype(jnp.bfloat16))
        grad_w_down = jnp.einsum(
            "rf,rd->fd", activated, grad_down_rows, preferred_element_type=jnp.float32
        )
        grad_act = jnp.einsum("rd,fd->rf", grad_down_rows, w_d, preferred_element_type=jnp.float32)
        gelu_value, gelu_pull = jax.vjp(gelu_exact, hidden)
        grad_hidden = gelu_pull(grad_act)[0].astype(jnp.bfloat16)
        hidden_grad_local = jnp.sum(grad_hidden.astype(jnp.float32), axis=0)
        grad_w_up = jnp.einsum(
            "rd,rf->df", normed_two, grad_hidden, preferred_element_type=jnp.float32
        )
        grad_normed_two = sum_grads(
            jnp.einsum("rf,df->rd", grad_hidden, w_u, preferred_element_type=jnp.float32)
        )
        norm_value, norm_pull = jax.vjp(
            layer_norm, middle, norm_gain[layer, 1], norm_shift[layer, 1]
        )
        grad_mid_norm, gain_two, shift_two = norm_pull(grad_normed_two)
        grad_middle = gradient + grad_mid_norm
        out_bias_grad = jnp.sum(grad_middle, axis=0)
        grad_attn_rows = spread_grads(grad_middle.astype(jnp.bfloat16))
        grad_w_out = jnp.einsum(
            "rc,rd->cd", attended, grad_attn_rows, preferred_element_type=jnp.float32
        )
        grad_mixed = jnp.einsum(
            "rd,cd->rc", grad_attn_rows, w_o, preferred_element_type=jnp.float32
        )
        grad_mixed = grad_mixed.astype(jnp.bfloat16).reshape(head_shape)
        grad_query, grad_key, grad_value = lax.map(
            attend_back, (queries, key_rows, value_rows, valid_len, log_total, grad_mixed)
        )
        grad_projected = jnp.stack(
            [
                grad_query.reshape(-1, part_cols),
                grad_key.reshape(-1, part_cols),
                grad_value.reshape(-1, part_cols),
            ],
            axis=1,
        )
        query_bias_grad = jnp.sum(grad_projected[:, 0].astype(jnp.float32), axis=0)
        value_bias_grad = jnp.sum(grad_projected[:, 2].astype(jnp.float32), axis=0)
        grad_w_qkv = jnp.einsum(
            "rd,rkc->dkc", normed_one, grad_projected, preferred_element_type=jnp.float32
        )
        grad_normed_one = sum_grads(
            jnp.einsum("rkc,dkc->rd", grad_projected, w_q, preferred_element_type=jnp.float32)
        )
        first_value, first_pull = jax.vjp(
            layer_norm, layer_in, norm_gain[layer, 0], norm_shift[layer, 0]
        )
        grad_in_norm, gain_one, shift_one = first_pull(grad_normed_one)
        gradient = grad_middle + grad_in_norm
        zero_width = jnp.zeros((width,), jnp.float32)
        query_full = lax.dynamic_update_slice_in_dim(zero_width, query_bias_grad, col_start, 0)
        value_full = lax.dynamic_update_slice_in_dim(zero_width, value_bias_grad, col_start, 0)
        gain_grads[layer] = jnp.stack([gain_one, gain_two])
        shift_grads[layer] = jnp.stack([shift_one, shift_two])
        bias_grads[layer] = jnp.stack([query_full, value_full, out_bias_grad, down_bias_grad])
        hidden_bias_grads[layer] = lax.dynamic_update_slice_in_dim(
            jnp.zeros((full_hidden,), jnp.float32), hidden_grad_local, hid_start, 0
        )
        layer_grads = (grad_w_qkv, grad_w_out, grad_w_up, grad_w_down)
        summed_grads[layer] = (
            lax.psum_scatter(
                layer_grads[0].astype(jnp.bfloat16), "dp", scatter_dimension=0, tiled=True
            ).astype(jnp.float32),
            lax.psum_scatter(
                layer_grads[1].astype(jnp.bfloat16), "dp", scatter_dimension=1, tiled=True
            ).astype(jnp.float32),
            lax.psum_scatter(
                layer_grads[2].astype(jnp.bfloat16), "dp", scatter_dimension=0, tiled=True
            ).astype(jnp.float32),
            lax.psum_scatter(
                layer_grads[3].astype(jnp.bfloat16), "dp", scatter_dimension=1, tiled=True
            ).astype(jnp.float32),
        )
    grad_qkv = jnp.stack([item[0] for item in summed_grads])
    grad_out = jnp.stack([item[1] for item in summed_grads])
    grad_up = jnp.stack([item[2] for item in summed_grads])
    grad_down = jnp.stack([item[3] for item in summed_grads])
    grad_gain, grad_shift, grad_bias, grad_up_bias = lax.psum(
        (
            jnp.stack(gain_grads),
            jnp.stack(shift_grads),
            jnp.stack(bias_grads),
            jnp.stack(hidden_bias_grads),
        ),
        ("dp", "tensor"),
    )
    return (
        state.astype(jnp.bfloat16),
        gradient,
        grad_qkv,
        grad_out,
        grad_up,
        grad_down,
        grad_gain,
        grad_shift,
        grad_bias,
        grad_up_bias,
    )


def solution(mesh):
    in_specs = (
        P(("dp", "tensor"), None),
        P("dp"),
        P(None, "dp", None, "tensor"),
        P(None, "tensor", "dp"),
        P(None, "dp", "tensor"),
        P(None, "tensor", "dp"),
        P(),
        P(),
        P(),
        P(),
        P(("dp", "tensor"), None),
    )
    out_specs = (
        P(("dp", "tensor"), None),
        P(("dp", "tensor"), None),
        P(None, "dp", None, "tensor"),
        P(None, "tensor", "dp"),
        P(None, "dp", "tensor"),
        P(None, "tensor", "dp"),
        P(),
        P(),
        P(),
        P(),
    )
    return jax.shard_map(
        per_device, mesh=mesh, in_specs=in_specs, out_specs=out_specs, check_vma=False
    )
```

profile of v0, /device:TPU:1, one launch (start us, length us, event | category | flops | bytes accessed | tf_op | source)
XLA Modules:
  0.0 1662.8 jit_solution(4319087858978493921)
XLA Ops:
  19.1 27.8 %all-gather.1 = bf16[1,128,1024]{1,2,0:T(8,128)(2,1)S(1)} all-gather(bf16[1,128,64]{1,2,0:T(8,128)(2,1)S(1)} %get-tuple-element.440), channel_id=3, replica_groups=mesh['dp'=16,'tensor'=8] {'dp'}, dimensions={2}, use_global_device_ids=true | all-gather | bytes 278528 | tf_op jit(solution)/shard_map/all_gather | solution.py:115
  88.9 34.4 %fusion = bf16[152,1024]{1,0:T(8,128)(2,1)} fusion(bf16[1168,1024]{1,0:T(8,128)(2,1)S(1)} %convolution_convert_fusion.5), kind=kCustom, calls=%all-reduce-scatter | all-reduce-scatter fusion | flops 1245185 | bytes 2703872
  134.2 36.6 %all-gather.39.cloned.1.call-done = bf16[8,146,1024]{2,1,0:T(8,128)(2,1)} async-done(((bf16[1,146,1024]{2,1,0:T(8,128)(2,1)}), bf16[8,146,1024]{2,1,0:T(8,128)(2,1)}) %all-gather.39.cloned.1.call-update) | async-done | bytes 2392080 | tf_op jit(solution)/shard_map/all_gather | solution.py:76
  173.8 49.4 %all-gather.29.cloned.1.call-done = bf16[1,1024,512]{2,1,0:T(8,128)(2,1)} async-done(((bf16[1,64,512]{2,1,0:T(8,128)(2,1)}), bf16[1,1024,512]{2,1,0:T(8,128)(2,1)}) %all-gather.29.cloned.1.call-update) | async-done | bytes 1048592 | tf_op jit(solution)/shard_map/all_gather | solution.py:116
  232.6 37.3 %all-gather.31.cloned.1.call-done = bf16[1,512,1024]{1,2,0:T(8,128)(2,1)} async-done(((bf16[1,512,64]{1,2,0:T(8,128)(2,1)}), bf16[1,512,1024]{1,2,0:T(8,128)(2,1)}) %all-gather.31.cloned.1.call-update) | async-done | bytes 1048592 | tf_op jit(solution)/shard_map/all_gather | solution.py:117
  274.0 35.3 %fusion.1 = bf16[152,1024]{1,0:T(8,128)(2,1)S(1)} fusion(bf16[1168,1024]{1,0:T(8,128)(2,1)} %convolution_convert_fusion.3), kind=kCustom, calls=%all-reduce-scatter.1 | all-reduce-scatter fusion | flops 1245185 | bytes 2703872
  388.0 38.3 %fusion.2 = bf16[152,1024]{1,0:T(8,128)(2,1)S(1)} fusion(bf16[1168,1024]{1,0:T(8,128)(2,1)} %convolution_convert_fusion.4), kind=kCustom, calls=%all-reduce-scatter.2 | all-reduce-scatter fusion | flops 1245185 | bytes 2703872
  437.2 35.7 %all-gather.43.cloned.1.call-done = bf16[8,146,1024]{2,1,0:T(8,128)(2,1)} async-done(((bf16[1,146,1024]{2,1,0:T(8,128)(2,1)}), bf16[8,146,1024]{2,1,0:T(8,128)(2,1)}) %all-gather.43.cloned.1.call-update) | async-done | bytes 2392080 | tf_op jit(solution)/shard_map/all_gather | solution.py:76
  475.9 49.5 %all-gather.33.cloned.1.call-done = bf16[1,1024,512]{2,1,0:T(8,128)(2,1)} async-done(((bf16[1,64,512]{2,1,0:T(8,128)(2,1)}), bf16[1,1024,512]{2,1,0:T(8,128)(2,1)}) %all-gather.33.cloned.1.call-update) | async-done | bytes 1048592 | tf_op jit(solution)/shard_map/all_gather | solution.py:116
  535.0 37.2 %all-gather.35.cloned.1.call-done = bf16[1,512,1024]{1,2,0:T(8,128)(2,1)} async-done(((bf16[1,512,64]{1,2,0:T(8,128)(2,1)}), bf16[1,512,1024]{1,2,0:T(8,128)(2,1)}) %all-gather.35.cloned.1.call-update) | async-done | bytes 1048592 | tf_op jit(solution)/shard_map/all_gather | solution.py:117
  581.9 35.2 %fusion.4 = bf16[152,1024]{1,0:T(8,128)(2,1)S(1)} fusion(bf16[1168,1024]{1,0:T(8,128)(2,1)} %convolution_convert_fusion.1), kind=kCustom, calls=%all-reduce-scatter.4 | all-reduce-scatter fusion | flops 1245185 | bytes 2703872
  623.4 40.1 %all-gather.47.cloned.1.call-done = bf16[8,146,1024]{2,1,0:T(8,128)(2,1)} async-done(((bf16[1,146,1024]{2,1,0:T(8,128)(2,1)}), bf16[8,146,1024]{2,1,0:T(8,128)(2,1)}) %all-gather.47.cloned.1.call-update) | async-done | bytes 2392080 | tf_op jit(solution)/shard_map/all_gather | solution.py:86
  710.6 32.7 %fusion.5 = bf16[152,1024]{1,0:T(8,128)(2,1)} fusion(bf16[1168,1024]{1,0:T(8,128)(2,1)} %bitcast_convert_fusion.1), kind=kCustom, calls=%all-reduce-scatter.5 | all-reduce-scatter fusion | flops 1245185 | bytes 2703872
  756.8 46.4 %all-gather.49.cloned.1.call-done = bf16[8,146,1024]{2,1,0:T(8,128)(2,1)} async-done(((bf16[1,146,1024]{2,1,0:T(8,128)(2,1)}), bf16[8,146,1024]{2,1,0:T(8,128)(2,1)}) %all-gather.49.cloned.1.call-update) | async-done | bytes 2392080 | tf_op jit(solution)/shard_map/all_gather | solution.py:86
  816.0 32.9 %fusion.6 = bf16[152,1024]{1,0:T(8,128)(2,1)} fusion(bf16[1168,1024]{1,0:T(8,128)(2,1)} %convolution_convert_fusion), kind=kCustom, calls=%all-reduce-scatter.6 | all-reduce-scatter fusion | flops 1245185 | bytes 2703872
  919.2 62.8 %reduce-scatter.39.cloned.1.call-done = bf16[512,64]{0,1:T(8,128)(2,1)} async-done(((bf16[512,1024]{0,1:T(8,128)(2,1)}), bf16[512,64]{0,1:T(8,128)(2,1)}) %reduce-scatter.39.cloned.1.call-update) | async-done | bytes 65552 | tf_op jit(solution)/shard_map/reduce_scatter | solution.py:265
  982.0 70.0 %reduce-scatter.37.cloned.1.call-done = bf16[512,64]{0,1:T(8,128)(2,1)} async-done(((bf16[512,1024]{0,1:T(8,128)(2,1)}), bf16[512,64]{0,1:T(8,128)(2,1)}) %reduce-scatter.37.cloned.1.call-update) | async-done | bytes 65552 | tf_op jit(solution)/shard_map/reduce_scatter | solution.py:265
  1053.6 67.9 %reduce-scatter.35.cloned.1.call-done = bf16[64,512]{1,0:T(8,128)(2,1)} async-done(((bf16[1024,512]{1,0:T(8,128)(2,1)}), bf16[64,512]{1,0:T(8,128)(2,1)}) %reduce-scatter.35.cloned.1.call-update) | async-done | bytes 65552 | tf_op jit(solution)/shard_map/reduce_scatter | solution.py:262
  1121.5 70.0 %reduce-scatter.33.cloned.1.call-done = bf16[64,512]{1,0:T(8,128)(2,1)} async-done(((bf16[1024,512]{1,0:T(8,128)(2,1)}), bf16[64,512]{1,0:T(8,128)(2,1)}) %reduce-scatter.33.cloned.1.call-update) | async-done | bytes 65552 | tf_op jit(solution)/shard_map/reduce_scatter | solution.py:262
  1211.1 58.0 %fusion.193 = (bf16[152,1024]{1,0:T(8,128)(2,1)S(1)}, bf16[152,1024]{1,0:T(8,128)(2,1)S(1)}) fusion(bf16[1168,1024]{1,0:T(8,128)(2,1)} %convolution_convert_fusion.2, bf16[1168,1024]{1,0:T(8,128)(2,1)} %bitcast_convert_fusion), kind=kCustom, calls=%all-reduce-scatter.8 | all-reduce-scatter fusion | flops 2490369 | bytes 5407232
  1297.7 68.1 %reduce-scatter.29.cloned.1.call-done = bf16[128,64]{0,1:T(8,128)(2,1)} async-done(((bf16[128,1024]{0,1:T(8,128)(2,1)}), bf16[128,64]{0,1:T(8,128)(2,1)}) %reduce-scatter.29.cloned.1.call-update) | async-done | bytes 16400 | tf_op jit(solution)/shard_map/reduce_scatter | solution.py:259
  1367.1 67.4 %reduce-scatter.27.cloned.1.call-done = bf16[64,3,128]{2,0,1:T(8,128)(2,1)} async-done(((bf16[1024,3,128]{2,0,1:T(8,128)(2,1)}), bf16[64,3,128]{2,0,1:T(8,128)(2,1)}) %reduce-scatter.27.cloned.1.call-update) | async-done | bytes 49168 | tf_op jit(solution)/shard_map/reduce_scatter | solution.py:256
  1434.5 68.5 %reduce-scatter.25.cloned.1.call-done = bf16[64,3,128]{2,0,1:T(8,128)(2,1)} async-done(((bf16[1024,3,128]{2,0,1:T(8,128)(2,1)}), bf16[64,3,128]{2,0,1:T(8,128)(2,1)}) %reduce-scatter.25.cloned.1.call-update) | async-done | bytes 49168 | tf_op jit(solution)/shard_map/reduce_scatter | solution.py:256
  1504.6 145.6 %all-reduce.20.cloned.1.call-done = (f32[2,2,1024]{2,1,0:T(2,128)}, f32[2,2,1024]{2,1,0:T(2,128)}, f32[2,4,1024]{2,1,0:T(4,128)}, f32[2,4096]{1,0:T(2,128)}) async-done(((f32[2,2,1024]{2,1,0:T(2,128)}, f32[2,2,1024]{2,1,0:T(2,128)}, f32[2,4,1024]{2,1,0:T(4,128)}, f32[2,4096]{1,0:T(2,128)}), (f32[2,2,1024]{2,1,0:T(2,128)}, f32[2,2,1024]{2,1,0:T(2,128)}, f32[2,4,1024]{2,1,0:T(4,128)}, ...) | async-done | bytes 98320 | tf_op jit(solution)/shard_map/psum | solution.py:273
  (542 shorter events, 439.2 us)
Async XLA Ops:
  7.2 63.8 %all-gather.37.cloned.1.call-start = ((), (), s32[]{:S(2)}) async-start(), calls=%async_computation.20 | async-start | bytes 2801664 | tf_op jit(solution)/shard_map/all_gather | solution.py:76
  14.8 155.9 %all-gather.39.cloned.1.call-start = ((), (), s32[]{:S(2)}) async-start(), calls=%async_computation.21 | async-start | bytes 2801664 | tf_op jit(solution)/shard_map/all_gather | solution.py:76
  124.3 3.9 collective-permute-start
  131.8 91.5 %all-gather.29.cloned.1.call-start = ((), (), s32[]{:S(2)}) async-start(), calls=%async_computation.16 | async-start | bytes 1114112 | tf_op jit(solution)/shard_map/all_gather | solution.py:116
  132.5 137.4 %all-gather.31.cloned.1.call-start = ((), (), s32[]{:S(2)}) async-start(), calls=%async_computation.17 | async-start | bytes 1114112 | tf_op jit(solution)/shard_map/all_gather | solution.py:117
  133.3 235.3 %all-gather.41.cloned.1.call-start = ((), (), s32[]{:S(2)}) async-start(), calls=%async_computation.22 | async-start | bytes 2801664 | tf_op jit(solution)/shard_map/all_gather | solution.py:76
  314.3 119.8 %all-gather.45.cloned.1.call-start = ((), (), s32[]{:S(2)}) async-start(), calls=%async_computation.24 | async-start | bytes 2801664 | tf_op jit(solution)/shard_map/all_gather | solution.py:86
  314.9 158.0 %all-gather.43.cloned.1.call-start = ((), (), s32[]{:S(2)}) async-start(), calls=%async_computation.23 | async-start | bytes 2801664 | tf_op jit(solution)/shard_map/all_gather | solution.py:76
  431.5 93.9 %all-gather.33.cloned.1.call-start = ((), (), s32[]{:S(2)}) async-start(), calls=%async_computation.18 | async-start | bytes 1114112 | tf_op jit(solution)/shard_map/all_gather | solution.py:116
  432.2 140.0 %all-gather.35.cloned.1.call-start = ((), (), s32[]{:S(2)}) async-start(), calls=%async_computation.19 | async-start | bytes 1114112 | tf_op jit(solution)/shard_map/all_gather | solution.py:117
  432.9 230.5 %all-gather.47.cloned.1.call-start = ((), (), s32[]{:S(2)}) async-start(), calls=%async_computation.25 | async-start | bytes 2801664 | tf_op jit(solution)/shard_map/all_gather | solution.py:86
  623.1 180.1 %all-gather.49.cloned.1.call-start = ((), (), s32[]{:S(2)}) async-start(), calls=%async_computation.26 | async-start | bytes 2801664 | tf_op jit(solution)/shard_map/all_gather | solution.py:86
  756.7 153.0 %all-gather.51.cloned.1.call-start = ((), (), s32[]{:S(2)}) async-start(), calls=%async_computation.27 | async-start | bytes 2801664 | tf_op jit(solution)/shard_map/all_gather | solution.py:86
  862.7 119.3 %reduce-scatter.39.cloned.1.call-start = ((), (), s32[]{:S(2)}) async-start(), calls=%async_computation.15 | async-start | bytes 1114112 | tf_op jit(solution)/shard_map/reduce_scatter | solution.py:265
  867.4 184.5 %reduce-scatter.37.cloned.1.call-start = ((), (), s32[]{:S(2)}) async-start(), calls=%async_computation.14 | async-start | bytes 1114112 | tf_op jit(solution)/shard_map/reduce_scatter | solution.py:265
  872.1 249.3 %reduce-scatter.35.cloned.1.call-start = ((), (), s32[]{:S(2)}) async-start(), calls=%async_computation.13 | async-start | bytes 1114112 | tf_op jit(solution)/shard_map/reduce_scatter | solution.py:262
  876.7 314.7 %reduce-scatter.33.cloned.1.call-start = ((), (), s32[]{:S(2)}) async-start(), calls=%async_computation.12 | async-start | bytes 1114112 | tf_op jit(solution)/shard_map/reduce_scatter | solution.py:262
  881.4 416.3 %reduce-scatter.31.cloned.1.call-start = ((), (), s32[]{:S(2)}) async-start(), calls=%async_computation.11 | async-start | bytes 278528 | tf_op jit(solution)/shard_map/reduce_scatter | solution.py:259
  889.4 476.4 %reduce-scatter.29.cloned.1.call-start = ((), (), s32[]{:S(2)}) async-start(), calls=%async_computation.10 | async-start | bytes 278528 | tf_op jit(solution)/shard_map/reduce_scatter | solution.py:259
  913.7 520.9 %reduce-scatter.27.cloned.1.call-start = ((), (), s32[]{:S(2)}) async-start(), calls=%async_computation.9 | async-start | bytes 835584 | tf_op jit(solution)/shard_map/reduce_scatter | solution.py:256
  918.4 584.7 %reduce-scatter.25.cloned.1.call-start = ((), (), s32[]{:S(2)}) async-start(), calls=%async_computation.8 | async-start | bytes 835584 | tf_op jit(solution)/shard_map/reduce_scatter | solution.py:256
  1269.6 9.2 collective-permute-start.7
  1271.9 8.2 collective-permute-start.3
  1278.1 372.1 %all-reduce.20.cloned.1.call-start = ((), (), s32[]{:S(2)}) async-start(), calls=%async_computation.28 | async-start | bytes 196608 | tf_op jit(solution)/shard_map/psum | solution.py:273
  (108 other events, 2400.5 us)
Sparse Core Ops, SparseCore 0:
  15.0 43.2 all-gather.36
  131.9 38.7 all-gather.38
  173.8 49.4 all-gather.28
  226.1 43.7 all-gather.30
  314.4 40.7 all-gather.40
  356.7 44.2 all-gather.44
  431.6 41.2 all-gather.42
  475.9 49.4 all-gather.32
  528.4 43.7 all-gather.34
  623.3 40.1 all-gather.46
  756.9 46.2 all-gather.48
  862.8 46.8 all-gather.50
  913.6 68.3 reduce-scatter.38
  986.2 65.7 reduce-scatter.36
  1055.6 65.7 reduce-scatter.34
  1125.6 65.7 reduce-scatter.32
  1195.0 102.6 reduce-scatter.30
  1301.7 64.0 reduce-scatter.28
  1369.5 64.9 reduce-scatter.26
  1438.1 64.9 reduce-scatter.24
  1509.6 140.4 all-reduce.19
where the time goes:
time: 1670 us; the launch traced here: 1660 us
  waiting for transfers between devices  998 us (60%)
  blocking collectives  369 us (22%)
  matrix products  116 us (7%)
  local copies, waits for them, and re-layouts  102 us (6%)
  other arithmetic  44.9 us (3%)
  between operations  17.1 us (1%)
    unnamed x7, blocking collectives  267 us
    psum x1, waiting for transfers between devices, per_device(): lax.psum((jnp.stack(gain_grads), jnp.stack(shift_grads), jnp.stack(bias_g...  146 us
    reduce_scatter x2, waiting for transfers between devices, per_device(): lax.psum_scatter(layer_grads[2].astype(jnp.bfloat16), 'dp', scatter_dimen...  138 us
    reduce_scatter x2, waiting for transfers between devices, per_device(): lax.psum_scatter(layer_grads[0].astype(jnp.bfloat16), 'dp', scatter_dimen...  136 us
    reduce_scatter x2, waiting for transfers between devices, per_device(): lax.psum_scatter(layer_grads[3].astype(jnp.bfloat16), 'dp', scatter_dimen...  133 us
    all_gather x4, waiting for transfers between devices, spread_grads(): return lax.all_gather(rows_local, 'tensor', axis=0, tiled=True)  107 us
    all_gather x2, waiting for transfers between devices, per_device(): lax.all_gather(w_up[layer], 'dp', axis=0, tiled=True)  98.9 us
    reduce_scatter x2, waiting for transfers between devices, per_device(): lax.psum_scatter(layer_grads[1].astype(jnp.bfloat16), 'dp', scatter_dimen...  81.9 us
  transfers between devices with their start and end apart: 29, of which 24 were waited for; matrix products, arithmetic and copies ran while one was open for 13% of the time, Pallas kernels for 0%

commit v1 on v0

v1 whole, which is shorter than its diff:
```python
import functools

import jax
import jax.numpy as jnp
from jax import lax
from jax.experimental import pallas as pl
from jax.experimental.pallas import tpu as pltpu
from jax.sharding import PartitionSpec as P

MESH = pl.DeviceIdType.MESH
F32, BF16 = jnp.float32, jnp.bfloat16

D = 1024
ROWS = 146
PAD = 160
COLS = 128
HEAD = 64
HID = 512
MEMBERS = 8
WCOLS = 1536
EPSILON = 1e-06
NEG_FILL = -1e30
VMEM_BYTES = 60 * 1024 * 1024

NN = (((1,), (0,)), ((), ()))
NT = (((1,), (1,)), ((), ()))
TN = (((0,), (0,)), ((), ()))


def dot(a, b, dims=NN):
    return lax.dot_general(a, b, dims, preferred_element_type=F32)


class Place:
    def __init__(self):
        self.dp = lax.axis_index("dp")
        self.tensor = lax.axis_index("tensor")
        self.core = self.dp % 2
        self.pair = self.dp // 2
        self.zlo = self.tensor // 4
        self.x = self.tensor % 4
        self.slot = self.core * 4 + self.x
        self.group = self.pair * 2 + self.zlo

    def peer(self, core, x):
        return {"dp": self.pair * 2 + core, "tensor": self.zlo * 4 + x}

    def sibling(self):
        return self.peer(1 - self.core, self.x)


def greet(me, plane):
    barrier = pltpu.get_barrier_semaphore()

    def member(i, carry):
        pl.semaphore_signal(
            barrier,
            inc=1,
            device_id=me.peer((me.core + i // 4) % 2, (me.x + i) % 4),
            device_id_type=MESH,
        )
        return carry

    lax.fori_loop(1, MEMBERS, member, 0)
    count = MEMBERS - 1
    if plane:

        def other(i, carry):
            pair = (me.pair + i // 4) % 8
            zlo = (me.zlo + (i // 2) % 2) % 2
            pl.semaphore_signal(
                barrier,
                inc=1,
                device_id={"dp": pair * 2 + i % 2, "tensor": zlo * 4 + me.x},
                device_id_type=MESH,
            )
            return carry

        lax.fori_loop(2, 32, other, 0)
        count += 30
    pl.semaphore_wait(barrier, count)


def remote(src, dst, send, recv, device):
    return pltpu.make_async_remote_copy(
        src_ref=src,
        dst_ref=dst,
        send_sem=send,
        recv_sem=recv,
        device_id=device,
        device_id_type=MESH,
    )


def near(o):
    return o + (o // 2) * (5 - 2 * o)


def gather_start(me, g, send, recv):
    own = g.at[me.slot]
    remote(own, own, send.at[4], recv.at[4], me.sibling()).start()
    for dx in (1, 3, 2):
        remote(own, own, send.at[dx], recv.at[dx], me.peer(me.core, (me.x + dx) % 4)).start()


def gather_run(me, g, send, recv, consume):
    def step(i, carry):
        dx, dc = near(i // 2), i % 2
        k = dc * 4 + dx
        slot = ((me.core + dc) % 2) * 4 + (me.x + 4 - dx) % 4
        block = g.at[slot]

        @pl.when(i > 0)
        def _():
            remote(block, block, send.at[k], recv.at[k], me.sibling()).wait_recv()

        @pl.when((dc == 0) & (i > 0))
        def _():
            remote(block, block, send.at[4 + dx], recv.at[4 + dx], me.sibling()).start()

        consume(slot)
        return carry

    lax.fori_loop(0, MEMBERS, step, 0)


def gather_end(me, g, send, recv):
    def step(k, carry):
        block = g.at[0]
        remote(block, block, send.at[k], recv.at[k], me.sibling()).wait_send()
        return carry

    lax.fori_loop(1, MEMBERS, step, 0)


GATHER_SEMS = [pltpu.SemaphoreType.DMA((8,)), pltpu.SemaphoreType.DMA((8,))]

SUM_SCRATCH = [
    pltpu.VMEM((4, PAD, D), BF16),
    pltpu.VMEM((4, PAD, D), BF16),
    pltpu.VMEM((3, PAD, D), BF16),
    pltpu.VMEM((3, PAD, D), BF16),
    pltpu.VMEM((PAD, D), F32),
    pltpu.SemaphoreType.DMA((4,)),
    pltpu.SemaphoreType.DMA((4,)),
    pltpu.SemaphoreType.DMA((3,)),
    pltpu.SemaphoreType.DMA((3,)),
]


def sum_rows(me, produce, bufs, fill=None):
    s1, r1, s2, r2, acc, ss1, rs1, ss2, rs2 = bufs
    sibling = me.sibling()

    def to_sibling(i):
        return remote(s1.at[i], r1.at[i], ss1.at[i], rs1.at[i], sibling)

    def to_chip(i):
        peer = me.peer(me.core, (me.x + i + 1) % 4)
        return remote(s2.at[i], r2.at[i], ss2.at[i], rs2.at[i], peer)

    def first(i, carry):
        s1[i] = produce((1 - me.core) * 4 + (me.x + i + 1) % 4).astype(BF16)
        to_sibling(i).start()
        return carry

    lax.fori_loop(0, 4, first, 0)

    def second(i, carry):
        part = produce(me.core * 4 + (me.x + i + 1) % 4)
        to_sibling(i).wait_recv()
        s2[i] = (part + r1[i].astype(F32)).astype(BF16)
        to_chip(i).start()
        return carry

    lax.fori_loop(0, 3, second, 0)
    part = produce(me.slot)
    to_sibling(3).wait_recv()
    acc[...] = part + r1[3].astype(F32)
    if fill is not None:
        fill()
    for i in range(3):
        to_chip(i).wait_recv()
    total = acc[...] + r2[0].astype(F32) + r2[1].astype(F32) + r2[2].astype(F32)
    for i in range(4):
        to_sibling(i).wait_send()
    for i in range(3):
        to_chip(i).wait_send()
    return total


PLANE_SEMS = [pltpu.SemaphoreType.DMA((16,)), pltpu.SemaphoreType.DMA((16,))]


def weights_copy(me, i, shard, full, send, recv):
    pair, zlo = (me.pair + i // 2) % 8, (me.zlo + i) % 2
    device = {"dp": pair * 2 + me.zlo, "tensor": zlo * 4 + me.x}
    return remote(shard, full.at[me.dp], send.at[i], recv.at[me.dp], device)


def weights_start(me, shard, full, send, recv):
    def step(i, carry):
        weights_copy(me, i, shard, full, send, recv).start()
        return carry

    own = me.core == me.zlo

    @pl.when(own)
    def _():
        pltpu.make_async_copy(shard, full.at[me.dp], recv.at[me.dp]).start()

    @pl.when(jnp.logical_not(own))
    def _():
        weights_copy(me, 0, shard, full, send, recv).start()

    lax.fori_loop(1, 16, step, 0)


def weights_arrived(me, shard, full, send, recv):
    def step(i, carry):
        remote(shard, full.at[i], send.at[i], recv.at[i], me.sibling()).wait_recv()
        return carry

    lax.fori_loop(0, 16, step, 0)


def weights_sent(me, shard, full, send, recv):
    @pl.when(me.core != me.zlo)
    def _():
        weights_copy(me, 0, shard, full, send, recv).wait_send()

    def step(i, carry):
        weights_copy(me, i, shard, full, send, recv).wait_send()
        return carry

    lax.fori_loop(1, 16, step, 0)


def grads_copy(me, i, part, land, send, recv):
    to = (me.dp + i) % 16
    device = {"dp": to, "tensor": me.slot}
    return remote(part.at[to], land.at[me.group], send.at[i], recv.at[me.group], device)


def grads_start(me, part, land, send, recv):
    own = me.zlo == me.core

    @pl.when(own)
    def _():
        pltpu.make_async_copy(part.at[me.dp], land.at[me.group], recv.at[me.group]).start()

    @pl.when(jnp.logical_not(own))
    def _():
        grads_copy(me, 0, part, land, send, recv).start()

    def step(i, carry):
        grads_copy(me, i, part, land, send, recv).start()
        return carry

    lax.fori_loop(1, 16, step, 0)


def grads_end(me, part, land, send, recv, out):
    def arrived(i, carry):
        remote(part.at[0], land.at[i], send.at[i], recv.at[i], me.sibling()).wait_recv()
        return carry

    lax.fori_loop(0, 16, arrived, 0)

    @pl.when(me.zlo != me.core)
    def _():
        grads_copy(me, 0, part, land, send, recv).wait_send()

    def sent(i, carry):
        grads_copy(me, i, part, land, send, recv).wait_send()
        return carry

    lax.fori_loop(1, 16, sent, 0)
    total = land[0].astype(F32)
    for i in range(1, 16):
        total = total + land[i].astype(F32)
    out[...] = total


def normalized(rows):
    centred = rows - jnp.mean(rows, axis=-1, keepdims=True)
    scale = lax.rsqrt(jnp.mean(centred * centred, axis=-1, keepdims=True) + EPSILON)
    return centred * scale, scale


def layer_norm(rows, gain, shift):
    return normalized(rows)[0] * gain + shift


def layer_norm_back(rows, gain, grad):
    unit, scale = normalized(rows)
    inner = grad * gain
    mean_one = jnp.mean(inner, axis=-1, keepdims=True)
    mean_two = jnp.mean(inner * unit, axis=-1, keepdims=True)
    back = scale * (inner - mean_one - unit * mean_two)
    return back, jnp.sum(grad * unit, axis=0, keepdims=True), jnp.sum(grad, axis=0, keepdims=True)


def erf(v):
    v = jnp.clip(v, -4.0, 4.0)
    s = v * v
    top = F32(-2.72614225801306e-10)
    for a in (
        2.77068142495902e-08,
        -2.10102402082508e-06,
        -5.69250639462346e-05,
        -7.34990630326855e-04,
        -2.95459980854025e-03,
        -1.60960333262415e-02,
    ):
        top = top * s + F32(a)
    low = F32(-1.45660718464996e-05)
    for b in (
        -2.13374055278905e-04,
        -1.68282697438203e-03,
        -7.37332916720468e-03,
        -1.42647390514189e-02,
    ):
        low = low * s + F32(b)
    return v * top / low


def normal_below(v):
    return 0.5 * (1.0 + erf(v * F32(0.7071067811865476)))


def gelu_slope(v):
    return normal_below(v) + v * jnp.exp(-0.5 * v * v) * F32(0.3989422804014327)


def weight_grad(left, right, out, at, width):
    def tile(i, carry):
        a = left[:, :, pl.ds(pl.multiple_of(i * 256, 256), 256)].reshape(MEMBERS * PAD, 256)
        b = right[...].reshape(MEMBERS * PAD, width)
        block = dot(a, b, TN).astype(BF16).reshape(4, 64, width)
        out[pl.ds(i * 4, 4), :, at : at + width] = block
        return carry

    lax.fori_loop(0, D // 256, tile, 0)


def columns(w, at, width):
    return w[:, :, at : at + width].reshape(D, width)


def column_sum(ref):
    def step(i, total):
        return total + jnp.sum(ref[i].astype(F32), axis=0, keepdims=True)

    return lax.fori_loop(0, MEMBERS, step, jnp.zeros((1, ref.shape[2]), F32))


def call(kernel, outs, scratch, collective_id, args, flops):
    return pl.pallas_call(
        kernel,
        out_shape=[jax.ShapeDtypeStruct(s, t) for s, t in outs],
        in_specs=[pl.BlockSpec(memory_space=pltpu.VMEM)] * len(args),
        out_specs=[pl.BlockSpec(memory_space=pltpu.VMEM)] * len(outs),
        scratch_shapes=scratch,
        compiler_params=pltpu.CompilerParams(
            collective_id=collective_id, has_side_effects=True, vmem_limit_bytes=VMEM_BYTES
        ),
        cost_estimate=pl.CostEstimate(flops=flops, bytes_accessed=1 << 20, transcendentals=0),
    )(*args)


def project(me, g, w, bias, qkv):
    def consume(slot):
        qkv[slot] = (dot(g[slot], columns(w, 0, 384)) + bias[...]).astype(BF16)

    return consume


def enter_kernel(x, shard, gain, shift, qbias, qkv, normed, w, *sems):
    gs, gr, ws, wr = sems
    me = Place()
    greet(me, True)
    weights_start(me, shard, w, ws, wr)
    normed[me.slot] = layer_norm(x[...].astype(F32), gain[...], shift[...]).astype(BF16)
    gather_start(me, normed, gs, gr)
    weights_arrived(me, shard, w, ws, wr)
    gather_run(me, normed, gs, gr, project(me, normed, w, qbias, qkv))
    gather_end(me, normed, gs, gr)
    weights_sent(me, shard, w, ws, wr)


def forward_rest(me, attended, state, w, gain, shift, bias_out, up_bias, middle, normed, hidden, act, sum1, sum2, gather):
    def out_product(slot):
        return dot(attended[slot], columns(w, 384, 128), NT)

    branch = sum_rows(me, out_product, sum1)
    middle[...] = state[...].astype(F32) + (branch + bias_out[...])
    normed[me.slot] = layer_norm(middle[...], gain[...], shift[...]).astype(BF16)
    gs, gr = gather
    gather_start(me, normed, gs, gr)

    def consume(slot):
        h = dot(normed[slot], columns(w, 512, 512)) + up_bias[...]
        hidden[slot] = h
        act[slot] = (h * normal_below(h)).astype(BF16)

    gather_run(me, normed, gs, gr, consume)

    def down_product(slot):
        return dot(act[slot], columns(w, 1024, 512), NT)

    total = sum_rows(me, down_product, sum2)
    gather_end(me, normed, gs, gr)
    return middle[...] + total


def between_kernel(
    attended, state, w, shard, gain, shift, bias_out, up_bias, bias_down, gain_next, shift_next, qbias,
    middle, normed_two, hidden, act, new_state, normed_next, qkv, w_next, *scratch,
):
    sum1, sum2, g1, g2, wsem = scratch[0:9], scratch[9:18], scratch[18:20], scratch[20:22], scratch[22:24]
    me = Place()
    greet(me, True)
    weights_start(me, shard, w_next, *wsem)
    new_state[...] = (
        forward_rest(
            me, attended, state, w, gain, shift, bias_out, up_bias, middle, normed_two, hidden, act, sum1, sum2, g1
        )
        + bias_down[...]
    )
    normed_next[me.slot] = layer_norm(new_state[...], gain_next[...], shift_next[...]).astype(BF16)
    gather_start(me, normed_next, *g2)
    weights_arrived(me, shard, w_next, *wsem)
    gather_run(me, normed_next, *g2, project(me, normed_next, w_next, qbias, qkv))
    gather_end(me, normed_next, *g2)
    weights_sent(me, shard, w_next, *wsem)


def backward_rest(
    me, g_own, g_rows, w, hidden, act, normed, middle, gain, grad_hid, dw, grad_mid, g_attn, grad_att, wide, row, up_sum,
    gather1, sums, gather2,
):
    def consume(slot):
        grad_act = dot(g_rows[slot], columns(w, 1024, 512))
        grad_hid[slot] = (grad_act * gelu_slope(hidden[slot])).astype(BF16)

    gather_run(me, g_rows, *gather1, consume)

    def up_back(slot):
        return dot(grad_hid[slot], columns(w, 512, 512), NT)

    def fill():
        weight_grad(g_rows, act, dw, 512, 512)
        up_sum[...] = column_sum(grad_hid)

    grad = sum_rows(me, up_back, sums, fill)
    gather_end(me, g_rows, *gather1)
    back, gain_sum, shift_sum = layer_norm_back(middle[...], gain[...], grad)
    mid = g_own[...].astype(F32) + back
    grad_mid[...] = mid
    g_attn[me.slot] = mid.astype(BF16)
    gather_start(me, g_attn, *gather2)
    wide[row : row + 1] = jnp.sum(g_own[...].astype(F32), axis=0, keepdims=True)
    wide[row + 1 : row + 2] = gain_sum
    wide[row + 2 : row + 3] = shift_sum
    wide[row + 3 : row + 4] = jnp.sum(mid, axis=0, keepdims=True)
    weight_grad(normed, grad_hid, dw, 0, 512)

    def att_back(slot):
        grad_att[slot] = dot(g_attn[slot], columns(w, 384, 128)).astype(BF16)

    gather_run(me, g_attn, *gather2, att_back)
    gather_end(me, g_attn, *gather2)


def turn_kernel(
    attended, state, w, cot, gain, shift, bias_out, up_bias, bias_down,
    out_rows, dw, grad_mid, g_attn, grad_att, wide, up_sum, *scratch,
):
    sum1, sum2, sum3 = scratch[0:9], scratch[9:18], scratch[18:27]
    g1, g2, g3 = scratch[27:29], scratch[29:31], scratch[31:33]
    middle, normed, hidden, act, g_rows, grad_hid = scratch[33:39]
    me = Place()
    greet(me, False)
    g_rows[me.slot] = cot[...]
    gather_start(me, g_rows, *g2)
    total = forward_rest(
        me, attended, state, w, gain, shift, bias_out, up_bias, middle, normed, hidden, act, sum1, sum2, g1
    )
    out_rows[...] = (total + bias_down[...]).astype(BF16)
    wide[...] = jnp.zeros_like(wide)
    backward_rest(
        me, cot, g_rows, w, hidden, act, normed, middle, gain, grad_hid, dw, grad_mid, g_attn, grad_att, wide, 0, up_sum,
        g2, sum3, g3,
    )


def first_back(me, grad_qkv, normed_one, w, g_attn, attended, state, grad_mid, gain, dwb, wide, row, q_sum, sums, more):
    def back_product(slot):
        return dot(grad_qkv[slot], columns(w, 0, 384), NT)

    def fill():
        weight_grad(normed_one, grad_qkv, dwb, 0, 384)
        weight_grad(g_attn, attended, dwb, 384, 128)
        more()
        q_sum[...] = column_sum(grad_qkv)

    grad = sum_rows(me, back_product, sums, fill)
    back, gain_sum, shift_sum = layer_norm_back(state[...].astype(F32), gain[...], grad)
    wide[row : row + 1] = gain_sum
    wide[row + 1 : row + 2] = shift_sum
    return grad_mid[...] + back


def back_kernel(
    grad_qkv, normed_one, w, g_attn_one, attended_one, state, grad_mid_one, gain_one, dwa_one,
    w_low, hidden, act, normed_two, middle, gain_two,
    suma, sumb, dw, grad_mid, g_attn, grad_att, wide, up_sum, q_sum, *scratch,
):
    sum1, sum2 = scratch[0:9], scratch[9:18]
    g2, g3 = scratch[18:20], scratch[20:22]
    pa, pb = scratch[22:24], scratch[24:26]
    landa, landb, dwb, gradient, g_rows, grad_hid = scratch[26:32]
    me = Place()
    greet(me, True)
    grads_start(me, dwa_one, landa, *pa)
    wide[...] = jnp.zeros_like(wide)

    def more():
        grads_start(me, dwb, landb, *pb)

    gradient[...] = first_back(
        me, grad_qkv, normed_one, w, g_attn_one, attended_one, state, grad_mid_one, gain_one, dwb, wide, 0, q_sum,
        sum1, more,
    )
    g_rows[me.slot] = gradient[...].astype(BF16)
    gather_start(me, g_rows, *g2)
    backward_rest(
        me, gradient, g_rows, w_low, hidden, act, normed_two, middle, gain_two, grad_hid, dw, grad_mid, g_attn,
        grad_att, wide, 2, up_sum, g2, sum2, g3,
    )
    grads_end(me, dwa_one, landa, *pa, suma)
    grads_end(me, dwb, landb, *pb, sumb)


def vectors_start(me, wide, va, vl, send, recv):
    for s in range(MEMBERS):
        va[s] = wide[:, s * 128 : (s + 1) * 128]

    def step(i, carry):
        core, x = (me.core + i // 4) % 2, (me.x + i) % 4
        remote(va.at[core * 4 + x], vl.at[i], send.at[i], recv.at[i], me.peer(core, x)).start()
        return carry

    lax.fori_loop(1, MEMBERS, step, 0)


def vectors_end(me, narrow, va, vl, send, recv, vb, piece, send2, recv2, out, send3, recv3):
    total = va[me.slot]
    for i in range(1, MEMBERS):
        remote(va.at[0], vl.at[i], send.at[i], recv.at[i], me.sibling()).wait()
        total = total + vl[i]
    piece[0:16] = total
    piece[16:32] = narrow[...]

    def to_group(i):
        pair, zlo = (me.pair + i // 2) % 8, (me.zlo + i) % 2
        device = {"dp": pair * 2 + me.core, "tensor": zlo * 4 + me.x}
        return remote(piece, vb.at[me.group], send2.at[i], recv2.at[me.group], device)

    def start(i, carry):
        to_group(i).start()
        return carry

    lax.fori_loop(1, 16, start, 0)
    vb[me.group] = piece[...]

    def end(i, carry):
        to_group(i).wait_send()
        group = (me.group + i) % 16
        remote(piece, vb.at[group], send2.at[i], recv2.at[group], me.sibling()).wait_recv()
        return carry

    lax.fori_loop(1, 16, end, 0)
    total = vb[0]
    for i in range(1, 16):
        total = total + vb[i]
    out[me.slot] = total
    own = out.at[me.slot]

    def to_member(i):
        core, x = (me.core + i // 4) % 2, (me.x + i) % 4
        return remote(own, own, send3.at[i], recv3.at[me.slot], me.peer(core, x))

    def start_three(i, carry):
        to_member(i).start()
        return carry

    lax.fori_loop(1, MEMBERS, start_three, 0)

    def end_three(i, carry):
        to_member(i).wait_send()
        slot = ((me.core + i // 4) % 2) * 4 + (me.x + i) % 4
        remote(own, out.at[slot], send3.at[i], recv3.at[slot], me.sibling()).wait_recv()
        return carry

    lax.fori_loop(1, MEMBERS, end_three, 0)


def exit_kernel(
    grad_qkv, normed_one, w, g_attn, attended, state, grad_mid, gain, dwa, wide_in, narrow_in,
    gradient, suma, sumb, vectors, *scratch,
):
    sum1, pa, pb = scratch[0:9], scratch[9:11], scratch[11:13]
    landa, landb, dwb, wide, q_sum, narrow, va, vl, vb, piece = scratch[13:23]
    v1, v2, v3 = scratch[23:25], scratch[25:27], scratch[27:29]
    me = Place()
    greet(me, True)
    grads_start(me, dwa, landa, *pa)

    def more():
        grads_start(me, dwb, landb, *pb)

    wide[...] = wide_in[...]
    gradient[...] = first_back(
        me, grad_qkv, normed_one, w, g_attn, attended, state, grad_mid, gain, dwb, wide, 0, q_sum, sum1, more
    )
    narrow[...] = narrow_in[...]
    narrow[0:1] = q_sum[:, 0:128]
    narrow[1:2] = q_sum[:, 256:384]
    vectors_start(me, wide, va, vl, *v1)
    vectors_end(me, narrow, va, vl, *v1, vb, piece, *v2, vectors, *v3)
    grads_end(me, dwa, landa, *pa, suma)
    grads_end(me, dwb, landb, *pb, sumb)


def key_mask(shape, dim, length):
    at = lax.broadcasted_iota(jnp.int32, shape, dim)
    block = (at >= PAD).astype(jnp.int32) + (at >= 2 * PAD).astype(jnp.int32) + (at >= 3 * PAD).astype(jnp.int32)
    row = at - block * PAD
    return (row < ROWS) & (row + block * ROWS < length)


def head_parts(qkv, at):
    return qkv[:, :, at * COLS : (at + 1) * COLS].reshape(4 * PAD, COLS)


def attend_kernel(length, qkv, out):
    q, k, v = (head_parts(qkv, i) for i in range(3))
    valid = key_mask((1, 4 * PAD), 1, length[pl.program_id(0)])
    lane = lax.broadcasted_iota(jnp.int32, (1, COLS), 1)
    total = None
    for h in range(2):
        mine = (lane >= h * HEAD) & (lane < (h + 1) * HEAD)
        scores = dot(jnp.where(mine, q, jnp.zeros_like(q)), k, NT) * F32(HEAD**-0.5)
        scores = jnp.where(valid, scores, NEG_FILL)
        e = jnp.exp(scores - jnp.max(scores, axis=-1, keepdims=True))
        prob = (e * (1.0 / jnp.sum(e, axis=-1, keepdims=True))).astype(BF16)
        mixed = dot(prob, v)
        total = mixed if total is None else jnp.where(mine, mixed, total)
    out[...] = total.astype(BF16).reshape(4, PAD, COLS)


def attend_back_kernel(length, qkv, grad, out):
    q, k, v = (head_parts(qkv, i) for i in range(3))
    g = grad[...].reshape(4 * PAD, COLS)
    valid = key_mask((4 * PAD, 1), 0, length[pl.program_id(0)])
    lane = lax.broadcasted_iota(jnp.int32, (1, COLS), 1)
    parts = [None, None, None]
    for h in range(2):
        mine = (lane >= h * HEAD) & (lane < (h + 1) * HEAD)
        scores = dot(k, jnp.where(mine, q, jnp.zeros_like(q)), NT) * F32(HEAD**-0.5)
        scores = jnp.where(valid, scores, NEG_FILL)
        e = jnp.exp(scores - jnp.max(scores, axis=0, keepdims=True))
        prob = e * (1.0 / jnp.sum(e, axis=0, keepdims=True))
        grad_value = dot(prob.astype(BF16), g)
        grad_prob = dot(v, jnp.where(mine, g, jnp.zeros_like(g)), NT)
        inner = jnp.sum(grad_prob * prob, axis=0, keepdims=True)
        grad_scores = (prob * (grad_prob - inner)).astype(BF16)
        grad_key = dot(grad_scores, q) * F32(HEAD**-0.5)
        grad_query = dot(grad_scores, k, TN) * F32(HEAD**-0.5)
        new = [grad_query, grad_key, grad_value]
        parts = new if h == 0 else [jnp.where(mine, n, p) for n, p in zip(new, parts)]
    for i in range(3):
        out[:, :, i * COLS : (i + 1) * COLS] = parts[i].astype(BF16).reshape(4, PAD, COLS)


def attention(kernel, length, arrays, width):
    def spec(w):
        return pl.BlockSpec((4, PAD, w), lambda i: (i, 0, 0))

    return pl.pallas_call(
        kernel,
        grid=(2,),
        out_shape=jax.ShapeDtypeStruct((MEMBERS, PAD, width), BF16),
        in_specs=[pl.BlockSpec(memory_space=pltpu.SMEM)] + [spec(a.shape[2]) for a in arrays],
        out_specs=spec(width),
        compiler_params=pltpu.CompilerParams(vmem_limit_bytes=VMEM_BYTES),
    )(length, *arrays)


def swap(value):
    pairs = []
    for pair in range(8):
        for a in range(2):
            for b in range(2):
                for x in range(4):
                    pairs.append(((pair * 2 + a) * 8 + b * 4 + x, (pair * 2 + b) * 8 + a * 4 + x))
    return lax.ppermute(value, ("dp", "tensor"), pairs)


def per_device(
    x_in, valid_len, w_qkv, w_out, w_up, w_down, norm_gain, norm_shift, bias, up_bias, cotangent
):
    dp, tensor = lax.axis_index("dp"), lax.axis_index("tensor")
    slot = (dp % 2) * 4 + tensor % 4

    def padded(rows):
        return jnp.pad(rows, ((0, PAD - ROWS), (0, 0)))

    x = padded(swap(x_in))
    cot = padded(swap(cotangent))
    length = swap(valid_len)
    shards = jnp.concatenate(
        [
            w_qkv.reshape(2, 64, 384),
            jnp.swapaxes(w_out, 1, 2),
            w_up,
            jnp.swapaxes(w_down, 1, 2),
        ],
        axis=2,
    )
    gain = [[norm_gain[l, i][None] for i in range(2)] for l in range(2)]
    shift = [[norm_shift[l, i][None] for i in range(2)] for l in range(2)]
    bias_rows = [[bias[l, i][None] for i in range(4)] for l in range(2)]
    own_bias = lax.dynamic_slice_in_dim(bias, slot * COLS, COLS, axis=2)
    own_up = lax.dynamic_slice_in_dim(up_bias, slot * HID, HID, axis=1)
    qbias = [
        jnp.concatenate([own_bias[l, 0], jnp.zeros((COLS,), F32), own_bias[l, 1]])[None] for l in range(2)
    ]
    ubias = [own_up[l][None] for l in range(2)]

    rows_all, rows_own = (MEMBERS, PAD, D), (PAD, D)
    qkv0, normed0, w0 = call(
        enter_kernel,
        [((MEMBERS, PAD, 384), BF16), (rows_all, BF16), ((16, 64, WCOLS), BF16)],
        GATHER_SEMS + PLANE_SEMS,
        0,
        [x, shards[0], gain[0][0], shift[0][0], qbias[0]],
        1 << 30,
    )
    attended0 = attention(attend_kernel, length, [qkv0], COLS)
    middle0, normed_two0, hidden0, act0, state1, normed1, qkv1, w1 = call(
        between_kernel,
        [
            (rows_own, F32),
            (rows_all, BF16),
            ((MEMBERS, PAD, HID), F32),
            ((MEMBERS, PAD, HID), BF16),
            (rows_own, F32),
            (rows_all, BF16),
            ((MEMBERS, PAD, 384), BF16),
            ((16, 64, WCOLS), BF16),
        ],
        SUM_SCRATCH * 2 + GATHER_SEMS * 2 + PLANE_SEMS,
        1,
        [
            attended0, x, w0, shards[1], gain[0][1], shift[0][1], bias_rows[0][2], ubias[0], bias_rows[0][3],
            gain[1][0], shift[1][0], qbias[1],
        ],
        4 << 30,
    )
    attended1 = attention(attend_kernel, length, [qkv1], COLS)
    out_rows, dwa1, grad_mid1, g_attn1, grad_att1, wide1, up1 = call(
        turn_kernel,
        [
            (rows_own, BF16),
            ((16, 64, 1024), BF16),
            (rows_own, F32),
            (rows_all, BF16),
            ((MEMBERS, PAD, COLS), BF16),
            ((8, D), F32),
            ((1, HID), F32),
        ],
        SUM_SCRATCH * 3
        + GATHER_SEMS * 3
        + [
            pltpu.VMEM(rows_own, F32),
            pltpu.VMEM(rows_all, BF16),
            pltpu.VMEM((MEMBERS, PAD, HID), F32),
            pltpu.VMEM((MEMBERS, PAD, HID), BF16),
            pltpu.VMEM(rows_all, BF16),
            pltpu.VMEM((MEMBERS, PAD, HID), BF16),
        ],
        2,
        [attended1, state1, w1, cot, gain[1][1], shift[1][1], bias_rows[1][2], ubias[1], bias_rows[1][3]],
        8 << 30,
    )
    out_rows = swap(out_rows[:ROWS])
    grad_qkv1 = attention(attend_back_kernel, length, [qkv1, grad_att1], 384)
    suma1, sumb1, dwa0, grad_mid0, g_attn0, grad_att0, wide0, up0, q1 = call(
        back_kernel,
        [
            ((64, 1024), F32),
            ((64, 512), F32),
            ((16, 64, 1024), BF16),
            (rows_own, F32),
            (rows_all, BF16),
            ((MEMBERS, PAD, COLS), BF16),
            ((8, D), F32),
            ((1, HID), F32),
            ((1, 384), F32),
        ],
        SUM_SCRATCH * 2
        + GATHER_SEMS * 2
        + PLANE_SEMS * 2
        + [
            pltpu.VMEM((16, 64, 1024), BF16),
            pltpu.VMEM((16, 64, 512), BF16),
            pltpu.VMEM((16, 64, 512), BF16),
            pltpu.VMEM(rows_own, F32),
            pltpu.VMEM(rows_all, BF16),
            pltpu.VMEM((MEMBERS, PAD, HID), BF16),
        ],
        3,
        [
            grad_qkv1, normed1, w1, g_attn1, attended1, state1, grad_mid1, gain[1][0], dwa1,
            w0, hidden0, act0, normed_two0, middle0, gain[0][1],
        ],
        8 << 30,
    )
    grad_qkv0 = attention(attend_back_kernel, length, [qkv0, grad_att0], 384)
    wide = jnp.concatenate(
        [jnp.zeros((2, D), F32), wide0[2:6], wide0[0:2], wide1[0:4], jnp.zeros((4, D), F32)], axis=0
    )
    zeros = jnp.zeros((2, COLS), F32)
    narrow = jnp.concatenate(
        [
            zeros,
            up0.reshape(4, COLS),
            q1[:, 0:COLS],
            q1[:, 2 * COLS :],
            up1.reshape(4, COLS),
            jnp.zeros((4, COLS), F32),
        ],
        axis=0,
    )
    gradient, suma0, sumb0, vectors = call(
        exit_kernel,
        [(rows_own, F32), ((64, 1024), F32), ((64, 512), F32), ((MEMBERS, 32, 128), F32)],
        SUM_SCRATCH
        + PLANE_SEMS * 2
        + [
            pltpu.VMEM((16, 64, 1024), BF16),
            pltpu.VMEM((16, 64, 512), BF16),
            pltpu.VMEM((16, 64, 512), BF16),
            pltpu.VMEM((16, D), F32),
            pltpu.VMEM((1, 384), F32),
            pltpu.VMEM((16, 128), F32),
            pltpu.VMEM((MEMBERS, 16, 128), F32),
            pltpu.VMEM((MEMBERS, 16, 128), F32),
            pltpu.VMEM((16, 32, 128), F32),
            pltpu.VMEM((32, 128), F32),
        ]
        + [pltpu.SemaphoreType.DMA((8,))] * 2
        + PLANE_SEMS
        + [pltpu.SemaphoreType.DMA((8,))] * 2,
        4,
        [grad_qkv0, normed0, w0, g_attn0, attended0, x, grad_mid0, gain[0][0], dwa0, wide, narrow],
        4 << 30,
    )
    suma, sumb = jnp.stack([suma0, suma1]), jnp.stack([sumb0, sumb1])
    full = jnp.transpose(vectors[:, 0:12], (1, 0, 2)).reshape(2, 6, D)
    own = vectors[:, 16:28].reshape(MEMBERS, 2, 6, COLS)
    q_bias = jnp.transpose(own[:, :, 0], (1, 0, 2)).reshape(2, D)
    v_bias = jnp.transpose(own[:, :, 1], (1, 0, 2)).reshape(2, D)
    return (
        out_rows,
        swap(gradient[:ROWS]),
        sumb[:, :, 0:384].reshape(2, 64, 3, COLS),
        jnp.swapaxes(sumb[:, :, 384:], 1, 2),
        suma[:, :, 0:HID],
        jnp.swapaxes(suma[:, :, HID:], 1, 2),
        jnp.stack([full[:, 0], full[:, 3]], axis=1),
        jnp.stack([full[:, 1], full[:, 4]], axis=1),
        jnp.stack([q_bias, v_bias, full[:, 5], full[:, 2]], axis=1),
        jnp.transpose(own[:, :, 2:], (1, 0, 2, 3)).reshape(2, 4096),
    )


def solution(mesh):
    rows = P(("dp", "tensor"), None)
    weights = (P(None, "dp", None, "tensor"), P(None, "tensor", "dp"), P(None, "dp", "tensor"), P(None, "tensor", "dp"))
    return jax.shard_map(
        per_device,
        mesh=mesh,
        in_specs=(rows, P("dp"), *weights, P(), P(), P(), P(), rows),
        out_specs=(rows, rows, *weights, P(), P(), P(), P()),
        check_vma=False,
    )
```

time: 1670 us -> 524 us (0.31)
  waiting for transfers between devices: 998 us -> 3.95 us
  Pallas kernels: 0 us -> 478 us
  blocking collectives: 369 us -> 0 us
  matrix products: 116 us -> 0 us
  local copies, waits for them, and re-layouts: 102 us -> 18.9 us
  other arithmetic: 44.9 us -> 5.07 us
    reduce_scatter x8 -> x0, waiting for transfers between devices: 488 us -> none  [the longest x2 138 us: per_device(): lax.psum_scatter(layer_grads[2].astype(jnp.bfloat16), 'dp', scatter_dimen...]
    pallas_call x0 -> x9, Pallas kernels: none -> 478 us  [the longest x5 448 us: call(): pl.pallas_call(kernel, out_shape=[jax.ShapeDtypeStruct(s, t) for s, t in...]
    all_gather x12 -> x0, waiting for transfers between devices: 352 us -> none  [the longest x4 107 us: spread_grads(): return lax.all_gather(rows_local, 'tensor', axis=0, tiled=True)]
    unnamed x7 -> x0, blocking collectives: 267 us -> none
    psum x1 -> x0, waiting for transfers between devices: 146 us -> none  [per_device(): lax.psum((jnp.stack(gain_grads), jnp.stack(shift_grads), jnp.stack(bias_g...]
    dot_general x52 -> x0, matrix products: 116 us -> none  [the longest x2 19 us: per_device(): hidden = jnp.dot(normed_two, w_u, preferred_element_type=jnp.float32)]
    all_gather x4 -> x0, blocking collectives: 103 us -> none  [the longest x2 54.4 us: per_device(): lax.all_gather(w_out[layer], 'dp', axis=1, tiled=True)]
    unnamed x199 -> x20, local copies, waits for them, and re-layouts: 50.5 us -> 2.09 us
  transfers between devices with their start and end apart: 29 -> 5, of which waited for: 24 -> 1; matrix products, arithmetic and copies ran while one was open for 13% -> 3% of each run, Pallas kernels for 0% -> 34%
where the time goes in v1:
time: 524 us; the launch traced here: 523 us
  Pallas kernels  478 us (91%)
  local copies, waits for them, and re-layouts  18.9 us (4%)
  starting transfers between devices  16.2 us (3%)
    pallas_call x5, Pallas kernels, call(): pl.pallas_call(kernel, out_shape=[jax.ShapeDtypeStruct(s, t) for s, t in...  448 us
    pallas_call x4, Pallas kernels, attention(): pl.pallas_call(kernel, grid=(2,), out_shape=jax.ShapeDtypeStruct((MEMBERS...  29.6 us
    ppermute x5, starting transfers between devices, swap(): return lax.ppermute(value, ('dp', 'tensor'), pairs)  16.2 us
  transfers between devices with their start and end apart: 5, of which 1 were waited for; matrix products, arithmetic and copies ran while one was open for 3% of the time, Pallas kernels for 34%

profile of v1, /device:TPU:1, one launch (start us, length us, event | category | flops | bytes accessed | tf_op | source)
XLA Modules:
  0.0 522.9 jit_solution(9019832170645697095)
XLA Ops:
  0.7 5.1 collective-permute-start
  5.7 1.9 collective-permute-start.1
  7.7 3.6 collective-permute-start.2
  11.4 1.0 pad_maximum_fusion
  13.1 1.4 slice_bitcast_fusion.4
  14.5 0.8 fusion.7
  16.5 1.4 fusion.13
  18.0 1.4 slice_bitcast_fusion.6
  20.2 71.2 %shard_map.186 = (bf16[8,160,384]{2,1,0:T(8,128)(2,1)}, bf16[8,160,1024]{2,1,0:T(8,128)(2,1)}, bf16[16,64,1536]{2,1,0:T(8,128)(2,1)}) custom-call(bf16[160,1024]{1,0:T(8,128)(2,1)} %pad.7.x.state, bf16[64,1536]{1,0:T(8,128)(2,1)} %get-tuple-element.105.shard, f32[1,1024]{1,0:T(1,128)} %get-tuple-element.139.gain, f32[1,1024]{1,0:T(1,128)} %get-tuple-element.128.shift, ...), custom_call_target="tpu_custom_call" | custom-call | flops 1073741824 | bytes 1048576 | tf_op jit(solution)/shard_map/pallas_call | solution.py:359
  91.9 5.9 %shard_map.187.attended = bf16[8,160,128]{2,1,0:T(8,128)(2,1)} custom-call(s32[2]{0:T(128)} %copy-done.6, bf16[8,160,384]{2,1,0:T(8,128)(2,1)} %get-tuple-element.41.qkv), custom_call_target="tpu_custom_call" | custom-call | tf_op jit(solution)/shard_map/pallas_call | solution.py:692
  97.9 93.6 %shard_map.188 = (f32[160,1024]{1,0:T(8,128)}, bf16[8,160,1024]{2,1,0:T(8,128)(2,1)}, f32[8,160,512]{2,1,0:T(8,128)}, bf16[8,160,512]{2,1,0:T(8,128)(2,1)}, f32[...) custom-call(bf16[8,160,128]{2,1,0:T(8,128)(2,1)} %shard_map.187.atte, ...), custom_call_target="tpu_custom_call" | custom-call | flops 4294967296 | bytes 1048576 | tf_op jit(solution)/shard_map/pallas_call | solution.py:359
  191.5 5.9 %shard_map.189.attended.attended_one = bf16[8,160,128]{2,1,0:T(8,128)(2,1)} custom-call(s32[2]{0:T(128)} %copy-done.6, bf16[8,160,384]{2,1,0:T(8,128)(2,1)} %get-tuple-element.43.qkv), custom_call_target="tpu_custom_call" | custom-call | tf_op jit(solution)/shard_map/pallas_call | solution.py:692
  198.2 124.4 %shard_map.190 = (bf16[160,1024]{1,0:T(8,128)(2,1)}, bf16[16,64,1024]{2,1,0:T(8,128)(2,1)}, f32[160,1024]{1,0:T(8,128)}, bf16[8,160,1024]{2,1,0:T(8,128)(2,1)}, ...) custom-call(bf16[8,160,128]{2,1,0:T(8,128)(2,1)} %shard_map.189.attended.attended_one, ...), custom_call_target="tpu_custom_call" | custom-call | flops 8589934592 | bytes 1048576 | tf_op jit(solution)/shard_map/pallas_call | solution.py:359
  322.6 9.0 %shard_map.191.grad_qkv = bf16[8,160,384]{2,1,0:T(8,128)(2,1)} custom-call(s32[2]{0:T(128)} %copy-done.6, bf16[8,160,384]{2,1,0:T(8,128)(2,1)} %get-tuple-element.43.qkv, bf16[8,160,128]{2,1,0:T(8,128)(2,1)} %get-tuple-element.47.grad), custom_call_target="tpu_custom_call" | custom-call | tf_op jit(solution)/shard_map/pallas_call | solution.py:692
  331.6 96.7 %shard_map.192 = (f32[64,1024]{1,0:T(8,128)}, f32[64,512]{1,0:T(8,128)}, bf16[16,64,1024]{2,1,0:T(8,128)(2,1)}, f32[160,1024]{1,0:T(8,128)}, bf16[8,160,1024]{2,...) custom-call(bf16[8,160,384]{2,1,0:T(8,128)(2,1)} %shard_map.191.grad_, ...), custom_call_target="tpu_custom_call" | custom-call | flops 8589934592 | bytes 1048576 | tf_op jit(solution)/shard_map/pallas_call | solution.py:359
  430.6 1.3 concatenate.18.wide_in
  431.8 1.9 concatenate.19.narrow_in
  433.7 8.7 %shard_map.193.grad_qkv = bf16[8,160,384]{2,1,0:T(8,128)(2,1)} custom-call(s32[2]{0:T(128)} %copy-done.6, bf16[8,160,384]{2,1,0:T(8,128)(2,1)} %get-tuple-element.41.qkv, bf16[8,160,128]{2,1,0:T(8,128)(2,1)} %get-tuple-element.56.grad), custom_call_target="tpu_custom_call" | custom-call | tf_op jit(solution)/shard_map/pallas_call | solution.py:692
  442.5 62.3 %shard_map.194 = (f32[160,1024]{1,0:T(8,128)}, f32[64,1024]{1,0:T(8,128)}, f32[64,512]{1,0:T(8,128)}, f32[8,32,128]{2,1,0:T(8,128)}) custom-call(bf16[8,160,384]{2,1,0:T(8,128)(2,1)} %shard_map.193.grad_qkv, bf16[8,160,1024]{2,1,0:T(8,128)(2,1)} %get-tuple-element.57.normed_one, bf16[16,64,1536]{2,1,0:T(8,128)(2,1)} %get-tuple-element.42.w.w_low, ...), custom_call_target="tpu_custom_call" | custom-call | flops 4294967296 | bytes 1048576 | tf_op jit(solution)/shard_map/pallas_call | solution.py:359
  504.9 1.0 fusion.10
  505.9 2.8 collective-permute-start.3
  508.7 1.1 slice.152
  509.8 2.8 collective-permute-start.4
  517.4 3.9 collective-permute-done.4
  (55 shorter events, 12.6 us)
Async XLA Ops:
  0.6 10.7 %copy-start = (bf16[2,64,3,128]{3,1,2,0:T(8,128)(2,1)S(1)}, bf16[2,64,3,128]{3,1,2,0:T(8,128)(2,1)}, u32[]{:S(2)}) copy-start(bf16[2,64,3,128]{3,1,2,0:T(8,128)(2,1)} %param.13) | copy-start | bytes 294916
  0.7 90.8 %collective-permute-start = (s32[2]{0:T(128)}, s32[2]{0:T(128)S(1)}, u32[]{:S(2)}, u32[]{:S(2)}) collective-permute-start(s32[2]{0:T(128)} %param.12), channel_id=1, source_target_pairs={{0,0},{1,1},{2,2},{3,3},{4,8},{5,9},{6,10},{7,11},{8,4},{9,5},{10,... | collective-permute-start | bytes 32 | tf_op jit(solution)/shard_map/ppermute | solution.py:709
  5.7 13.7 %collective-permute-start.1 = (bf16[146,1024]{1,0:T(8,128)(2,1)}, bf16[146,1024]{1,0:T(8,128)(2,1)S(1)}, u32[]{:S(2)}, u32[]{:S(2)}) collective-permute-start(bf16[146,1024]{1,0:T(8,128)(2,1)} %param.11), channel_id=1, source_target_pairs={{0,0},{1,1},{2,2},{3,3},{4,8},{5,9},{6,10},{7,11},{8,4},{9,5},{10,... | collective-permute-start | bytes 897032 | tf_op jit(solution)/shard_map/ppermute | solution.py:709
  7.7 189.7 %collective-permute-start.2 = (bf16[146,1024]{1,0:T(8,128)(2,1)}, bf16[146,1024]{1,0:T(8,128)(2,1)S(1)}, u32[]{:S(2)}, u32[]{:S(2)}) collective-permute-start(bf16[146,1024]{1,0:T(8,128)(2,1)} %param.21), channel_id=1, source_target_pairs={{0,0},{1,1},{2,2},{3,3},{4,8},{5,9},{6,10},{7,11},{8,4},{9,5},{10,... | collective-permute-start | bytes 897032 | tf_op jit(solution)/shard_map/ppermute | solution.py:709
  91.4 0.5 copy-start.6
  331.6 98.2 %copy-start.7 = (f32[8,1024]{1,0:T(8,128)S(1)}, f32[8,1024]{1,0:T(8,128)}, u32[]{:S(2)}) copy-start(f32[8,1024]{1,0:T(8,128)} %get-tuple-element.62) | copy-start | bytes 98308
  331.6 100.2 %copy-start.8 = (f32[1,512]{1,0:T(1,128)S(1)}, f32[1,512]{1,0:T(1,128)}, u32[]{:S(2)}) copy-start(f32[1,512]{1,0:T(1,128)} %get-tuple-element.65) | copy-start | bytes 6148
  442.5 63.4 %copy-start.3 = (bf16[160,1024]{1,0:T(8,128)(2,1)S(1)}, bf16[160,1024]{1,0:T(8,128)(2,1)}, u32[]{:S(2)}) copy-start(bf16[160,1024]{1,0:T(8,128)(2,1)} %get-tuple-element.46) | copy-start | bytes 983044
  504.8 9.8 %copy-start.1 = (f32[64,512]{1,0:T(8,128)S(1)}, f32[64,512]{1,0:T(8,128)}, u32[]{:S(2)}) copy-start(f32[64,512]{1,0:T(8,128)} %get-tuple-element.68) | copy-start | bytes 393220
  504.8 9.8 %copy-start.2 = (f32[64,512]{1,0:T(8,128)S(1)}, f32[64,512]{1,0:T(8,128)}, u32[]{:S(2)}) copy-start(f32[64,512]{1,0:T(8,128)} %get-tuple-element.67) | copy-start | bytes 393220
  504.8 11.8 %copy-start.4 = (f32[64,1024]{1,0:T(8,128)S(1)}, f32[64,1024]{1,0:T(8,128)}, u32[]{:S(2)}) copy-start(f32[64,1024]{1,0:T(8,128)} %get-tuple-element.70) | copy-start | bytes 786436
  504.9 11.7 %copy-start.5 = (f32[64,1024]{1,0:T(8,128)S(1)}, f32[64,1024]{1,0:T(8,128)}, u32[]{:S(2)}) copy-start(f32[64,1024]{1,0:T(8,128)} %get-tuple-element.69) | copy-start | bytes 786436
  505.9 11.5 %collective-permute-start.3 = (bf16[146,1024]{1,0:T(8,128)(2,1)S(1)}, bf16[146,1024]{1,0:T(8,128)(2,1)S(1)}, u32[]{:S(2)}, u32[]{:S(2)}) collective-permute-start(bf16[146,1024]{1,0:T(8,128)(2,1)S(1)} %slice.146), channel_id=1, source_target_pairs={{0,0},{1,1},{2,2},{3,3},{4,8},{5,9},{6,10},{7,11},{8,4},{9,5},{10,... | collective-permute-start | bytes 897032 | tf_op jit(solution)/shard_map/ppermute | solution.py:709
  509.8 11.6 %collective-permute-start.4 = (f32[146,1024]{1,0:T(8,128)S(1)}, f32[146,1024]{1,0:T(8,128)S(1)}, u32[]{:S(2)}, u32[]{:S(2)}) collective-permute-start(f32[146,1024]{1,0:T(8,128)S(1)} %slice.152), channel_id=1, source_target_pairs={{0,0},{1,1},{2,2},{3,3},{4,8},{5,9},{6,10},{7,11},{8,4},{9,5},{10,... | collective-permute-start | bytes 1794056 | tf_op jit(solution)/shard_map/ppermute | solution.py:709

commit v2 on v1

--- a/solution.py
+++ b/solution.py
@@ -92,100 +92,204 @@
     )
 
 
-def near(o):
-    return o + (o // 2) * (5 - 2 * o)
-
-
-def gather_start(me, g, send, recv):
-    own = g.at[me.slot]
-    remote(own, own, send.at[4], recv.at[4], me.sibling()).start()
-    for dx in (1, 3, 2):
-        remote(own, own, send.at[dx], recv.at[dx], me.peer(me.core, (me.x + dx) % 4)).start()
-
-
-def gather_run(me, g, send, recv, consume):
-    def step(i, carry):
-        dx, dc = near(i // 2), i % 2
-        k = dc * 4 + dx
-        slot = ((me.core + dc) % 2) * 4 + (me.x + 4 - dx) % 4
-        block = g.at[slot]
-
-        @pl.when(i > 0)
-        def _():
-            remote(block, block, send.at[k], recv.at[k], me.sibling()).wait_recv()
-
-        @pl.when((dc == 0) & (i > 0))
-        def _():
-            remote(block, block, send.at[4 + dx], recv.at[4 + dx], me.sibling()).start()
-
-        consume(slot)
-        return carry
-
-    lax.fori_loop(0, MEMBERS, step, 0)
-
-
-def gather_end(me, g, send, recv):
-    def step(k, carry):
-        block = g.at[0]
-        remote(block, block, send.at[k], recv.at[k], me.sibling()).wait_send()
-        return carry
-
-    lax.fori_loop(1, MEMBERS, step, 0)
-
-
-GATHER_SEMS = [pltpu.SemaphoreType.DMA((8,)), pltpu.SemaphoreType.DMA((8,))]
+def slot_at(me, i):
+    sibling = (i == 1) | (i == 4) | (i == 5) | (i == 7)
+    far = (i >= 6).astype(jnp.int32) * 2
+    left = ((i == 2) | (i == 4)).astype(jnp.int32) * 3
+    right = ((i == 3) | (i == 5)).astype(jnp.int32)
+    core = (me.core + sibling.astype(jnp.int32)) % 2
+    return core * 4 + (me.x + far + left + right) % 4
+
+
+HALF = PAD // 2
+TOP, BOTTOM = pl.ds(0, HALF), pl.ds(HALF, HALF)
+
+
+class Gather:
+    def __init__(self, me, g, send, recv):
+        self.me, self.g, self.send, self.recv = me, g, send, recv
+        self.right = me.peer(me.core, (me.x + 1) % 4)
+        self.left = me.peer(me.core, (me.x + 3) % 4)
+        self.from_left = me.core * 4 + (me.x + 3) % 4
+        self.from_right = me.core * 4 + (me.x + 1) % 4
+        self.from_far = me.core * 4 + (me.x + 2) % 4
+
+    def copy(self, k, slot, rows, device):
+        block = self.g.at[slot] if rows is None else self.g.at[slot, rows]
+        return remote(block, block, self.send.at[k], self.recv.at[k], device)
+
+    def table(self):
+        me = self.me
+        sibling = me.sibling()
+        return [
+            (0, me.slot, TOP, self.right),
+            (1, me.slot, BOTTOM, self.right),
+            (2, me.slot, TOP, self.left),
+            (3, me.slot, BOTTOM, self.left),
+            (4, self.from_left, TOP, self.right),
+            (5, self.from_right, BOTTOM, self.left),
+            (6, me.slot, None, sibling),
+            (7, self.from_left, None, sibling),
+            (8, self.from_right, None, sibling),
+            (9, self.from_far, None, sibling),
+        ]
+
+    def start_copies(self, *which):
+        for k in which:
+            self.copy(*self.table()[k]).start()
+
+    def start(self):
+        self.start_copies(6, 0, 3, 1, 2)
+
+    def arrived(self, *which):
+        for k in which:
+            _, slot, rows, device = self.table()[k]
+            self.copy(k, slot, rows, device).wait_recv()
+
+    def relay(self):
+        self.arrived(0)
+        self.start_copies(4)
+        self.arrived(3)
+        self.start_copies(5)
+
+    def run(self, consume, fill=None, relayed=False):
+        def step(i, carry):
+            @pl.when(i == 1)
+            def _():
+                self.arrived(6)
+
+            @pl.when(i == 2)
+            def _():
+                if not relayed:
+                    self.relay()
+                if fill is not None:
+                    fill()
+                self.arrived(1)
+                self.start_copies(7)
+
+            @pl.when(i == 3)
+            def _():
+                self.arrived(2)
+                self.start_copies(8)
+
+            @pl.when(i == 4)
+            def _():
+                self.arrived(7)
+
+            @pl.when(i == 5)
+            def _():
+                self.arrived(8)
+
+            @pl.when(i == 6)
+            def _():
+                self.arrived(4, 5)
+                self.start_copies(9)
+
+            @pl.when(i == 7)
+            def _():
+                self.arrived(9)
+
+            consume(slot_at(self.me, i))
+            return carry
+
+        lax.fori_loop(0, MEMBERS, step, 0)
+
+    def end(self):
+        for row in self.table():
+            self.copy(*row).wait_send()
+
+
+GATHER_SEMS = [pltpu.SemaphoreType.DMA((10,)), pltpu.SemaphoreType.DMA((10,))]
 
 SUM_SCRATCH = [
     pltpu.VMEM((4, PAD, D), BF16),
     pltpu.VMEM((4, PAD, D), BF16),
     pltpu.VMEM((3, PAD, D), BF16),
-    pltpu.VMEM((3, PAD, D), BF16),
+    pltpu.VMEM((PAD, D), BF16),
+    pltpu.VMEM((2, PAD, D), BF16),
     pltpu.VMEM((PAD, D), F32),
+    pltpu.VMEM((2, HALF, D), F32),
     pltpu.SemaphoreType.DMA((4,)),
     pltpu.SemaphoreType.DMA((4,)),
-    pltpu.SemaphoreType.DMA((3,)),
-    pltpu.SemaphoreType.DMA((3,)),
+    pltpu.SemaphoreType.DMA((6,)),
+    pltpu.SemaphoreType.DMA((6,)),
 ]
+NSUM = len(SUM_SCRATCH)
 
 
 def sum_rows(me, produce, bufs, fill=None):
-    s1, r1, s2, r2, acc, ss1, rs1, ss2, rs2 = bufs
+    s1, r1, s2, ra, rb, acc, hold, ss1, rs1, ss2, rs2 = bufs
     sibling = me.sibling()
+    right, left = me.peer(me.core, (me.x + 1) % 4), me.peer(me.core, (me.x + 3) % 4)
+
+    def chip(i):
+        return (me.x + 2 + (i == 1).astype(jnp.int32) * 3 + (i == 2).astype(jnp.int32) + (i == 3).astype(jnp.int32) * 2) % 4
 
     def to_sibling(i):
         return remote(s1.at[i], r1.at[i], ss1.at[i], rs1.at[i], sibling)
 
-    def to_chip(i):
-        peer = me.peer(me.core, (me.x + i + 1) % 4)
-        return remote(s2.at[i], r2.at[i], ss2.at[i], rs2.at[i], peer)
-
-    def first(i, carry):
-        s1[i] = produce((1 - me.core) * 4 + (me.x + i + 1) % 4).astype(BF16)
+    def along(k):
+        src, dst, device = (
+            (s2.at[0, TOP], ra.at[TOP], right),
+            (s2.at[0, BOTTOM], ra.at[BOTTOM], left),
+            (s2.at[1, BOTTOM], rb.at[0, BOTTOM], right),
+            (s2.at[2, TOP], rb.at[1, TOP], left),
+            (s2.at[1, TOP], rb.at[0, TOP], right),
+            (s2.at[2, BOTTOM], rb.at[1, BOTTOM], left),
+        )[k]
+        return remote(src, dst, ss2.at[k], rs2.at[k], device)
+
+    def for_sibling(i, carry):
+        s1[i] = produce((1 - me.core) * 4 + chip(i)).astype(BF16)
         to_sibling(i).start()
         return carry
 
-    lax.fori_loop(0, 4, first, 0)
-
-    def second(i, carry):
-        part = produce(me.core * 4 + (me.x + i + 1) % 4)
+    def own(i, carry):
+        part = produce(me.core * 4 + chip(i))
         to_sibling(i).wait_recv()
-        s2[i] = (part + r1[i].astype(F32)).astype(BF16)
-        to_chip(i).start()
-        return carry
-
-    lax.fori_loop(0, 3, second, 0)
-    part = produce(me.slot)
-    to_sibling(3).wait_recv()
-    acc[...] = part + r1[3].astype(F32)
+        acc[...] = part + r1[i].astype(F32)
+
+        @pl.when(i == 0)
+        def _():
+            s2[0] = acc[...].astype(BF16)
+            along(0).start()
+            along(1).start()
+
+        @pl.when(i == 1)
+        def _():
+            s2[1, BOTTOM] = acc[BOTTOM].astype(BF16)
+            along(2).start()
+            hold[0] = acc[TOP]
+
+        @pl.when(i == 2)
+        def _():
+            s2[2, TOP] = acc[TOP].astype(BF16)
+            along(3).start()
+            hold[1] = acc[BOTTOM]
+
+        @pl.when(i < 2)
+        def _():
+            for_sibling(i + 2, 0)
+
+        return carry
+
+    lax.fori_loop(0, 2, for_sibling, 0)
+    lax.fori_loop(0, 4, own, 0)
+    along(0).wait_recv()
+    s2[1, TOP] = (hold[0] + ra[TOP].astype(F32)).astype(BF16)
+    along(4).start()
+    along(1).wait_recv()
+    s2[2, BOTTOM] = (hold[1] + ra[BOTTOM].astype(F32)).astype(BF16)
+    along(5).start()
     if fill is not None:
         fill()
-    for i in range(3):
-        to_chip(i).wait_recv()
-    total = acc[...] + r2[0].astype(F32) + r2[1].astype(F32) + r2[2].astype(F32)
+    for k in range(2, 6):
+        along(k).wait_recv()
+    total = acc[...] + rb[0].astype(F32) + rb[1].astype(F32)
     for i in range(4):
         to_sibling(i).wait_send()
-    for i in range(3):
-        to_chip(i).wait_send()
+    for k in range(6):
+        along(k).wait_send()
     return total
 
 
@@ -369,7 +473,21 @@
     )(*args)
 
 
-def project(me, g, w, bias, qkv):
+class Weights:
+    def __init__(self, me, shard, full, send, recv):
+        self.args = (me, shard, full, send, recv)
+
+    def start(self):
+        weights_start(*self.args)
+
+    def arrived(self):
+        weights_arrived(*self.args)
+
+    def sent(self):
+        weights_sent(*self.args)
+
+
+def project(g, w, bias, qkv):
     def consume(slot):
         qkv[slot] = (dot(g[slot], columns(w, 0, 384)) + bias[...]).astype(BF16)
 
@@ -377,122 +495,166 @@
 
 
 def enter_kernel(x, shard, gain, shift, qbias, qkv, normed, w, *sems):
-    gs, gr, ws, wr = sems
     me = Place()
     greet(me, True)
-    weights_start(me, shard, w, ws, wr)
+    weights = Weights(me, shard, w, *sems[2:4])
+    weights.start()
     normed[me.slot] = layer_norm(x[...].astype(F32), gain[...], shift[...]).astype(BF16)
-    gather_start(me, normed, gs, gr)
-    weights_arrived(me, shard, w, ws, wr)
-    gather_run(me, normed, gs, gr, project(me, normed, w, qbias, qkv))
-    gather_end(me, normed, gs, gr)
-    weights_sent(me, shard, w, ws, wr)
-
-
-def forward_rest(me, attended, state, w, gain, shift, bias_out, up_bias, middle, normed, hidden, act, sum1, sum2, gather):
+    gather = Gather(me, normed, *sems[0:2])
+    gather.start()
+    gather.relay()
+    weights.arrived()
+    gather.run(project(normed, w, qbias, qkv), relayed=True)
+    gather.end()
+    weights.sent()
+
+
+def forward_rest(
+    me, attended, state, w, up, down, later, gain, shift, bias_out, up_bias, middle, normed, hidden, act, sum1, sum2, gather
+):
     def out_product(slot):
         return dot(attended[slot], columns(w, 384, 128), NT)
 
     branch = sum_rows(me, out_product, sum1)
     middle[...] = state[...].astype(F32) + (branch + bias_out[...])
     normed[me.slot] = layer_norm(middle[...], gain[...], shift[...]).astype(BF16)
-    gs, gr = gather
-    gather_start(me, normed, gs, gr)
+    gather = Gather(me, normed, *gather)
+    gather.start()
+    down.start()
+    up.arrived()
+    up_full = up.args[2]
+    down_full = down.args[2]
 
     def consume(slot):
-        h = dot(normed[slot], columns(w, 512, 512)) + up_bias[...]
+        h = dot(normed[slot], columns(up_full, 0, 512)) + up_bias[...]
         hidden[slot] = h
         act[slot] = (h * normal_below(h)).astype(BF16)
 
-    gather_run(me, normed, gs, gr, consume)
+    gather.run(consume)
+    down.arrived()
+    if later is not None:
+        later.start()
 
     def down_product(slot):
-        return dot(act[slot], columns(w, 1024, 512), NT)
+        return dot(act[slot], columns(down_full, 0, 512), NT)
 
     total = sum_rows(me, down_product, sum2)
-    gather_end(me, normed, gs, gr)
+    gather.end()
+    up.sent()
+    down.sent()
     return middle[...] + total
 
 
 def between_kernel(
-    attended, state, w, shard, gain, shift, bias_out, up_bias, bias_down, gain_next, shift_next, qbias,
-    middle, normed_two, hidden, act, new_state, normed_next, qkv, w_next, *scratch,
+    attended, state, w, up_shard, down_shard, shard, gain, shift, bias_out, up_bias, bias_down, gain_next, shift_next, qbias,
+    middle, normed_two, hidden, act, new_state, normed_next, qkv, up_full, down_full, w_next, *scratch,
 ):
-    sum1, sum2, g1, g2, wsem = scratch[0:9], scratch[9:18], scratch[18:20], scratch[20:22], scratch[22:24]
+    sum1, sum2, sems = scratch[0:NSUM], scratch[NSUM : 2 * NSUM], scratch[2 * NSUM :]
     me = Place()
     greet(me, True)
-    weights_start(me, shard, w_next, *wsem)
+    up = Weights(me, up_shard, up_full, *sems[4:6])
+    down = Weights(me, down_shard, down_full, *sems[6:8])
+    later = Weights(me, shard, w_next, *sems[8:10])
+    up.start()
     new_state[...] = (
         forward_rest(
-            me, attended, state, w, gain, shift, bias_out, up_bias, middle, normed_two, hidden, act, sum1, sum2, g1
+            me, attended, state, w, up, down, later, gain, shift, bias_out, up_bias, middle, normed_two, hidden, act, sum1,
+            sum2, sems[0:2],
         )
         + bias_down[...]
     )
     normed_next[me.slot] = layer_norm(new_state[...], gain_next[...], shift_next[...]).astype(BF16)
-    gather_start(me, normed_next, *g2)
-    weights_arrived(me, shard, w_next, *wsem)
-    gather_run(me, normed_next, *g2, project(me, normed_next, w_next, qbias, qkv))
-    gather_end(me, normed_next, *g2)
-    weights_sent(me, shard, w_next, *wsem)
+    gather = Gather(me, normed_next, *sems[2:4])
+    gather.start()
+    later.arrived()
+    gather.run(project(normed_next, w_next, qbias, qkv))
+    gather.end()
+    later.sent()
 
 
 def backward_rest(
-    me, g_own, g_rows, w, hidden, act, normed, middle, gain, grad_hid, dw, grad_mid, g_attn, grad_att, wide, row, up_sum,
-    gather1, sums, gather2,
+    me, g_own, g_rows, w, up_full, down_full, hidden, act, normed, middle, gain, grad_hid, dwd, dwu, after_down, after_up,
+    grad_mid, g_attn, grad_att, wide, row, up_sum, gather1, sums, gather2,
 ):
     def consume(slot):
-        grad_act = dot(g_rows[slot], columns(w, 1024, 512))
+        grad_act = dot(g_rows[slot], columns(down_full, 0, 512))
         grad_hid[slot] = (grad_act * gelu_slope(hidden[slot])).astype(BF16)
 
-    gather_run(me, g_rows, *gather1, consume)
+    gather1.run(consume)
 
     def up_back(slot):
-        return dot(grad_hid[slot], columns(w, 512, 512), NT)
+        return dot(grad_hid[slot], columns(up_full, 0, 512), NT)
 
     def fill():
-        weight_grad(g_rows, act, dw, 512, 512)
+        weight_grad(g_rows, act, dwd, 0, 512)
+        after_down()
         up_sum[...] = column_sum(grad_hid)
 
     grad = sum_rows(me, up_back, sums, fill)
-    gather_end(me, g_rows, *gather1)
+    gather1.end()
     back, gain_sum, shift_sum = layer_norm_back(middle[...], gain[...], grad)
     mid = g_own[...].astype(F32) + back
     grad_mid[...] = mid
     g_attn[me.slot] = mid.astype(BF16)
-    gather_start(me, g_attn, *gather2)
+    gather2.start()
     wide[row : row + 1] = jnp.sum(g_own[...].astype(F32), axis=0, keepdims=True)
     wide[row + 1 : row + 2] = gain_sum
     wide[row + 2 : row + 3] = shift_sum
     wide[row + 3 : row + 4] = jnp.sum(mid, axis=0, keepdims=True)
-    weight_grad(normed, grad_hid, dw, 0, 512)
+
+    def fill_two():
+        weight_grad(normed, grad_hid, dwu, 0, 512)
+        after_up()
 
     def att_back(slot):
         grad_att[slot] = dot(g_attn[slot], columns(w, 384, 128)).astype(BF16)
 
-    gather_run(me, g_attn, *gather2, att_back)
-    gather_end(me, g_attn, *gather2)
+    gather2.run(att_back, fill_two)
+    gather2.end()
+
+
+def nothing():
+    pass
+
+
+class Grads:
+    def __init__(self, me, part, land, send, recv):
+        self.args = (me, part, land, send, recv)
+
+    def start(self):
+        grads_start(*self.args)
+
+    def end(self, out):
+        grads_end(*self.args, out)
 
 
 def turn_kernel(
-    attended, state, w, cot, gain, shift, bias_out, up_bias, bias_down,
-    out_rows, dw, grad_mid, g_attn, grad_att, wide, up_sum, *scratch,
+    attended, state, w, up_shard, down_shard, cot, gain, shift, bias_out, up_bias, bias_down,
+    out_rows, sumd, dwu, grad_mid, g_attn, grad_att, wide, up_sum, *scratch,
 ):
-    sum1, sum2, sum3 = scratch[0:9], scratch[9:18], scratch[18:27]
-    g1, g2, g3 = scratch[27:29], scratch[29:31], scratch[31:33]
-    middle, normed, hidden, act, g_rows, grad_hid = scratch[33:39]
+    sum1, sum2, sum3 = (scratch[i * NSUM : (i + 1) * NSUM] for i in range(3))
+    sems = scratch[3 * NSUM : 3 * NSUM + 12]
+    middle, normed, hidden, act, g_rows, grad_hid, up_full, down_full, dwd, land = scratch[3 * NSUM + 12 :]
     me = Place()
-    greet(me, False)
+    greet(me, True)
+    up = Weights(me, up_shard, up_full, *sems[6:8])
+    down = Weights(me, down_shard, down_full, *sems[8:10])
+    grads = Grads(me, dwd, land, *sems[10:12])
+    up.start()
     g_rows[me.slot] = cot[...]
-    gather_start(me, g_rows, *g2)
+    gather2 = Gather(me, g_rows, *sems[2:4])
+    gather2.start()
     total = forward_rest(
-        me, attended, state, w, gain, shift, bias_out, up_bias, middle, normed, hidden, act, sum1, sum2, g1
+        me, attended, state, w, up, down, None, gain, shift, bias_out, up_bias, middle, normed, hidden, act, sum1, sum2,
+        sems[0:2],
     )
     out_rows[...] = (total + bias_down[...]).astype(BF16)
     wide[...] = jnp.zeros_like(wide)
     backward_rest(
-        me, cot, g_rows, w, hidden, act, normed, middle, gain, grad_hid, dw, grad_mid, g_attn, grad_att, wide, 0, up_sum,
-        g2, sum3, g3,
-    )
+        me, cot, g_rows, w, up_full, down_full, hidden, act, normed, middle, gain, grad_hid, dwd, dwu, grads.start, nothing,
+        grad_mid, g_attn, grad_att, wide, 0, up_sum, gather2, sum3, Gather(me, g_attn, *sems[4:6]),
+    )
+    grads.end(sumd)
 
 
 def first_back(me, grad_qkv, normed_one, w, g_attn, attended, state, grad_mid, gain, dwb, wide, row, q_sum, sums, more):
@@ -513,34 +675,37 @@
 
 
 def back_kernel(
-    grad_qkv, normed_one, w, g_attn_one, attended_one, state, grad_mid_one, gain_one, dwa_one,
-    w_low, hidden, act, normed_two, middle, gain_two,
-    suma, sumb, dw, grad_mid, g_attn, grad_att, wide, up_sum, q_sum, *scratch,
+    grad_qkv, normed_one, w, g_attn_one, attended_one, state, grad_mid_one, gain_one, dwu_one,
+    w_low, up_full, down_full, hidden, act, normed_two, middle, gain_two,
+    sumu_one, sumb_one, sumd, sumu, grad_mid, g_attn, grad_att, wide, up_sum, q_sum, *scratch,
 ):
-    sum1, sum2 = scratch[0:9], scratch[9:18]
-    g2, g3 = scratch[18:20], scratch[20:22]
-    pa, pb = scratch[22:24], scratch[24:26]
-    landa, landb, dwb, gradient, g_rows, grad_hid = scratch[26:32]
+    sum1, sum2 = scratch[0:NSUM], scratch[NSUM : 2 * NSUM]
+    sems = scratch[2 * NSUM : 2 * NSUM + 12]
+    landu_one, landb_one, landd, landu, dwb, dwd, dwu, gradient, g_rows, grad_hid = scratch[2 * NSUM + 12 :]
     me = Place()
     greet(me, True)
-    grads_start(me, dwa_one, landa, *pa)
+    grads_u_one = Grads(me, dwu_one, landu_one, *sems[4:6])
+    grads_b_one = Grads(me, dwb, landb_one, *sems[6:8])
+    grads_d = Grads(me, dwd, landd, *sems[8:10])
+    grads_u = Grads(me, dwu, landu, *sems[10:12])
+    grads_u_one.start()
     wide[...] = jnp.zeros_like(wide)
-
-    def more():
-        grads_start(me, dwb, landb, *pb)
-
     gradient[...] = first_back(
         me, grad_qkv, normed_one, w, g_attn_one, attended_one, state, grad_mid_one, gain_one, dwb, wide, 0, q_sum,
-        sum1, more,
+        sum1, grads_b_one.start,
     )
     g_rows[me.slot] = gradient[...].astype(BF16)
-    gather_start(me, g_rows, *g2)
+    gather1 = Gather(me, g_rows, *sems[0:2])
+    gather1.start()
     backward_rest(
-        me, gradient, g_rows, w_low, hidden, act, normed_two, middle, gain_two, grad_hid, dw, grad_mid, g_attn,
-        grad_att, wide, 2, up_sum, g2, sum2, g3,
-    )
-    grads_end(me, dwa_one, landa, *pa, suma)
-    grads_end(me, dwb, landb, *pb, sumb)
+        me, gradient, g_rows, w_low, up_full, down_full, hidden, act, normed_two, middle, gain_two, grad_hid, dwd, dwu,
+        grads_d.start, grads_u.start, grad_mid, g_attn, grad_att, wide, 2, up_sum, gather1, sum2,
+        Gather(me, g_attn, *sems[2:4]),
+    )
+    grads_u_one.end(sumu_one)
+    grads_b_one.end(sumb_one)
+    grads_d.end(sumd)
+    grads_u.end(sumu)
 
 
 def vectors_start(me, wide, va, vl, send, recv):
@@ -608,30 +773,25 @@
 
 
 def exit_kernel(
-    grad_qkv, normed_one, w, g_attn, attended, state, grad_mid, gain, dwa, wide_in, narrow_in,
-    gradient, suma, sumb, vectors, *scratch,
+    grad_qkv, normed_one, w, g_attn, attended, state, grad_mid, gain, wide_in, narrow_in,
+    gradient, sumb, vectors, *scratch,
 ):
-    sum1, pa, pb = scratch[0:9], scratch[9:11], scratch[11:13]
-    landa, landb, dwb, wide, q_sum, narrow, va, vl, vb, piece = scratch[13:23]
-    v1, v2, v3 = scratch[23:25], scratch[25:27], scratch[27:29]
+    sum1, scratch = scratch[0:NSUM], scratch[NSUM:]
+    landb, dwb, wide, q_sum, narrow, va, vl, vb, piece = scratch[0:9]
+    pb, v1, v2, v3 = scratch[9:11], scratch[11:13], scratch[13:15], scratch[15:17]
     me = Place()
     greet(me, True)
-    grads_start(me, dwa, landa, *pa)
-
-    def more():
-        grads_start(me, dwb, landb, *pb)
-
+    grads = Grads(me, dwb, landb, *pb)
     wide[...] = wide_in[...]
     gradient[...] = first_back(
-        me, grad_qkv, normed_one, w, g_attn, attended, state, grad_mid, gain, dwb, wide, 0, q_sum, sum1, more
+        me, grad_qkv, normed_one, w, g_attn, attended, state, grad_mid, gain, dwb, wide, 0, q_sum, sum1, grads.start
     )
     narrow[...] = narrow_in[...]
     narrow[0:1] = q_sum[:, 0:128]
     narrow[1:2] = q_sum[:, 256:384]
     vectors_start(me, wide, va, vl, *v1)
     vectors_end(me, narrow, va, vl, *v1, vb, piece, *v2, vectors, *v3)
-    grads_end(me, dwa, landa, *pa, suma)
-    grads_end(me, dwb, landb, *pb, sumb)
+    grads.end(sumb)
 
 
 def key_mask(shape, dim, length):
@@ -721,15 +881,8 @@
     x = padded(swap(x_in))
     cot = padded(swap(cotangent))
     length = swap(valid_len)
-    shards = jnp.concatenate(
-        [
-            w_qkv.reshape(2, 64, 384),
-            jnp.swapaxes(w_out, 1, 2),
-            w_up,
-            jnp.swapaxes(w_down, 1, 2),
-        ],
-        axis=2,
-    )
+    qo_shards = jnp.concatenate([w_qkv.reshape(2, 64, 384), jnp.swapaxes(w_out, 1, 2)], axis=2)
+    down_shards = jnp.swapaxes(w_down, 1, 2)
     gain = [[norm_gain[l, i][None] for i in range(2)] for l in range(2)]
     shift = [[norm_shift[l, i][None] for i in range(2)] for l in range(2)]
     bias_rows = [[bias[l, i][None] for i in range(4)] for l in range(2)]
@@ -740,92 +893,90 @@
     ]
     ubias = [own_up[l][None] for l in range(2)]
 
-    rows_all, rows_own = (MEMBERS, PAD, D), (PAD, D)
+    rows_all, rows_own, part = (MEMBERS, PAD, D), (PAD, D), (16, 64, 512)
+    hid, att, summed = (MEMBERS, PAD, HID), (MEMBERS, PAD, COLS), (64, 512)
     qkv0, normed0, w0 = call(
         enter_kernel,
-        [((MEMBERS, PAD, 384), BF16), (rows_all, BF16), ((16, 64, WCOLS), BF16)],
+        [((MEMBERS, PAD, 384), BF16), (rows_all, BF16), (part, BF16)],
         GATHER_SEMS + PLANE_SEMS,
         0,
-        [x, shards[0], gain[0][0], shift[0][0], qbias[0]],
+        [x, qo_shards[0], gain[0][0], shift[0][0], qbias[0]],
         1 << 30,
     )
     attended0 = attention(attend_kernel, length, [qkv0], COLS)
-    middle0, normed_two0, hidden0, act0, state1, normed1, qkv1, w1 = call(
+    middle0, normed_two0, hidden0, act0, state1, normed1, qkv1, wup0, wdown0, w1 = call(
         between_kernel,
         [
             (rows_own, F32),
             (rows_all, BF16),
-            ((MEMBERS, PAD, HID), F32),
-            ((MEMBERS, PAD, HID), BF16),
+            (hid, F32),
+            (hid, BF16),
             (rows_own, F32),
             (rows_all, BF16),
             ((MEMBERS, PAD, 384), BF16),
-            ((16, 64, WCOLS), BF16),
+            (part, BF16),
+            (part, BF16),
+            (part, BF16),
         ],
-        SUM_SCRATCH * 2 + GATHER_SEMS * 2 + PLANE_SEMS,
+        SUM_SCRATCH * 2 + GATHER_SEMS * 2 + PLANE_SEMS * 3,
         1,
         [
-            attended0, x, w0, shards[1], gain[0][1], shift[0][1], bias_rows[0][2], ubias[0], bias_rows[0][3],
-            gain[1][0], shift[1][0], qbias[1],
+            attended0, x, w0, w_up[0], down_shards[0], qo_shards[1], gain[0][1], shift[0][1], bias_rows[0][2], ubias[0],
+            bias_rows[0][3], gain[1][0], shift[1][0], qbias[1],
         ],
         4 << 30,
     )
     attended1 = attention(attend_kernel, length, [qkv1], COLS)
-    out_rows, dwa1, grad_mid1, g_attn1, grad_att1, wide1, up1 = call(
+    out_rows, sumd1, dwu1, grad_mid1, g_attn1, grad_att1, wide1, up1 = call(
         turn_kernel,
         [
             (rows_own, BF16),
-            ((16, 64, 1024), BF16),
+            (summed, F32),
+            (part, BF16),
             (rows_own, F32),
             (rows_all, BF16),
-            ((MEMBERS, PAD, COLS), BF16),
+            (att, BF16),
             ((8, D), F32),
             ((1, HID), F32),
         ],
         SUM_SCRATCH * 3
         + GATHER_SEMS * 3
-        + [
-            pltpu.VMEM(rows_own, F32),
-            pltpu.VMEM(rows_all, BF16),
-            pltpu.VMEM((MEMBERS, PAD, HID), F32),
-            pltpu.VMEM((MEMBERS, PAD, HID), BF16),
-            pltpu.VMEM(rows_all, BF16),
-            pltpu.VMEM((MEMBERS, PAD, HID), BF16),
+        + PLANE_SEMS * 3
+        + [pltpu.VMEM(rows_own, F32), pltpu.VMEM(rows_all, BF16), pltpu.VMEM(hid, F32), pltpu.VMEM(hid, BF16)]
+        + [pltpu.VMEM(rows_all, BF16), pltpu.VMEM(hid, BF16)]
+        + [pltpu.VMEM(part, BF16)] * 4,
+        2,
+        [
+            attended1, state1, w1, w_up[1], down_shards[1], cot, gain[1][1], shift[1][1], bias_rows[1][2], ubias[1],
+            bias_rows[1][3],
         ],
-        2,
-        [attended1, state1, w1, cot, gain[1][1], shift[1][1], bias_rows[1][2], ubias[1], bias_rows[1][3]],
         8 << 30,
     )
     out_rows = swap(out_rows[:ROWS])
     grad_qkv1 = attention(attend_back_kernel, length, [qkv1, grad_att1], 384)
-    suma1, sumb1, dwa0, grad_mid0, g_attn0, grad_att0, wide0, up0, q1 = call(
+    sumu1, sumb1, sumd0, sumu0, grad_mid0, g_attn0, grad_att0, wide0, up0, q1 = call(
         back_kernel,
         [
-            ((64, 1024), F32),
-            ((64, 512), F32),
-            ((16, 64, 1024), BF16),
+            (summed, F32),
+            (summed, F32),
+            (summed, F32),
+            (summed, F32),
             (rows_own, F32),
             (rows_all, BF16),
-            ((MEMBERS, PAD, COLS), BF16),
+            (att, BF16),
             ((8, D), F32),
             ((1, HID), F32),
             ((1, 384), F32),
         ],
         SUM_SCRATCH * 2
         + GATHER_SEMS * 2
-        + PLANE_SEMS * 2
-        + [
-            pltpu.VMEM((16, 64, 1024), BF16),
-            pltpu.VMEM((16, 64, 512), BF16),
-            pltpu.VMEM((16, 64, 512), BF16),
-            pltpu.VMEM(rows_own, F32),
-            pltpu.VMEM(rows_all, BF16),
-            pltpu.VMEM((MEMBERS, PAD, HID), BF16),
-        ],
+        + PLANE_SEMS * 4
+        + [pltpu.VMEM(part, BF16)] * 7
+        + [pltpu.VMEM(rows_own, F32), pltpu.VMEM(rows_all, BF16), pltpu.VMEM(hid, BF16)],
         3,
         [
-            grad_qkv1, normed1, w1, g_attn1, attended1, state1, grad_mid1, gain[1][0], dwa1,
-            w0, hidden0, act0, normed_two0, middle0, gain[0][1],
+            grad_qkv1, normed1, w1, g_attn1, attended1, state1, grad_mid1, gain[1][0], dwu1,
+            w0, wup0, wdown0, hidden0, act0, normed_two0, middle0, gain[0][1],
         ],
         8 << 30,
     )
@@ -833,10 +984,9 @@
     wide = jnp.concatenate(
         [jnp.zeros((2, D), F32), wide0[2:6], wide0[0:2], wide1[0:4], jnp.zeros((4, D), F32)], axis=0
     )
-    zeros = jnp.zeros((2, COLS), F32)
     narrow = jnp.concatenate(
         [
-            zeros,
+            jnp.zeros((2, COLS), F32),
             up0.reshape(4, COLS),
             q1[:, 0:COLS],
             q1[:, 2 * COLS :],
@@ -845,15 +995,13 @@
         ],
         axis=0,
     )
-    gradient, suma0, sumb0, vectors = call(
+    gradient, sumb0, vectors = call(
         exit_kernel,
-        [(rows_own, F32), ((64, 1024), F32), ((64, 512), F32), ((MEMBERS, 32, 128), F32)],
+        [(rows_own, F32), (summed, F32), ((MEMBERS, 32, 128), F32)],
         SUM_SCRATCH
-        + PLANE_SEMS * 2
         + [
-            pltpu.VMEM((16, 64, 1024), BF16),
-            pltpu.VMEM((16, 64, 512), BF16),
-            pltpu.VMEM((16, 64, 512), BF16),
+            pltpu.VMEM(part, BF16),
+            pltpu.VMEM(part, BF16),
             pltpu.VMEM((16, D), F32),
             pltpu.VMEM((1, 384), F32),
             pltpu.VMEM((16, 128), F32),
@@ -862,14 +1010,15 @@
             pltpu.VMEM((16, 32, 128), F32),
             pltpu.VMEM((32, 128), F32),
         ]
+        + PLANE_SEMS
         + [pltpu.SemaphoreType.DMA((8,))] * 2
         + PLANE_SEMS
         + [pltpu.SemaphoreType.DMA((8,))] * 2,
         4,
-        [grad_qkv0, normed0, w0, g_attn0, attended0, x, grad_mid0, gain[0][0], dwa0, wide, narrow],
+        [grad_qkv0, normed0, w0, g_attn0, attended0, x, grad_mid0, gain[0][0], wide, narrow],
         4 << 30,
     )
-    suma, sumb = jnp.stack([suma0, suma1]), jnp.stack([sumb0, sumb1])
+    sumb = jnp.stack([sumb0, sumb1])
     full = jnp.transpose(vectors[:, 0:12], (1, 0, 2)).reshape(2, 6, D)
     own = vectors[:, 16:28].reshape(MEMBERS, 2, 6, COLS)
     q_bias = jnp.transpose(own[:, :, 0], (1, 0, 2)).reshape(2, D)
@@ -879,8 +1028,8 @@
         swap(gradient[:ROWS]),
         sumb[:, :, 0:384].reshape(2, 64, 3, COLS),
         jnp.swapaxes(sumb[:, :, 384:], 1, 2),
-        suma[:, :, 0:HID],
-        jnp.swapaxes(suma[:, :, HID:], 1, 2),
+        jnp.stack([sumu0, sumu1]),
+        jnp.swapaxes(jnp.stack([sumd0, sumd1]), 1, 2),
         jnp.stack([full[:, 0], full[:, 3]], axis=1),
         jnp.stack([full[:, 1], full[:, 4]], axis=1),
         jnp.stack([q_bias, v_bias, full[:, 5], full[:, 2]], axis=1),

time: 524 us -> 417 us (0.80)
  Pallas kernels: 478 us -> 370 us
    pallas_call x5, Pallas kernels: 448 us -> 340 us  [call(): pl.pallas_call(kernel, out_shape=[jax.ShapeDtypeStruct(s, t) for s, t in...]
  transfers between devices with their start and end apart: 5 -> 5, of which waited for: 1 -> 1; matrix products, arithmetic and copies ran while one was open for 3% -> 4% of each run, Pallas kernels for 34% -> 29%
where the time goes in v2:
time: 417 us
  Pallas kernels  370 us (89%)
  local copies, waits for them, and re-layouts  19.7 us (5%)
  starting transfers between devices  16.2 us (4%)
  other arithmetic  6.07 us (1%)
    pallas_call x5, Pallas kernels, call(): pl.pallas_call(kernel, out_shape=[jax.ShapeDtypeStruct(s, t) for s, t in...  340 us
    pallas_call x4, Pallas kernels, attention(): pl.pallas_call(kernel, grid=(2,), out_shape=jax.ShapeDtypeStruct((MEMBERS...  29.3 us
    ppermute x5, starting transfers between devices, swap(): return lax.ppermute(value, ('dp', 'tensor'), pairs)  16.2 us
  transfers between devices with their start and end apart: 5, of which 1 were waited for; matrix products, arithmetic and copies ran while one was open for 4% of the time, Pallas kernels for 29%

profile of v2, /device:TPU:1, one launch (start us, length us, event | category | flops | bytes accessed | tf_op | source)
XLA Modules:
  0.0 416.5 jit_solution(10817511043187558472)
XLA Ops:
  0.7 5.1 %collective-permute-start = (s32[2]{0:T(128)}, s32[2]{0:T(128)S(1)}, u32[]{:S(2)}, u32[]{:S(2)}) collective-permute-start(s32[2]{0:T(128)} %param.12), channel_id=1, source_target_pairs={{0,0},{1,1},{2,2},{3,3},{4,8},{5,9},{6,10},{7,11},{8,4},{9,5},{10,... | collective-permute-start | bytes 32 | tf_op jit(solution)/shard_map/ppermute | solution.py:869
  5.7 1.9 collective-permute-start.1
  7.7 3.6 collective-permute-start.2
  11.4 1.4 slice_bitcast_fusion.6
  14.7 1.4 fusion.5
  16.1 1.4 slice_bitcast_fusion.8
  17.6 1.4 fusion.14
  19.0 1.6 slice_bitcast_fusion
  21.4 30.2 %shard_map.186 = (bf16[8,160,384]{2,1,0:T(8,128)(2,1)}, bf16[8,160,1024]{2,1,0:T(8,128)(2,1)}, bf16[16,64,512]{2,1,0:T(8,128)(2,1)}) custom-call(bf16[160,1024]{1,0:T(8,128)(2,1)} %pad.7.x.state, bf16[64,512]{1,0:T(8,128)(2,1)} %get-tuple-element.115.shard, f32[1,1024]{1,0:T(1,128)} %get-tuple-element.147.gain, f32[1,1024]{1,0:T(1,128)} %get-tuple-element.136.shift, ...), custom_call_target="tpu_custom_call" | custom-call | flops 1073741824 | bytes 1048576 | tf_op jit(solution)/shard_map/pallas_call | solution.py:463
  52.1 5.9 %shard_map.187.attended = bf16[8,160,128]{2,1,0:T(8,128)(2,1)} custom-call(s32[2]{0:T(128)} %copy-done.8, bf16[8,160,384]{2,1,0:T(8,128)(2,1)} %get-tuple-element.44.qkv), custom_call_target="tpu_custom_call" | custom-call | tf_op jit(solution)/shard_map/pallas_call | solution.py:852
  58.0 77.7 %shard_map.188 = (f32[160,1024]{1,0:T(8,128)}, bf16[8,160,1024]{2,1,0:T(8,128)(2,1)}, f32[8,160,512]{2,1,0:T(8,128)}, bf16[8,160,512]{2,1,0:T(8,128)(2,1)}, f32[...) custom-call(bf16[8,160,128]{2,1,0:T(8,128)(2,1)} %shard_map.187.atte, ...), custom_call_target="tpu_custom_call" | custom-call | flops 4294967296 | bytes 1048576 | tf_op jit(solution)/shard_map/pallas_call | solution.py:463
  135.8 5.9 %shard_map.189.attended.attended_one = bf16[8,160,128]{2,1,0:T(8,128)(2,1)} custom-call(s32[2]{0:T(128)} %copy-done.8, bf16[8,160,384]{2,1,0:T(8,128)(2,1)} %get-tuple-element.46.qkv), custom_call_target="tpu_custom_call" | custom-call | tf_op jit(solution)/shard_map/pallas_call | solution.py:852
  142.4 101.1 %shard_map.190 = (bf16[160,1024]{1,0:T(8,128)(2,1)}, f32[64,512]{1,0:T(8,128)}, bf16[16,64,512]{2,1,0:T(8,128)(2,1)}, f32[160,1024]{1,0:T(8,128)}, bf16[8,160,10...) custom-call(bf16[8,160,128]{2,1,0:T(8,128)(2,1)} %shard_map.189.attended.attended_one, ...), custom_call_target="tpu_custom_call" | custom-call | flops 8589934592 | bytes 1048576 | tf_op jit(solution)/shard_map/pallas_call | solution.py:463
  243.6 8.7 %shard_map.191.grad_qkv = bf16[8,160,384]{2,1,0:T(8,128)(2,1)} custom-call(s32[2]{0:T(128)} %copy-done.8, bf16[8,160,384]{2,1,0:T(8,128)(2,1)} %get-tuple-element.46.qkv, bf16[8,160,128]{2,1,0:T(8,128)(2,1)} %get-tuple-element.50.grad), custom_call_target="tpu_custom_call" | custom-call | tf_op jit(solution)/shard_map/pallas_call | solution.py:852
  252.3 86.2 %shard_map.192 = (f32[64,512]{1,0:T(8,128)}, f32[64,512]{1,0:T(8,128)}, f32[64,512]{1,0:T(8,128)}, f32[64,512]{1,0:T(8,128)}, f32[160,1024]{1,0:T(8,128)}, /*ind...) custom-call(bf16[8,160,384]{2,1,0:T(8,128)(2,1)} %shard_map.191.grad, ...), custom_call_target="tpu_custom_call" | custom-call | flops 8589934592 | bytes 1048576 | tf_op jit(solution)/shard_map/pallas_call | solution.py:463
  340.7 1.3 concatenate.18.wide_in
  342.0 1.9 concatenate.19.narrow_in
  343.9 8.8 %shard_map.193.grad_qkv = bf16[8,160,384]{2,1,0:T(8,128)(2,1)} custom-call(s32[2]{0:T(128)} %copy-done.8, bf16[8,160,384]{2,1,0:T(8,128)(2,1)} %get-tuple-element.44.qkv, bf16[8,160,128]{2,1,0:T(8,128)(2,1)} %get-tuple-element.61.grad), custom_call_target="tpu_custom_call" | custom-call | tf_op jit(solution)/shard_map/pallas_call | solution.py:852
  352.6 45.0 %shard_map.194 = (f32[160,1024]{1,0:T(8,128)}, f32[64,512]{1,0:T(8,128)}, f32[8,32,128]{2,1,0:T(8,128)}) custom-call(bf16[8,160,384]{2,1,0:T(8,128)(2,1)} %shard_map.193.grad_qkv, bf16[8,160,1024]{2,1,0:T(8,128)(2,1)} %get-tuple-element.62.normed_one, bf16[16,64,512]{2,1,0:T(8,128)(2,1)} %get-tuple-element.45.w.w_low, ...), custom_call_target="tpu_custom_call" | custom-call | flops 4294967296 | bytes 1048576 | tf_op jit(solution)/shard_map/pallas_call | solution.py:463
  397.7 1.0 fusion.11
  398.8 3.5 collective-permute-start.3
  402.3 1.1 slice.162
  403.4 2.1 collective-permute-start.4
  411.0 4.0 collective-permute-done.4
  (60 shorter events, 13.2 us)
Async XLA Ops:
  0.6 10.7 %copy-start = (bf16[2,64,3,128]{3,1,2,0:T(8,128)(2,1)S(1)}, bf16[2,64,3,128]{3,1,2,0:T(8,128)(2,1)}, u32[]{:S(2)}) copy-start(bf16[2,64,3,128]{3,1,2,0:T(8,128)(2,1)} %param.13) | copy-start | bytes 294916
  0.7 50.9 %collective-permute-start = (s32[2]{0:T(128)}, s32[2]{0:T(128)S(1)}, u32[]{:S(2)}, u32[]{:S(2)}) collective-permute-start(s32[2]{0:T(128)} %param.12), channel_id=1, source_target_pairs={{0,0},{1,1},{2,2},{3,3},{4,8},{5,9},{6,10},{7,11},{8,4},{9,5},{10,... | collective-permute-start | bytes 32 | tf_op jit(solution)/shard_map/ppermute | solution.py:869
  5.7 14.9 %collective-permute-start.1 = (bf16[146,1024]{1,0:T(8,128)(2,1)}, bf16[146,1024]{1,0:T(8,128)(2,1)S(1)}, u32[]{:S(2)}, u32[]{:S(2)}) collective-permute-start(bf16[146,1024]{1,0:T(8,128)(2,1)} %param.11), channel_id=1, source_target_pairs={{0,0},{1,1},{2,2},{3,3},{4,8},{5,9},{6,10},{7,11},{8,4},{9,5},{10,... | collective-permute-start | bytes 897032 | tf_op jit(solution)/shard_map/ppermute | solution.py:869
  7.7 134.0 %collective-permute-start.2 = (bf16[146,1024]{1,0:T(8,128)(2,1)}, bf16[146,1024]{1,0:T(8,128)(2,1)S(1)}, u32[]{:S(2)}, u32[]{:S(2)}) collective-permute-start(bf16[146,1024]{1,0:T(8,128)(2,1)} %param.21), channel_id=1, source_target_pairs={{0,0},{1,1},{2,2},{3,3},{4,8},{5,9},{6,10},{7,11},{8,4},{9,5},{10,... | collective-permute-start | bytes 897032 | tf_op jit(solution)/shard_map/ppermute | solution.py:869
  51.6 0.5 copy-start.8
  252.3 87.7 %copy-start.9 = (f32[8,1024]{1,0:T(8,128)S(1)}, f32[8,1024]{1,0:T(8,128)}, u32[]{:S(2)}) copy-start(f32[8,1024]{1,0:T(8,128)} %get-tuple-element.66) | copy-start | bytes 98308
  252.3 89.7 %copy-start.10 = (f32[1,512]{1,0:T(1,128)S(1)}, f32[1,512]{1,0:T(1,128)}, u32[]{:S(2)}) copy-start(f32[1,512]{1,0:T(1,128)} %get-tuple-element.69) | copy-start | bytes 6148
  352.6 46.1 %copy-start.3 = (bf16[160,1024]{1,0:T(8,128)(2,1)S(1)}, bf16[160,1024]{1,0:T(8,128)(2,1)}, u32[]{:S(2)}) copy-start(bf16[160,1024]{1,0:T(8,128)(2,1)} %get-tuple-element.49) | copy-start | bytes 983044
  397.7 9.9 %copy-start.1 = (f32[64,512]{1,0:T(8,128)S(1)}, f32[64,512]{1,0:T(8,128)}, u32[]{:S(2)}) copy-start(f32[64,512]{1,0:T(8,128)} %get-tuple-element.72) | copy-start | bytes 393220
  397.7 9.8 %copy-start.2 = (f32[64,512]{1,0:T(8,128)S(1)}, f32[64,512]{1,0:T(8,128)}, u32[]{:S(2)}) copy-start(f32[64,512]{1,0:T(8,128)} %get-tuple-element.71) | copy-start | bytes 393220
  397.7 11.8 %copy-start.6 = (f32[64,512]{1,0:T(8,128)S(1)}, f32[64,512]{1,0:T(8,128)}, u32[]{:S(2)}) copy-start(f32[64,512]{1,0:T(8,128)} %get-tuple-element.74) | copy-start | bytes 393220
  397.7 11.8 %copy-start.7 = (f32[64,512]{1,0:T(8,128)S(1)}, f32[64,512]{1,0:T(8,128)}, u32[]{:S(2)}) copy-start(f32[64,512]{1,0:T(8,128)} %get-tuple-element.73) | copy-start | bytes 393220
  397.7 12.5 %copy-start.4 = (f32[64,512]{1,0:T(8,128)S(1)}, f32[64,512]{1,0:T(8,128)}, u32[]{:S(2)}) copy-start(f32[64,512]{1,0:T(8,128)} %get-tuple-element.76) | copy-start | bytes 393220
  397.7 12.5 %copy-start.5 = (f32[64,512]{1,0:T(8,128)S(1)}, f32[64,512]{1,0:T(8,128)}, u32[]{:S(2)}) copy-start(f32[64,512]{1,0:T(8,128)} %get-tuple-element.75) | copy-start | bytes 393220
  398.8 12.1 %collective-permute-start.3 = (bf16[146,1024]{1,0:T(8,128)(2,1)S(1)}, bf16[146,1024]{1,0:T(8,128)(2,1)S(1)}, u32[]{:S(2)}, u32[]{:S(2)}) collective-permute-start(bf16[146,1024]{1,0:T(8,128)(2,1)S(1)} %slice.156), channel_id=1, source_target_pairs={{0,0},{1,1},{2,2},{3,3},{4,8},{5,9},{6,10},{7,11},{8,4},{9,5},{10,... | collective-permute-start | bytes 897032 | tf_op jit(solution)/shard_map/ppermute | solution.py:869
  403.4 11.6 %collective-permute-start.4 = (f32[146,1024]{1,0:T(8,128)S(1)}, f32[146,1024]{1,0:T(8,128)S(1)}, u32[]{:S(2)}, u32[]{:S(2)}) collective-permute-start(f32[146,1024]{1,0:T(8,128)S(1)} %slice.162), channel_id=1, source_target_pairs={{0,0},{1,1},{2,2},{3,3},{4,8},{5,9},{6,10},{7,11},{8,4},{9,5},{10,... | collective-permute-start | bytes 1794056 | tf_op jit(solution)/shard_map/ppermute | solution.py:869

commit v3 on v2

v3 whole, which is shorter than its diff:
```python
import types

import jax
import jax.numpy as jnp
from jax import lax
from jax.experimental import pallas as pl
from jax.experimental.pallas import tpu as pltpu
from jax.sharding import PartitionSpec as P

MESH = pl.DeviceIdType.MESH
F32, BF16 = jnp.float32, jnp.bfloat16

D = 1024
ROWS = 146
PAD = 160
COLS = 128
HEAD = 64
HID = 512
MEMBERS = 8
WCOLS = 1536
EPSILON = 1e-06
NEG_FILL = -1e30
VMEM_BYTES = 64 * 1024 * 1024 - 65536

NN = (((1,), (0,)), ((), ()))
NT = (((1,), (1,)), ((), ()))
TN = (((0,), (0,)), ((), ()))


def dot(a, b, dims=NN):
    return lax.dot_general(a, b, dims, preferred_element_type=F32)


class Place:
    def __init__(self):
        self.dp = lax.axis_index("dp")
        self.tensor = lax.axis_index("tensor")
        self.core = self.dp % 2
        self.pair = self.dp // 2
        self.zlo = self.tensor // 4
        self.x = self.tensor % 4
        self.slot = self.core * 4 + self.x
        self.group = self.pair * 2 + self.zlo

    def peer(self, core, x):
        return {"dp": self.pair * 2 + core, "tensor": self.zlo * 4 + x}

    def sibling(self):
        return self.peer(1 - self.core, self.x)


def greet(me, plane):
    barrier = pltpu.get_barrier_semaphore()

    def member(i, carry):
        pl.semaphore_signal(
            barrier,
            inc=1,
            device_id=me.peer((me.core + i // 4) % 2, (me.x + i) % 4),
            device_id_type=MESH,
        )
        return carry

    lax.fori_loop(1, MEMBERS, member, 0)
    count = MEMBERS - 1
    if plane:

        def other(i, carry):
            pair = (me.pair + i // 4) % 8
            zlo = (me.zlo + (i // 2) % 2) % 2
            pl.semaphore_signal(
                barrier,
                inc=1,
                device_id={"dp": pair * 2 + i % 2, "tensor": zlo * 4 + me.x},
                device_id_type=MESH,
            )
            return carry

        lax.fori_loop(2, 32, other, 0)
        count += 30
    pl.semaphore_wait(barrier, count)


def remote(src, dst, send, recv, device):
    return pltpu.make_async_remote_copy(
        src_ref=src,
        dst_ref=dst,
        send_sem=send,
        recv_sem=recv,
        device_id=device,
        device_id_type=MESH,
    )


def slot_at(me, i):
    sibling = (i == 1) | (i == 4) | (i == 5) | (i == 7)
    far = (i >= 6).astype(jnp.int32) * 2
    left = ((i == 2) | (i == 4)).astype(jnp.int32) * 3
    right = ((i == 3) | (i == 5)).astype(jnp.int32)
    core = (me.core + sibling.astype(jnp.int32)) % 2
    return core * 4 + (me.x + far + left + right) % 4


HALF = PAD // 2
TOP, BOTTOM = pl.ds(0, HALF), pl.ds(HALF, HALF)


class Gather:
    def __init__(self, me, g, send, recv):
        self.me, self.g, self.send, self.recv = me, g, send, recv
        self.right = me.peer(me.core, (me.x + 1) % 4)
        self.left = me.peer(me.core, (me.x + 3) % 4)
        self.from_left = me.core * 4 + (me.x + 3) % 4
        self.from_right = me.core * 4 + (me.x + 1) % 4
        self.from_far = me.core * 4 + (me.x + 2) % 4

    def copy(self, k, slot, rows, device):
        block = self.g.at[slot] if rows is None else self.g.at[slot, rows]
        return remote(block, block, self.send.at[k], self.recv.at[k], device)

    def table(self):
        me = self.me
        sibling = me.sibling()
        return [
            (0, me.slot, TOP, self.right),
            (1, me.slot, BOTTOM, self.right),
            (2, me.slot, TOP, self.left),
            (3, me.slot, BOTTOM, self.left),
            (4, self.from_left, TOP, self.right),
            (5, self.from_right, BOTTOM, self.left),
            (6, me.slot, None, sibling),
            (7, self.from_left, None, sibling),
            (8, self.from_right, None, sibling),
            (9, self.from_far, None, sibling),
        ]

    def start_copies(self, *which):
        for k in which:
            self.copy(*self.table()[k]).start()

    def start(self):
        self.start_copies(6, 0, 3, 1, 2)

    def arrived(self, *which):
        for k in which:
            _, slot, rows, device = self.table()[k]
            self.copy(k, slot, rows, device).wait_recv()

    def relay(self):
        self.arrived(0)
        self.start_copies(4)
        self.arrived(3)
        self.start_copies(5)

    def run(self, consume, fill=None, relayed=False):
        def step(i, carry):
            @pl.when(i == 1)
            def _():
                self.arrived(6)

            @pl.when(i == 2)
            def _():
                if not relayed:
                    self.relay()
                if fill is not None:
                    fill()
                self.arrived(1)
                self.start_copies(7)

            @pl.when(i == 3)
            def _():
                self.arrived(2)
                self.start_copies(8)

            @pl.when(i == 4)
            def _():
                self.arrived(7)

            @pl.when(i == 5)
            def _():
                self.arrived(8)

            @pl.when(i == 6)
            def _():
                self.arrived(4, 5)
                self.start_copies(9)

            @pl.when(i == 7)
            def _():
                self.arrived(9)

            consume(slot_at(self.me, i))
            return carry

        lax.fori_loop(0, MEMBERS, step, 0)

    def end(self):
        for row in self.table():
            self.copy(*row).wait_send()


GATHER_SEMS = [pltpu.SemaphoreType.DMA((10,)), pltpu.SemaphoreType.DMA((10,))]

SUM_SEND = [
    pltpu.VMEM((4, PAD, D), BF16),
    pltpu.VMEM((3, PAD, D), BF16),
    pltpu.VMEM((PAD, D), F32),
    pltpu.VMEM((2, HALF, D), F32),
]
SUM_LAND = [
    pltpu.VMEM((4, PAD, D), BF16),
    pltpu.VMEM((PAD, D), BF16),
    pltpu.VMEM((2, PAD, D), BF16),
    pltpu.SemaphoreType.DMA((4,)),
    pltpu.SemaphoreType.DMA((4,)),
    pltpu.SemaphoreType.DMA((6,)),
    pltpu.SemaphoreType.DMA((6,)),
]


def sum_rows(me, produce, send_bufs, land_bufs, fill=None):
    s1, s2, acc, hold = send_bufs
    r1, ra, rb, ss1, rs1, ss2, rs2 = land_bufs
    sibling = me.sibling()
    right, left = me.peer(me.core, (me.x + 1) % 4), me.peer(me.core, (me.x + 3) % 4)

    def chip(i):
        return (me.x + 2 + (i == 1).astype(jnp.int32) * 3 + (i == 2).astype(jnp.int32) + (i == 3).astype(jnp.int32) * 2) % 4

    def to_sibling(i):
        return remote(s1.at[i], r1.at[i], ss1.at[i], rs1.at[i], sibling)

    def along(k):
        src, dst, device = (
            (s2.at[0, TOP], ra.at[TOP], right),
            (s2.at[0, BOTTOM], ra.at[BOTTOM], left),
            (s2.at[1, BOTTOM], rb.at[0, BOTTOM], right),
            (s2.at[2, TOP], rb.at[1, TOP], left),
            (s2.at[1, TOP], rb.at[0, TOP], right),
            (s2.at[2, BOTTOM], rb.at[1, BOTTOM], left),
        )[k]
        return remote(src, dst, ss2.at[k], rs2.at[k], device)

    def for_sibling(i, carry):
        s1[i] = produce((1 - me.core) * 4 + chip(i)).astype(BF16)
        to_sibling(i).start()
        return carry

    def own(i, carry):
        part = produce(me.core * 4 + chip(i))
        to_sibling(i).wait_recv()
        acc[...] = part + r1[i].astype(F32)

        @pl.when(i == 0)
        def _():
            s2[0] = acc[...].astype(BF16)
            along(0).start()
            along(1).start()

        @pl.when(i == 1)
        def _():
            s2[1, BOTTOM] = acc[BOTTOM].astype(BF16)
            along(2).start()
            hold[0] = acc[TOP]

        @pl.when(i == 2)
        def _():
            s2[2, TOP] = acc[TOP].astype(BF16)
            along(3).start()
            hold[1] = acc[BOTTOM]

        @pl.when(i < 2)
        def _():
            for_sibling(i + 2, 0)

        return carry

    lax.fori_loop(0, 2, for_sibling, 0)
    lax.fori_loop(0, 4, own, 0)
    along(0).wait_recv()
    s2[1, TOP] = (hold[0] + ra[TOP].astype(F32)).astype(BF16)
    along(4).start()
    along(1).wait_recv()
    s2[2, BOTTOM] = (hold[1] + ra[BOTTOM].astype(F32)).astype(BF16)
    along(5).start()
    if fill is not None:
        fill()
    for k in range(2, 6):
        along(k).wait_recv()
    total = acc[...] + rb[0].astype(F32) + rb[1].astype(F32)
    for i in range(4):
        to_sibling(i).wait_send()
    for k in range(6):
        along(k).wait_send()
    return total


PLANE_SEMS = [pltpu.SemaphoreType.DMA((16,)), pltpu.SemaphoreType.DMA((16,))]


def weights_copy(me, i, shard, full, send, recv):
    pair, zlo = (me.pair + i // 2) % 8, (me.zlo + i) % 2
    device = {"dp": pair * 2 + me.zlo, "tensor": zlo * 4 + me.x}
    return remote(shard, full.at[me.dp], send.at[i], recv.at[me.dp], device)


def weights_start(me, shard, full, send, recv):
    def step(i, carry):
        weights_copy(me, i, shard, full, send, recv).start()
        return carry

    own = me.core == me.zlo

    @pl.when(own)
    def _():
        pltpu.make_async_copy(shard, full.at[me.dp], recv.at[me.dp]).start()

    @pl.when(jnp.logical_not(own))
    def _():
        weights_copy(me, 0, shard, full, send, recv).start()

    lax.fori_loop(1, 16, step, 0)


def weights_arrived(me, shard, full, send, recv):
    def step(i, carry):
        remote(shard, full.at[i], send.at[i], recv.at[i], me.sibling()).wait_recv()
        return carry

    lax.fori_loop(0, 16, step, 0)


def weights_sent(me, shard, full, send, recv):
    @pl.when(me.core != me.zlo)
    def _():
        weights_copy(me, 0, shard, full, send, recv).wait_send()

    def step(i, carry):
        weights_copy(me, i, shard, full, send, recv).wait_send()
        return carry

    lax.fori_loop(1, 16, step, 0)


def grads_copy(me, i, part, land, send, recv):
    to = (me.dp + i) % 16
    device = {"dp": to, "tensor": me.slot}
    return remote(part.at[to], land.at[me.group], send.at[i], recv.at[me.group], device)


def grads_start(me, part, land, send, recv):
    own = me.zlo == me.core

    @pl.when(own)
    def _():
        pltpu.make_async_copy(part.at[me.dp], land.at[me.group], recv.at[me.group]).start()

    @pl.when(jnp.logical_not(own))
    def _():
        grads_copy(me, 0, part, land, send, recv).start()

    def step(i, carry):
        grads_copy(me, i, part, land, send, recv).start()
        return carry

    lax.fori_loop(1, 16, step, 0)


def grads_end(me, part, land, send, recv, out):
    def arrived(i, carry):
        remote(part.at[0], land.at[i], send.at[i], recv.at[i], me.sibling()).wait_recv()
        return carry

    lax.fori_loop(0, 16, arrived, 0)

    @pl.when(me.zlo != me.core)
    def _():
        grads_copy(me, 0, part, land, send, recv).wait_send()

    def sent(i, carry):
        grads_copy(me, i, part, land, send, recv).wait_send()
        return carry

    lax.fori_loop(1, 16, sent, 0)
    total = land[0].astype(F32)
    for i in range(1, 16):
        total = total + land[i].astype(F32)
    out[...] = total


def normalized(rows):
    centred = rows - jnp.mean(rows, axis=-1, keepdims=True)
    scale = lax.rsqrt(jnp.mean(centred * centred, axis=-1, keepdims=True) + EPSILON)
    return centred * scale, scale


def layer_norm(rows, gain, shift):
    return normalized(rows)[0] * gain + shift


def layer_norm_back(rows, gain, grad):
    unit, scale = normalized(rows)
    inner = grad * gain
    mean_one = jnp.mean(inner, axis=-1, keepdims=True)
    mean_two = jnp.mean(inner * unit, axis=-1, keepdims=True)
    back = scale * (inner - mean_one - unit * mean_two)
    return back, jnp.sum(grad * unit, axis=0, keepdims=True), jnp.sum(grad, axis=0, keepdims=True)


def erf(v):
    v = jnp.clip(v, -4.0, 4.0)
    s = v * v
    top = F32(-2.72614225801306e-10)
    for a in (
        2.77068142495902e-08,
        -2.10102402082508e-06,
        -5.69250639462346e-05,
        -7.34990630326855e-04,
        -2.95459980854025e-03,
        -1.60960333262415e-02,
    ):
        top = top * s + F32(a)
    low = F32(-1.45660718464996e-05)
    for b in (
        -2.13374055278905e-04,
        -1.68282697438203e-03,
        -7.37332916720468e-03,
        -1.42647390514189e-02,
    ):
        low = low * s + F32(b)
    return v * top / low


def normal_below(v):
    return 0.5 * (1.0 + erf(v * F32(0.7071067811865476)))


def gelu_and_slope(v):
    below = normal_below(v)
    return v * below, below + v * jnp.exp(-0.5 * v * v) * F32(0.3989422804014327)


def weight_grad(left, right, out, at, width):
    def tile(i, carry):
        a = left[:, :, pl.ds(pl.multiple_of(i * 256, 256), 256)].reshape(MEMBERS * PAD, 256)
        b = right[...].reshape(MEMBERS * PAD, width)
        block = dot(a, b, TN).astype(BF16).reshape(4, 64, width)
        out[pl.ds(i * 4, 4), :, at : at + width] = block
        return carry

    lax.fori_loop(0, D // 256, tile, 0)


def columns(w, at, width):
    return w[:, :, at : at + width].reshape(D, width)


def column_sum(ref):
    def step(i, total):
        return total + jnp.sum(ref[i].astype(F32), axis=0, keepdims=True)

    return lax.fori_loop(0, MEMBERS, step, jnp.zeros((1, ref.shape[2]), F32))


def head_parts(qkv, i, at):
    return qkv[pl.ds(i * 4, 4), :, at * COLS : (at + 1) * COLS].reshape(4 * PAD, COLS)


def attend(qkv, mask, out):
    lane = lax.broadcasted_iota(jnp.int32, (1, COLS), 1)

    def image(i, carry):
        q, k, v = (head_parts(qkv, i, j) for j in range(3))
        valid = mask[i, 0:1] > 0.5
        total = None
        for h in range(2):
            mine = (lane >= h * HEAD) & (lane < (h + 1) * HEAD)
            scores = dot(jnp.where(mine, q, jnp.zeros_like(q)), k, NT) * F32(HEAD**-0.5)
            scores = jnp.where(valid, scores, NEG_FILL)
            e = jnp.exp(scores - jnp.max(scores, axis=-1, keepdims=True))
            prob = (e * (1.0 / jnp.sum(e, axis=-1, keepdims=True))).astype(BF16)
            mixed = dot(prob, v)
            total = mixed if total is None else jnp.where(mine, mixed, total)
        out[pl.ds(i * 4, 4)] = total.astype(BF16).reshape(4, PAD, COLS)
        return carry

    lax.fori_loop(0, 2, image, 0)


def attend_back(qkv, mask, grad):
    lane = lax.broadcasted_iota(jnp.int32, (1, COLS), 1)

    def image(i, carry):
        q, k, v = (head_parts(qkv, i, j) for j in range(3))
        g = grad[pl.ds(i * 4, 4)].reshape(4 * PAD, COLS)
        valid = mask[i].T[:, 0:1] > 0.5
        parts = [None, None, None]
        for h in range(2):
            mine = (lane >= h * HEAD) & (lane < (h + 1) * HEAD)
            scores = dot(k, jnp.where(mine, q, jnp.zeros_like(q)), NT) * F32(HEAD**-0.5)
            scores = jnp.where(valid, scores, NEG_FILL)
            e = jnp.exp(scores - jnp.max(scores, axis=0, keepdims=True))
            prob = e * (1.0 / jnp.sum(e, axis=0, keepdims=True))
            grad_value = dot(prob.astype(BF16), g)
            grad_prob = dot(v, jnp.where(mine, g, jnp.zeros_like(g)), NT)
            inner = jnp.sum(grad_prob * prob, axis=0, keepdims=True)
            grad_scores = (prob * (grad_prob - inner)).astype(BF16)
            grad_key = dot(grad_scores, q) * F32(HEAD**-0.5)
            grad_query = dot(grad_scores, k, TN) * F32(HEAD**-0.5)
            new = [grad_query, grad_key, grad_value]
            parts = new if h == 0 else [jnp.where(mine, n, p) for n, p in zip(new, parts)]
        for j in range(3):
            qkv[pl.ds(i * 4, 4), :, j * COLS : (j + 1) * COLS] = parts[j].astype(BF16).reshape(4, PAD, COLS)
        return carry

    lax.fori_loop(0, 2, image, 0)


def vectors_start(me, wide, va, vl, send, recv):
    for s in range(MEMBERS):
        va[s] = wide[:, s * 128 : (s + 1) * 128]

    def step(i, carry):
        core, x = (me.core + i // 4) % 2, (me.x + i) % 4
        remote(va.at[core * 4 + x], vl.at[i], send.at[i], recv.at[i], me.peer(core, x)).start()
        return carry

    lax.fori_loop(1, MEMBERS, step, 0)


def vectors_end(me, narrow, va, vl, send, recv, vb, piece, send2, recv2, out, send3, recv3):
    total = va[me.slot]
    for i in range(1, MEMBERS):
        remote(va.at[0], vl.at[i], send.at[i], recv.at[i], me.sibling()).wait()
        total = total + vl[i]
    piece[0:16] = total
    piece[16:32] = narrow[...]

    def to_group(i):
        pair, zlo = (me.pair + i // 2) % 8, (me.zlo + i) % 2
        device = {"dp": pair * 2 + me.core, "tensor": zlo * 4 + me.x}
        return remote(piece, vb.at[me.group], send2.at[i], recv2.at[me.group], device)

    def start(i, carry):
        to_group(i).start()
        return carry

    lax.fori_loop(1, 16, start, 0)
    vb[me.group] = piece[...]

    def end(i, carry):
        to_group(i).wait_send()
        group = (me.group + i) % 16
        remote(piece, vb.at[group], send2.at[i], recv2.at[group], me.sibling()).wait_recv()
        return carry

    lax.fori_loop(1, 16, end, 0)
    total = vb[0]
    for i in range(1, 16):
        total = total + vb[i]
    out[me.slot] = total
    own = out.at[me.slot]

    def to_member(i):
        core, x = (me.core + i // 4) % 2, (me.x + i) % 4
        return remote(own, own, send3.at[i], recv3.at[me.slot], me.peer(core, x))

    def start_three(i, carry):
        to_member(i).start()
        return carry

    lax.fori_loop(1, MEMBERS, start_three, 0)

    def end_three(i, carry):
        to_member(i).wait_send()
        slot = ((me.core + i // 4) % 2) * 4 + (me.x + i) % 4
        remote(own, out.at[slot], send3.at[i], recv3.at[slot], me.sibling()).wait_recv()
        return carry

    lax.fori_loop(1, MEMBERS, end_three, 0)


class Weights:
    def __init__(self, me, shard, full, send, recv):
        self.args, self.full = (me, shard, full, send, recv), full

    def start(self):
        weights_start(*self.args)

    def arrived(self):
        weights_arrived(*self.args)

    def sent(self):
        weights_sent(*self.args)


class Grads:
    def __init__(self, me, part, land, send, recv, out):
        self.args, self.part = (me, part, land, send, recv, out), part

    def start(self):
        grads_start(*self.args[:5])

    def end(self):
        grads_end(*self.args)


class Swap:
    def __init__(self, me, src, dst, sems, k):
        self.away = me.core != me.zlo
        self.src, self.dst = src, dst
        partner = {"dp": me.pair * 2 + me.zlo, "tensor": me.core * 4 + me.x}
        self.copy = remote(src, dst, sems[0].at[k], sems[1].at[k], partner)

    def start(self):
        @pl.when(self.away)
        def _():
            self.copy.start()

    def end(self):
        @pl.when(self.away)
        def _():
            self.copy.wait()

        @pl.when(jnp.logical_not(self.away))
        def _():
            self.dst[...] = self.src[...]


ROWS_ALL, ROWS_OWN, PART = (MEMBERS, PAD, D), (PAD, D), (16, 64, 512)
HID_ALL, ATT_ALL, QKV_ALL, SUMMED = (MEMBERS, PAD, HID), (MEMBERS, PAD, COLS), (MEMBERS, PAD, 384), (64, 512)
DMA = pltpu.SemaphoreType.DMA

INPUTS = ("x_in", "cot_in", "mask_in", "shards", "gain", "shift", "bias", "qbias", "ubias")
OUTPUTS = {
    "out_rows": (ROWS_OWN, BF16),
    "gradient": (ROWS_OWN, F32),
    "sum_qo": ((2, *SUMMED), F32),
    "sum_up": ((2, *SUMMED), F32),
    "sum_down": ((2, *SUMMED), F32),
    "vectors": ((MEMBERS, 32, 128), F32),
}


def scratch_table():
    table = {"padded": pltpu.VMEM(ROWS_OWN, F32)}

    def add(name, shape, dtype, count=None):
        if count is None:
            table[name] = pltpu.VMEM(shape, dtype)
        for i in range(count or 0):
            table[f"{name}{i}"] = pltpu.VMEM(shape, dtype)

    for name in ("x_own", "x_rows", "cot_own", "cot_rows", "rows_away", "rows_home"):
        add(name, ROWS_OWN, BF16)
    add("mask", (2, 8, 4 * PAD), F32)
    for name in ("qo", "up", "down", "land_qo", "land_up", "land_down"):
        add(name, PART, BF16, 2)
    for name in ("dw_qo", "dw_up", "dw_down"):
        add(name, PART, BF16)
    add("normed_one", ROWS_ALL, BF16, 2)
    add("normed_two", ROWS_ALL, BF16, 2)
    add("qkv", QKV_ALL, BF16, 2)
    add("attended", ATT_ALL, BF16, 2)
    add("slope", HID_ALL, BF16, 2)
    add("act", HID_ALL, BF16, 2)
    add("middle", ROWS_OWN, F32, 2)
    add("state", ROWS_OWN, F32)
    add("g_rows", ROWS_ALL, BF16)
    add("g_attn", ROWS_ALL, BF16)
    add("grad_att", ATT_ALL, BF16)
    add("grad_mid", ROWS_OWN, F32)
    add("grad", ROWS_OWN, F32)
    add("wide", (16, D), F32)
    add("narrow", (16, 128), F32)
    add("va", (MEMBERS, 16, 128), F32)
    add("vl", (MEMBERS, 16, 128), F32)
    add("vb", (16, 32, 128), F32)
    add("piece", (32, 128), F32)
    for i, spec in enumerate(SUM_SEND):
        table[f"sum_send{i}"] = spec
    for j in range(2):
        for i, spec in enumerate(SUM_LAND):
            table[f"sum_land{j}_{i}"] = spec
    for name, count in (("rows", 10), ("cot", 10), ("swap", 5), ("v1", 8), ("v2", 16), ("v3", 8)):
        table[name + "_send"], table[name + "_recv"] = DMA((count,)), DMA((count,))
    for name in ("w", "g"):
        table[name + "_send"], table[name + "_recv"] = DMA((6, 16)), DMA((6, 16))
    return table


def whole_kernel(*refs):
    table = scratch_table()
    names = [*INPUTS, *OUTPUTS, *table]
    b = types.SimpleNamespace(**dict(zip(names, refs, strict=True)))
    me = Place()
    greet(me, True)

    def both(name):
        return getattr(b, name + "_send"), getattr(b, name + "_recv")

    def pair(name):
        return [getattr(b, name + "0"), getattr(b, name + "1")]

    cuts = {"qo": pl.ds(0, 512), "up": pl.ds(512, 512), "down": pl.ds(1024, 512)}
    weights, grads = {}, {}
    for n, name in enumerate(cuts):
        for l in range(2):
            k = n * 2 + l
            shard = b.shards.at[l, :, cuts[name]]
            weights[name, l] = Weights(me, shard, pair(name)[l], b.w_send.at[k], b.w_recv.at[k])
            part = getattr(b, "dw_" + name)
            out = getattr(b, "sum_" + name).at[l]
            grads[name, l] = Grads(me, part, pair("land_" + name)[l], b.g_send.at[k], b.g_recv.at[k], out)
    send_bufs = [getattr(b, f"sum_send{i}") for i in range(len(SUM_SEND))]
    land = [[getattr(b, f"sum_land{j}_{i}") for i in range(len(SUM_LAND))] for j in range(2)]
    normed_one, normed_two, qkv, attended = (pair(n) for n in ("normed_one", "normed_two", "qkv", "attended"))
    slope, act, middle = (pair(n) for n in ("slope", "act", "middle"))
    weights["qo", 0].start()

    def padded(rows, out):
        b.padded[0:ROWS] = rows[...].astype(F32)
        b.padded[ROWS:PAD] = jnp.zeros((PAD - ROWS, D), F32)
        out[...] = b.padded[...].astype(BF16)

    padded(b.x_in, b.x_own)
    swap_x = Swap(me, b.x_own, b.x_rows, both("swap"), 0)
    swap_x.start()
    swap_mask = Swap(me, b.mask_in, b.mask, both("swap"), 1)
    swap_mask.start()
    padded(b.cot_in, b.cot_own)
    swap_cot = Swap(me, b.cot_own, b.cot_rows, both("swap"), 2)
    swap_cot.start()
    b.wide[...] = jnp.zeros_like(b.wide)
    b.narrow[...] = jnp.zeros_like(b.narrow)
    swap_x.end()

    def norm_rows(rows, l, i, out):
        out[me.slot] = layer_norm(rows, b.gain[l, i : i + 1], b.shift[l, i : i + 1]).astype(BF16)

    def project(l):
        w = weights["qo", l].full

        def consume(slot):
            qkv[l][slot] = (dot(normed_one[l][slot], columns(w, 0, 384)) + b.qbias[l : l + 1]).astype(BF16)

        return consume

    def forward(l, state, before_up, before_down, after_up):
        attend(qkv[l], b.mask, attended[l])
        before_up()
        w = weights["qo", l].full

        def out_product(slot):
            return dot(attended[l][slot], columns(w, 384, 128), NT)

        branch = sum_rows(me, out_product, send_bufs, land[0])
        middle[l][...] = state() + (branch + b.bias[l, 2:3])
        norm_rows(middle[l][...], l, 1, normed_two[l])
        gather = Gather(me, normed_two[l], *both("rows"))
        gather.start()
        before_down()
        weights["up", l].arrived()

        def consume(slot):
            h = dot(normed_two[l][slot], columns(weights["up", l].full, 0, 512)) + b.ubias[l : l + 1]
            value, slant = gelu_and_slope(h)
            act[l][slot] = value.astype(BF16)
            slope[l][slot] = slant.astype(BF16)

        gather.run(consume)
        weights["down", l].arrived()
        after_up()

        def down_product(slot):
            return dot(act[l][slot], columns(weights["down", l].full, 0, 512), NT)

        total = sum_rows(me, down_product, send_bufs, land[1])
        gather.end()
        return middle[l][...] + (total + b.bias[l, 3:4])

    norm_rows(b.x_rows[...].astype(F32), 0, 0, normed_one[0])
    gather = Gather(me, normed_one[0], *both("rows"))
    gather.start()
    swap_mask.end()
    swap_cot.end()
    b.g_rows[me.slot] = b.cot_rows[...]
    gather_cot = Gather(me, b.g_rows, *both("cot"))
    gather.relay()
    weights["qo", 0].arrived()
    weights["up", 0].start()
    gather.run(project(0), relayed=True)
    gather.end()
    gather_cot.start()
    b.state[...] = forward(
        0,
        lambda: b.x_rows[...].astype(F32),
        weights["down", 0].start,
        nothing,
        weights["qo", 1].start,
    )
    norm_rows(b.state[...], 1, 0, normed_one[1])
    gather = Gather(me, normed_one[1], *both("rows"))
    gather.start()
    weights["qo", 1].arrived()
    weights["up", 1].start()
    gather.run(project(1))
    gather.end()
    gather_cot.relay()
    b.rows_away[...] = forward(1, lambda: b.state[...], weights["down", 1].start, nothing, nothing).astype(BF16)
    swap_out = Swap(me, b.rows_away, b.out_rows, both("swap"), 3)
    swap_out.start()

    def narrow_sum(ref, row, at, count):
        total = column_sum(ref)
        for i in range(count):
            b.narrow[row + i : row + i + 1] = total[:, (at + i) * 128 : (at + i + 1) * 128]

    def backward(l, g_own, gather_g, after_down, after_up):
        down, up, w = weights["down", l].full, weights["up", l].full, weights["qo", l].full

        def consume(slot):
            grad_act = dot(b.g_rows[slot], columns(down, 0, 512))
            slope[l][slot] = (grad_act * slope[l][slot].astype(F32)).astype(BF16)

        gather_g.run(consume, relayed=l == 1)
        grad_hid = slope[l]

        def up_back(slot):
            return dot(grad_hid[slot], columns(up, 0, 512), NT)

        def fill():
            weight_grad(b.g_rows, act[l], b.dw_down, 0, 512)
            grads["down", l].start()
            narrow_sum(grad_hid, l * 6 + 2, 0, 4)
            after_down()

        grad = sum_rows(me, up_back, send_bufs, land[0], fill)
        gather_g.end()
        back, gain_sum, shift_sum = layer_norm_back(middle[l][...], b.gain[l, 1:2], grad)
        mid = g_own() + back
        b.grad_mid[...] = mid
        b.g_attn[me.slot] = mid.astype(BF16)
        gather = Gather(me, b.g_attn, *both("rows"))
        gather.start()
        row = l * 6 + 2
        b.wide[row : row + 1] = jnp.sum(g_own(), axis=0, keepdims=True)
        b.wide[row + 1 : row + 2] = gain_sum
        b.wide[row + 2 : row + 3] = shift_sum
        b.wide[row + 3 : row + 4] = jnp.sum(mid, axis=0, keepdims=True)

        def fill_two():
            after_up()
            weight_grad(normed_two[l], grad_hid, b.dw_up, 0, 512)
            grads["up", l].start()

        def att_back(slot):
            b.grad_att[slot] = dot(b.g_attn[slot], columns(w, 384, 128)).astype(BF16)

        gather.run(att_back, fill_two)
        gather.end()
        attend_back(qkv[l], b.mask, b.grad_att)

    def first_back(l, rows, more):
        w, grad_qkv = weights["qo", l].full, qkv[l]

        def back_product(slot):
            return dot(grad_qkv[slot], columns(w, 0, 384), NT)

        def fill():
            weight_grad(normed_one[l], grad_qkv, b.dw_qo, 0, 384)
            weight_grad(b.g_attn, attended[l], b.dw_qo, 384, 128)
            grads["qo", l].start()
            more()
            total = column_sum(grad_qkv)
            b.narrow[l * 6 : l * 6 + 1] = total[:, 0:128]
            b.narrow[l * 6 + 1 : l * 6 + 2] = total[:, 256:384]

        grad = sum_rows(me, back_product, send_bufs, land[1], fill)
        back, gain_sum, shift_sum = layer_norm_back(rows(), b.gain[l, 0:1], grad)
        b.wide[l * 6 : l * 6 + 1] = gain_sum
        b.wide[l * 6 + 1 : l * 6 + 2] = shift_sum
        return b.grad_mid[...] + back

    backward(1, lambda: b.cot_rows[...].astype(F32), gather_cot, nothing, nothing)
    b.grad[...] = first_back(1, lambda: b.state[...], grads["down", 1].end)
    b.g_rows[me.slot] = b.grad[...].astype(BF16)
    gather_g = Gather(me, b.g_rows, *both("cot"))
    gather_g.start()
    swap_out.end()
    backward(0, lambda: b.grad[...], gather_g, grads["up", 1].end, grads["qo", 1].end)
    b.gradient[...] = first_back(0, lambda: b.x_rows[...].astype(F32), grads["down", 0].end)
    b.rows_away[...] = b.gradient[...].astype(BF16)
    vectors_start(me, b.wide, b.va, b.vl, *both("v1"))
    swap_grad = Swap(me, b.rows_away, b.rows_home, both("swap"), 4)
    swap_grad.start()
    for name in cuts:
        for l in range(2):
            weights[name, l].sent()
    vectors_end(me, b.narrow, b.va, b.vl, *both("v1"), b.vb, b.piece, *both("v2"), b.vectors, *both("v3"))
    swap_grad.end()

    @pl.when(me.core != me.zlo)
    def _():
        b.gradient[...] = b.rows_home[...].astype(F32)

    grads["up", 0].end()
    grads["qo", 0].end()


def nothing():
    pass


def per_device(
    x_in, valid_len, w_qkv, w_out, w_up, w_down, norm_gain, norm_shift, bias, up_bias, cotangent
):
    dp, tensor = lax.axis_index("dp"), lax.axis_index("tensor")
    slot = (dp % 2) * 4 + tensor % 4
    at = jnp.arange(4 * PAD)
    token = (at // PAD) * ROWS + at % PAD
    mask = (at % PAD < ROWS) & (token < valid_len[:, None])
    mask = jnp.broadcast_to(mask[:, None].astype(F32), (2, 8, 4 * PAD))
    shards = jnp.concatenate(
        [w_qkv.reshape(2, 64, 384), jnp.swapaxes(w_out, 1, 2), w_up, jnp.swapaxes(w_down, 1, 2)], axis=2
    )
    own_bias = lax.dynamic_slice_in_dim(bias, slot * COLS, COLS, axis=2)
    qbias = jnp.concatenate([own_bias[:, 0], jnp.zeros((2, COLS), F32), own_bias[:, 1]], axis=1)
    ubias = lax.dynamic_slice_in_dim(up_bias, slot * HID, HID, axis=1)
    vmem = pl.BlockSpec(memory_space=pltpu.VMEM)
    out_rows, gradient, sum_qo, sum_up, sum_down, vectors = pl.pallas_call(
        whole_kernel,
        out_shape=[jax.ShapeDtypeStruct(s, t) for s, t in OUTPUTS.values()],
        in_specs=[vmem] * len(INPUTS),
        out_specs=[vmem] * len(OUTPUTS),
        scratch_shapes=list(scratch_table().values()),
        compiler_params=pltpu.CompilerParams(
            collective_id=0, has_side_effects=True, vmem_limit_bytes=VMEM_BYTES
        ),
    )(x_in, cotangent, mask, shards, norm_gain, norm_shift, bias, qbias, ubias)
    full = jnp.transpose(vectors[:, 0:12], (1, 0, 2)).reshape(2, 6, D)
    own = vectors[:, 16:28].reshape(MEMBERS, 2, 6, COLS)
    q_bias = jnp.transpose(own[:, :, 0], (1, 0, 2)).reshape(2, D)
    v_bias = jnp.transpose(own[:, :, 1], (1, 0, 2)).reshape(2, D)
    return (
        out_rows[:ROWS],
        gradient[:ROWS],
        sum_qo[:, :, 0:384].reshape(2, 64, 3, COLS),
        jnp.swapaxes(sum_qo[:, :, 384:], 1, 2),
        sum_up,
        jnp.swapaxes(sum_down, 1, 2),
        jnp.stack([full[:, 0], full[:, 3]], axis=1),
        jnp.stack([full[:, 1], full[:, 4]], axis=1),
        jnp.stack([q_bias, v_bias, full[:, 5], full[:, 2]], axis=1),
        jnp.transpose(own[:, :, 2:], (1, 0, 2, 3)).reshape(2, 4096),
    )


def solution(mesh):
    rows = P(("dp", "tensor"), None)
    weights = (P(None, "dp", None, "tensor"), P(None, "tensor", "dp"), P(None, "dp", "tensor"), P(None, "tensor", "dp"))
    return jax.shard_map(
        per_device,
        mesh=mesh,
        in_specs=(rows, P("dp"), *weights, P(), P(), P(), P(), rows),
        out_specs=(rows, rows, *weights, P(), P(), P(), P()),
        check_vma=False,
    )
```

time: 417 us -> 332 us (0.80)
  Pallas kernels: 370 us -> 318 us
  starting transfers between devices: 16.2 us -> 0 us
  local copies, waits for them, and re-layouts: 19.7 us -> 9.41 us
    pallas_call x9 -> x1, Pallas kernels: 370 us -> 318 us  [per_device(): pl.pallas_call(whole_kernel, out_shape=[jax.ShapeDtypeStruct(s, t) for s,...]
    ppermute x5 -> x0, starting transfers between devices: 16.2 us -> none  [swap(): return lax.ppermute(value, ('dp', 'tensor'), pairs)]
  transfers between devices with their start and end apart: 5 -> 0, of which waited for: 1 -> 0; matrix products, arithmetic and copies ran while one was open for 4% -> 0% of each run, Pallas kernels for 29% -> 0%
where the time goes in v3:
time: 332 us; the launch traced here: 331 us
  Pallas kernels  318 us (96%)
  local copies, waits for them, and re-layouts  9.41 us (3%)
  other arithmetic  3.52 us (1%)
    pallas_call x1, Pallas kernels, per_device(): pl.pallas_call(whole_kernel, out_shape=[jax.ShapeDtypeStruct(s, t) for s,...  318 us

profile of v3, /device:TPU:1, one launch (start us, length us, event | category | flops | bytes accessed | tf_op | source)
XLA Modules:
  0.0 331.5 jit_solution(6006175603102371104)
XLA Ops:
  0.6 0.0 copy-start.7
  0.7 0.8 constant_dynamic-slice_fusion
  1.6 0.0 copy-start.8
  1.6 0.6 pad_maximum_fusion.4.refs_7_
  2.2 1.3 constant_dynamic-slice_fusion.1.refs_8_
  3.5 0.0 copy-done.8
  3.5 0.1 and_convert_fusion
  3.6 0.6 broadcast_in_dim.4.refs_2_
  4.2 0.0 copy-done.7
  4.2 0.0 copy-done.5
  4.2 1.5 pad_maximum_fusion.refs_3_
  5.8 317.7 %shard_map.186 = (bf16[160,1024]{1,0:T(8,128)(2,1)}, f32[160,1024]{1,0:T(8,128)}, f32[2,64,512]{2,1,0:T(8,128)}, f32[2,64,512]{2,1,0:T(8,128)}, f32[2,64,512]{2,1,0:T(8,128)}, /*index=5*/f32[8,32,128]{2,1,0:T(8,128)}) custom-call(bf16[146,1024]{1,0:T(8,128)(2,1)} %refs_0_.1, bf16[146,1024]{1,0:T(8,128)(2,1)} %refs_1_.1, ...), custom_call_target="tpu_custom_call" | custom-call | tf_op jit(solution)/shard_map/pallas_call | solution.py:931
  323.5 1.7 slice.53
  325.3 0.0 copy-done.1
  325.3 0.6 slice_bitcast_fusion.2
  325.9 0.7 copy_bitcast_fusion
  326.7 0.6 reshape.99
  327.4 0.7 pad_maximum_fusion.1
  328.1 0.6 pad_maximum_fusion.2
  328.7 0.9 slice.54
  329.6 0.1 copy-done.3
  329.7 0.7 copy.47
  330.4 0.3 copy-done.2
  330.7 0.7 copy.48
  (23 shorter events, 0.2 us)
Async XLA Ops:
  0.6 3.6 %copy-start.7 = (bf16[2,64,3,128]{3,1,2,0:T(8,128)(2,1)S(1)}, bf16[2,64,3,128]{3,1,2,0:T(8,128)(2,1)}, u32[]{:S(2)}) copy-start(bf16[2,64,3,128]{3,1,2,0:T(8,128)(2,1)} %param.13) | copy-start | bytes 294916
  1.6 1.9 copy-start.8
  2.1 2.1 copy-start.5
  2.2 2.1 copy-start.6
  323.5 1.8 copy-start.1
  325.3 1.3 copy-start.4
  325.9 2.8 copy-start
  328.7 1.0 copy-start.3
  329.7 1.0 copy-start.2

commit v4 on v3

--- a/solution.py
+++ b/solution.py
@@ -49,7 +49,7 @@
         return self.peer(1 - self.core, self.x)
 
 
-def greet(me, plane):
+def greet(me, work):
     barrier = pltpu.get_barrier_semaphore()
 
     def member(i, carry):
@@ -62,23 +62,21 @@
         return carry
 
     lax.fori_loop(1, MEMBERS, member, 0)
-    count = MEMBERS - 1
-    if plane:
-
-        def other(i, carry):
-            pair = (me.pair + i // 4) % 8
-            zlo = (me.zlo + (i // 2) % 2) % 2
-            pl.semaphore_signal(
-                barrier,
-                inc=1,
-                device_id={"dp": pair * 2 + i % 2, "tensor": zlo * 4 + me.x},
-                device_id_type=MESH,
-            )
-            return carry
-
-        lax.fori_loop(2, 32, other, 0)
-        count += 30
-    pl.semaphore_wait(barrier, count)
+
+    def other(i, carry):
+        pair = (me.pair + i // 4) % 8
+        zlo = (me.zlo + (i // 2) % 2) % 2
+        pl.semaphore_signal(
+            barrier,
+            inc=1,
+            device_id={"dp": pair * 2 + i % 2, "tensor": zlo * 4 + me.x},
+            device_id_type=MESH,
+        )
+        return carry
+
+    lax.fori_loop(2, 32, other, 0)
+    work()
+    pl.semaphore_wait(barrier, MEMBERS - 1 + 30)
 
 
 def remote(src, dst, send, recv, device):
@@ -139,7 +137,12 @@
             self.copy(*self.table()[k]).start()
 
     def start(self):
-        self.start_copies(6, 0, 3, 1, 2)
+        self.start_copies(6, 0, 3)
+
+    def second(self):
+        for k in (0, 3):
+            self.copy(*self.table()[k]).wait_send()
+        self.start_copies(1, 2)
 
     def arrived(self, *which):
         for k in which:
@@ -156,6 +159,8 @@
         def step(i, carry):
             @pl.when(i == 1)
             def _():
+                if not relayed:
+                    self.second()
                 self.arrived(6)
 
             @pl.when(i == 2)
@@ -196,7 +201,8 @@
 
     def end(self):
         for row in self.table():
-            self.copy(*row).wait_send()
+            if row[0] not in (0, 3):
+                self.copy(*row).wait_send()
 
 
 GATHER_SEMS = [pltpu.SemaphoreType.DMA((10,)), pltpu.SemaphoreType.DMA((10,))]
@@ -277,14 +283,14 @@
 
     lax.fori_loop(0, 2, for_sibling, 0)
     lax.fori_loop(0, 4, own, 0)
+    if fill is not None:
+        fill()
     along(0).wait_recv()
     s2[1, TOP] = (hold[0] + ra[TOP].astype(F32)).astype(BF16)
     along(4).start()
     along(1).wait_recv()
     s2[2, BOTTOM] = (hold[1] + ra[BOTTOM].astype(F32)).astype(BF16)
     along(5).start()
-    if fill is not None:
-        fill()
     for k in range(2, 6):
         along(k).wait_recv()
     total = acc[...] + rb[0].astype(F32) + rb[1].astype(F32)
@@ -366,7 +372,7 @@
     lax.fori_loop(1, 16, step, 0)
 
 
-def grads_end(me, part, land, send, recv, out):
+def grads_end(me, part, land, send, recv, store):
     def arrived(i, carry):
         remote(part.at[0], land.at[i], send.at[i], recv.at[i], me.sibling()).wait_recv()
         return carry
@@ -385,7 +391,7 @@
     total = land[0].astype(F32)
     for i in range(1, 16):
         total = total + land[i].astype(F32)
-    out[...] = total
+    store(total)
 
 
 def normalized(rows):
@@ -471,11 +477,12 @@
 
     def image(i, carry):
         q, k, v = (head_parts(qkv, i, j) for j in range(3))
+        q = q * BF16(HEAD**-0.5)
         valid = mask[i, 0:1] > 0.5
         total = None
         for h in range(2):
             mine = (lane >= h * HEAD) & (lane < (h + 1) * HEAD)
-            scores = dot(jnp.where(mine, q, jnp.zeros_like(q)), k, NT) * F32(HEAD**-0.5)
+            scores = dot(jnp.where(mine, q, jnp.zeros_like(q)), k, NT)
             scores = jnp.where(valid, scores, NEG_FILL)
             e = jnp.exp(scores - jnp.max(scores, axis=-1, keepdims=True))
             prob = (e * (1.0 / jnp.sum(e, axis=-1, keepdims=True))).astype(BF16)
@@ -492,12 +499,13 @@
 
     def image(i, carry):
         q, k, v = (head_parts(qkv, i, j) for j in range(3))
+        q = q * BF16(HEAD**-0.5)
         g = grad[pl.ds(i * 4, 4)].reshape(4 * PAD, COLS)
         valid = mask[i].T[:, 0:1] > 0.5
         parts = [None, None, None]
         for h in range(2):
             mine = (lane >= h * HEAD) & (lane < (h + 1) * HEAD)
-            scores = dot(k, jnp.where(mine, q, jnp.zeros_like(q)), NT) * F32(HEAD**-0.5)
+            scores = dot(k, jnp.where(mine, q, jnp.zeros_like(q)), NT)
             scores = jnp.where(valid, scores, NEG_FILL)
             e = jnp.exp(scores - jnp.max(scores, axis=0, keepdims=True))
             prob = e * (1.0 / jnp.sum(e, axis=0, keepdims=True))
@@ -505,7 +513,7 @@
             grad_prob = dot(v, jnp.where(mine, g, jnp.zeros_like(g)), NT)
             inner = jnp.sum(grad_prob * prob, axis=0, keepdims=True)
             grad_scores = (prob * (grad_prob - inner)).astype(BF16)
-            grad_key = dot(grad_scores, q) * F32(HEAD**-0.5)
+            grad_key = dot(grad_scores, q)
             grad_query = dot(grad_scores, k, TN) * F32(HEAD**-0.5)
             new = [grad_query, grad_key, grad_value]
             parts = new if h == 0 else [jnp.where(mine, n, p) for n, p in zip(new, parts)]
@@ -631,14 +639,18 @@
 HID_ALL, ATT_ALL, QKV_ALL, SUMMED = (MEMBERS, PAD, HID), (MEMBERS, PAD, COLS), (MEMBERS, PAD, 384), (64, 512)
 DMA = pltpu.SemaphoreType.DMA
 
-INPUTS = ("x_in", "cot_in", "mask_in", "shards", "gain", "shift", "bias", "qbias", "ubias")
+INPUTS = ("x_in", "cot_in", "mask_in", "shards", "gain", "shift", "bias", "up_bias")
 OUTPUTS = {
-    "out_rows": (ROWS_OWN, BF16),
-    "gradient": (ROWS_OWN, F32),
-    "sum_qo": ((2, *SUMMED), F32),
-    "sum_up": ((2, *SUMMED), F32),
-    "sum_down": ((2, *SUMMED), F32),
-    "vectors": ((MEMBERS, 32, 128), F32),
+    "out_rows": ((ROWS, D), BF16),
+    "gradient": ((ROWS, D), F32),
+    "grad_qkv": ((2, 64, 3, COLS), F32),
+    "grad_out": ((2, COLS, 64), F32),
+    "grad_up": ((2, 64, HID), F32),
+    "grad_down": ((2, HID, 64), F32),
+    "grad_gain": ((2, 2, D), F32),
+    "grad_shift": ((2, 2, D), F32),
+    "grad_bias": ((2, 4, D), F32),
+    "grad_up_bias": ((2, 4096), F32),
 }
 
 
@@ -675,6 +687,8 @@
     add("narrow", (16, 128), F32)
     add("va", (MEMBERS, 16, 128), F32)
     add("vl", (MEMBERS, 16, 128), F32)
+    add("vectors", (MEMBERS, 32, 128), F32)
+    add("qbias", (2, 384), F32)
     add("vb", (16, 32, 128), F32)
     add("piece", (32, 128), F32)
     for i, spec in enumerate(SUM_SEND):
@@ -694,7 +708,26 @@
     names = [*INPUTS, *OUTPUTS, *table]
     b = types.SimpleNamespace(**dict(zip(names, refs, strict=True)))
     me = Place()
-    greet(me, True)
+
+    def padded(rows, out):
+        b.padded[0:ROWS] = rows[...].astype(F32)
+        b.padded[ROWS:PAD] = jnp.zeros((PAD - ROWS, D), F32)
+        out[...] = b.padded[...].astype(BF16)
+
+    own_cols = pl.ds(pl.multiple_of(me.slot * COLS, COLS), COLS)
+    own_hid = pl.ds(pl.multiple_of(me.slot * HID, HID), HID)
+
+    def work():
+        padded(b.x_in, b.x_own)
+        padded(b.cot_in, b.cot_own)
+        b.wide[...] = jnp.zeros_like(b.wide)
+        b.narrow[...] = jnp.zeros_like(b.narrow)
+        b.qbias[...] = jnp.zeros_like(b.qbias)
+        for l in range(2):
+            b.qbias[l : l + 1, 0:COLS] = b.bias[l, 0:1, own_cols]
+            b.qbias[l : l + 1, 2 * COLS :] = b.bias[l, 1:2, own_cols]
+
+    greet(me, work)
 
     def both(name):
         return getattr(b, name + "_send"), getattr(b, name + "_recv")
@@ -704,36 +737,48 @@
 
     cuts = {"qo": pl.ds(0, 512), "up": pl.ds(512, 512), "down": pl.ds(1024, 512)}
     weights, grads = {}, {}
+
+    def store_qo(l):
+        def store(total):
+            for j in range(3):
+                b.grad_qkv[l, :, j, :] = total[:, j * COLS : (j + 1) * COLS]
+            b.grad_out[l] = total[:, 3 * COLS :].T
+
+        return store
+
+    def store_up(l):
+        def store(total):
+            b.grad_up[l] = total
+
+        return store
+
+    def store_down(l):
+        def store(total):
+            b.grad_down[l] = total.T
+
+        return store
+
+    stores = {"qo": store_qo, "up": store_up, "down": store_down}
     for n, name in enumerate(cuts):
         for l in range(2):
             k = n * 2 + l
             shard = b.shards.at[l, :, cuts[name]]
             weights[name, l] = Weights(me, shard, pair(name)[l], b.w_send.at[k], b.w_recv.at[k])
             part = getattr(b, "dw_" + name)
-            out = getattr(b, "sum_" + name).at[l]
-            grads[name, l] = Grads(me, part, pair("land_" + name)[l], b.g_send.at[k], b.g_recv.at[k], out)
+            land_part = pair("land_" + name)[l]
+            grads[name, l] = Grads(me, part, land_part, b.g_send.at[k], b.g_recv.at[k], stores[name](l))
     send_bufs = [getattr(b, f"sum_send{i}") for i in range(len(SUM_SEND))]
     land = [[getattr(b, f"sum_land{j}_{i}") for i in range(len(SUM_LAND))] for j in range(2)]
     normed_one, normed_two, qkv, attended = (pair(n) for n in ("normed_one", "normed_two", "qkv", "attended"))
     slope, act, middle = (pair(n) for n in ("slope", "act", "middle"))
-    weights["qo", 0].start()
-
-    def padded(rows, out):
-        b.padded[0:ROWS] = rows[...].astype(F32)
-        b.padded[ROWS:PAD] = jnp.zeros((PAD - ROWS, D), F32)
-        out[...] = b.padded[...].astype(BF16)
-
-    padded(b.x_in, b.x_own)
+
     swap_x = Swap(me, b.x_own, b.x_rows, both("swap"), 0)
     swap_x.start()
     swap_mask = Swap(me, b.mask_in, b.mask, both("swap"), 1)
     swap_mask.start()
-    padded(b.cot_in, b.cot_own)
     swap_cot = Swap(me, b.cot_own, b.cot_rows, both("swap"), 2)
-    swap_cot.start()
-    b.wide[...] = jnp.zeros_like(b.wide)
-    b.narrow[...] = jnp.zeros_like(b.narrow)
     swap_x.end()
+    weights["qo", 0].start()
 
     def norm_rows(rows, l, i, out):
         out[me.slot] = layer_norm(rows, b.gain[l, i : i + 1], b.shift[l, i : i + 1]).astype(BF16)
@@ -763,7 +808,7 @@
         weights["up", l].arrived()
 
         def consume(slot):
-            h = dot(normed_two[l][slot], columns(weights["up", l].full, 0, 512)) + b.ubias[l : l + 1]
+            h = dot(normed_two[l][slot], columns(weights["up", l].full, 0, 512)) + b.up_bias[l : l + 1, own_hid]
             value, slant = gelu_and_slope(h)
             act[l][slot] = value.astype(BF16)
             slope[l][slot] = slant.astype(BF16)
@@ -783,19 +828,26 @@
     gather = Gather(me, normed_one[0], *both("rows"))
     gather.start()
     swap_mask.end()
+    gather.second()
+    gather.relay()
+    weights["qo", 0].arrived()
+    swap_cot.start()
+    weights["up", 0].start()
+    gather.run(project(0), relayed=True)
+    gather.end()
     swap_cot.end()
     b.g_rows[me.slot] = b.cot_rows[...]
     gather_cot = Gather(me, b.g_rows, *both("cot"))
-    gather.relay()
-    weights["qo", 0].arrived()
-    weights["up", 0].start()
-    gather.run(project(0), relayed=True)
-    gather.end()
     gather_cot.start()
+
+    def cot_second():
+        gather_cot.second()
+        weights["down", 0].start()
+
     b.state[...] = forward(
         0,
         lambda: b.x_rows[...].astype(F32),
-        weights["down", 0].start,
+        cot_second,
         nothing,
         weights["qo", 1].start,
     )
@@ -808,7 +860,7 @@
     gather.end()
     gather_cot.relay()
     b.rows_away[...] = forward(1, lambda: b.state[...], weights["down", 1].start, nothing, nothing).astype(BF16)
-    swap_out = Swap(me, b.rows_away, b.out_rows, both("swap"), 3)
+    swap_out = Swap(me, b.rows_away, b.rows_home, both("swap"), 3)
     swap_out.start()
 
     def narrow_sum(ref, row, at, count):
@@ -888,23 +940,45 @@
     gather_g = Gather(me, b.g_rows, *both("cot"))
     gather_g.start()
     swap_out.end()
+    b.out_rows[...] = b.rows_home[...].astype(F32)[:ROWS].astype(BF16)
     backward(0, lambda: b.grad[...], gather_g, grads["up", 1].end, grads["qo", 1].end)
-    b.gradient[...] = first_back(0, lambda: b.x_rows[...].astype(F32), grads["down", 0].end)
-    b.rows_away[...] = b.gradient[...].astype(BF16)
+    b.grad[...] = first_back(0, lambda: b.x_rows[...].astype(F32), grads["down", 0].end)
+    b.rows_away[...] = b.grad[...].astype(BF16)
     vectors_start(me, b.wide, b.va, b.vl, *both("v1"))
-    swap_grad = Swap(me, b.rows_away, b.rows_home, both("swap"), 4)
+    swap_grad = Swap(me, b.rows_away, b.x_own, both("swap"), 4)
     swap_grad.start()
     for name in cuts:
         for l in range(2):
             weights[name, l].sent()
+    grads["up", 0].end()
     vectors_end(me, b.narrow, b.va, b.vl, *both("v1"), b.vb, b.piece, *both("v2"), b.vectors, *both("v3"))
+    for s in range(MEMBERS):
+        cols = slice(s * COLS, (s + 1) * COLS)
+        for l in range(2):
+            for ref, at, row in (
+                (b.grad_gain, 0, 0),
+                (b.grad_shift, 0, 1),
+                (b.grad_bias, 3, 2),
+                (b.grad_gain, 1, 3),
+                (b.grad_shift, 1, 4),
+                (b.grad_bias, 2, 5),
+                (b.grad_bias, 0, 16),
+                (b.grad_bias, 1, 17),
+            ):
+                ref[l, at : at + 1, cols] = b.vectors[s, row + 6 * l : row + 6 * l + 1]
+            for j in range(4):
+                to = s * HID + j * COLS
+                b.grad_up_bias[l : l + 1, to : to + COLS] = b.vectors[s, 18 + 6 * l + j : 19 + 6 * l + j]
     swap_grad.end()
+
+    @pl.when(me.core == me.zlo)
+    def _():
+        b.gradient[...] = b.grad[...][:ROWS]
 
     @pl.when(me.core != me.zlo)
     def _():
-        b.gradient[...] = b.rows_home[...].astype(F32)
-
-    grads["up", 0].end()
+        b.gradient[...] = b.x_own[...].astype(F32)[:ROWS]
+
     grads["qo", 0].end()
 
 
@@ -915,8 +989,6 @@
 def per_device(
     x_in, valid_len, w_qkv, w_out, w_up, w_down, norm_gain, norm_shift, bias, up_bias, cotangent
 ):
-    dp, tensor = lax.axis_index("dp"), lax.axis_index("tensor")
-    slot = (dp % 2) * 4 + tensor % 4
     at = jnp.arange(4 * PAD)
     token = (at // PAD) * ROWS + at % PAD
     mask = (at % PAD < ROWS) & (token < valid_len[:, None])
@@ -924,11 +996,8 @@
     shards = jnp.concatenate(
         [w_qkv.reshape(2, 64, 384), jnp.swapaxes(w_out, 1, 2), w_up, jnp.swapaxes(w_down, 1, 2)], axis=2
     )
-    own_bias = lax.dynamic_slice_in_dim(bias, slot * COLS, COLS, axis=2)
-    qbias = jnp.concatenate([own_bias[:, 0], jnp.zeros((2, COLS), F32), own_bias[:, 1]], axis=1)
-    ubias = lax.dynamic_slice_in_dim(up_bias, slot * HID, HID, axis=1)
     vmem = pl.BlockSpec(memory_space=pltpu.VMEM)
-    out_rows, gradient, sum_qo, sum_up, sum_down, vectors = pl.pallas_call(
+    return pl.pallas_call(
         whole_kernel,
         out_shape=[jax.ShapeDtypeStruct(s, t) for s, t in OUTPUTS.values()],
         in_specs=[vmem] * len(INPUTS),
@@ -937,23 +1006,7 @@
         compiler_params=pltpu.CompilerParams(
             collective_id=0, has_side_effects=True, vmem_limit_bytes=VMEM_BYTES
         ),
-    )(x_in, cotangent, mask, shards, norm_gain, norm_shift, bias, qbias, ubias)
-    full = jnp.transpose(vectors[:, 0:12], (1, 0, 2)).reshape(2, 6, D)
-    own = vectors[:, 16:28].reshape(MEMBERS, 2, 6, COLS)
-    q_bias = jnp.transpose(own[:, :, 0], (1, 0, 2)).reshape(2, D)
-    v_bias = jnp.transpose(own[:, :, 1], (1, 0, 2)).reshape(2, D)
-    return (
-        out_rows[:ROWS],
-        gradient[:ROWS],
-        sum_qo[:, :, 0:384].reshape(2, 64, 3, COLS),
-        jnp.swapaxes(sum_qo[:, :, 384:], 1, 2),
-        sum_up,
-        jnp.swapaxes(sum_down, 1, 2),
-        jnp.stack([full[:, 0], full[:, 3]], axis=1),
-        jnp.stack([full[:, 1], full[:, 4]], axis=1),
-        jnp.stack([q_bias, v_bias, full[:, 5], full[:, 2]], axis=1),
-        jnp.transpose(own[:, :, 2:], (1, 0, 2, 3)).reshape(2, 4096),
-    )
+    )(x_in, cotangent, mask, shards, norm_gain, norm_shift, bias, up_bias)
 
 
 def solution(mesh):

time: 332 us -> 341 us (1.027)
  Pallas kernels: 318 us -> 327 us
    pallas_call x1, Pallas kernels: 318 us -> 327 us  [per_device(): pl.pallas_call(whole_kernel, out_shape=[jax.ShapeDtypeStruct(s, t) for s,...]
    pallas_call x0 -> x3, local copies, waits for them, and re-layouts: none -> 4.25 us  [per_device(): pl.pallas_call(whole_kernel, out_shape=[jax.ShapeDtypeStruct(s, t) for s,...]
    slice x7 -> x0, local copies, waits for them, and re-layouts: 3.53 us -> none  [the longest x1 1.75 us: per_device(): out_rows[:ROWS]]
where the time goes in v4:
time: 341 us
  Pallas kernels  327 us (96%)
  local copies, waits for them, and re-layouts  10.9 us (3%)
    pallas_call x1, Pallas kernels, per_device(): pl.pallas_call(whole_kernel, out_shape=[jax.ShapeDtypeStruct(s, t) for s,...  327 us

profile of v4, /device:TPU:1, one launch (start us, length us, event | category | flops | bytes accessed | tf_op | source)
XLA Modules:
  0.0 341.0 jit_solution(17777743576931990866)
XLA Ops:
  0.6 0.0 copy-start.5
  0.7 0.0 copy-start.4
  0.7 0.8 and_convert_fusion
  1.5 0.6 broadcast_in_dim.2.refs_2_
  2.1 0.9 copy_bitcast_fusion
  3.0 0.0 copy-done.5
  3.0 0.0 copy-done.4
  3.0 1.5 pad_maximum_fusion.refs_3_
  4.6 327.0 %shard_map.186 = (bf16[146,1024]{1,0:T(8,128)(2,1)}, f32[146,1024]{1,0:T(8,128)}, f32[2,64,3,128]{3,2,1,0:T(4,128)}, f32[2,128,64]{2,1,0:T(8,128)}, f32[2,64,512...) custom-call(bf16[146,1024]{1,0:T(8,128)(2,1)} %refs_0_.1, ...), custom_call_target="tpu_custom_call" | custom-call | tf_op jit(solution)/shard_map/pallas_call | solution.py:1000
  331.6 0.0 copy-start.1
  331.6 1.7 copy.27
  333.3 1.7 copy.26
  335.0 0.0 copy-done.1
  335.0 0.9 copy.28
  335.9 0.7 copy.38
  336.6 0.8 copy.39
  337.5 0.3 copy-done.3
  337.7 0.7 copy.40
  338.4 0.0 copy-done.9
  338.4 0.6 copy.41
  339.0 0.6 copy.42
  339.7 0.6 copy.43
  340.3 0.2 copy-done.6
  340.4 0.6 copy.44
  (13 shorter events, 0.0 us)
Async XLA Ops:
  0.6 2.4 copy-start.5
  0.7 2.4 copy-start.4
  331.6 3.4 copy-start.1
  333.3 2.6 copy-start.2
  335.0 1.6 copy-start
  336.6 1.1 copy-start.3
  337.7 0.7 copy-start.9
  337.7 1.3 copy-start.8
  338.4 1.2 copy-start.7
  339.7 0.8 copy-start.6

commit v5 on v4

--- a/solution.py
+++ b/solution.py
@@ -137,12 +137,7 @@
             self.copy(*self.table()[k]).start()
 
     def start(self):
-        self.start_copies(6, 0, 3)
-
-    def second(self):
-        for k in (0, 3):
-            self.copy(*self.table()[k]).wait_send()
-        self.start_copies(1, 2)
+        self.start_copies(6, 0, 3, 1, 2)
 
     def arrived(self, *which):
         for k in which:
@@ -159,8 +154,6 @@
         def step(i, carry):
             @pl.when(i == 1)
             def _():
-                if not relayed:
-                    self.second()
                 self.arrived(6)
 
             @pl.when(i == 2)
@@ -201,8 +194,7 @@
 
     def end(self):
         for row in self.table():
-            if row[0] not in (0, 3):
-                self.copy(*row).wait_send()
+            self.copy(*row).wait_send()
 
 
 GATHER_SEMS = [pltpu.SemaphoreType.DMA((10,)), pltpu.SemaphoreType.DMA((10,))]
@@ -641,17 +633,53 @@
 
 INPUTS = ("x_in", "cot_in", "mask_in", "shards", "gain", "shift", "bias", "up_bias")
 OUTPUTS = {
+    "out_rows": (ROWS_OWN, BF16),
+    "gradient": (ROWS_OWN, F32),
+    "sum_qo": ((2, *SUMMED), F32),
+    "sum_up": ((2, *SUMMED), F32),
+    "sum_down": ((2, *SUMMED), F32),
+    "vectors": ((MEMBERS, 32, 128), F32),
+}
+RESULTS = {
     "out_rows": ((ROWS, D), BF16),
     "gradient": ((ROWS, D), F32),
-    "grad_qkv": ((2, 64, 3, COLS), F32),
-    "grad_out": ((2, COLS, 64), F32),
+    "grad_qkv": ((2, 3, 64, COLS), F32),
+    "grad_out": ((2, 64, COLS), F32),
     "grad_up": ((2, 64, HID), F32),
-    "grad_down": ((2, HID, 64), F32),
+    "grad_down": ((2, 64, HID), F32),
     "grad_gain": ((2, 2, D), F32),
     "grad_shift": ((2, 2, D), F32),
     "grad_bias": ((2, 4, D), F32),
     "grad_up_bias": ((2, 4096), F32),
 }
+
+
+def result_kernel(*refs):
+    b = types.SimpleNamespace(**dict(zip([*["in_" + n for n in OUTPUTS], *RESULTS], refs, strict=True)))
+    b.out_rows[...] = b.in_out_rows[...].astype(F32)[:ROWS].astype(BF16)
+    b.gradient[...] = b.in_gradient[...][:ROWS]
+    for j in range(3):
+        b.grad_qkv[:, j] = b.in_sum_qo[:, :, j * COLS : (j + 1) * COLS]
+    b.grad_out[...] = b.in_sum_qo[:, :, 3 * COLS :]
+    b.grad_up[...] = b.in_sum_up[...]
+    b.grad_down[...] = b.in_sum_down[...]
+    for s in range(MEMBERS):
+        cols = slice(s * COLS, (s + 1) * COLS)
+        for l in range(2):
+            for ref, at, row in (
+                (b.grad_gain, 0, 0),
+                (b.grad_shift, 0, 1),
+                (b.grad_bias, 3, 2),
+                (b.grad_gain, 1, 3),
+                (b.grad_shift, 1, 4),
+                (b.grad_bias, 2, 5),
+                (b.grad_bias, 0, 16),
+                (b.grad_bias, 1, 17),
+            ):
+                ref[l, at : at + 1, cols] = b.in_vectors[s, row + 6 * l : row + 6 * l + 1]
+            for j in range(4):
+                to = s * HID + j * COLS
+                b.grad_up_bias[l : l + 1, to : to + COLS] = b.in_vectors[s, 18 + 6 * l + j : 19 + 6 * l + j]
 
 
 def scratch_table():
@@ -687,7 +715,6 @@
     add("narrow", (16, 128), F32)
     add("va", (MEMBERS, 16, 128), F32)
     add("vl", (MEMBERS, 16, 128), F32)
-    add("vectors", (MEMBERS, 32, 128), F32)
     add("qbias", (2, 384), F32)
     add("vb", (16, 32, 128), F32)
     add("piece", (32, 128), F32)
@@ -740,21 +767,19 @@
 
     def store_qo(l):
         def store(total):
-            for j in range(3):
-                b.grad_qkv[l, :, j, :] = total[:, j * COLS : (j + 1) * COLS]
-            b.grad_out[l] = total[:, 3 * COLS :].T
+            b.sum_qo[l] = total
 
         return store
 
     def store_up(l):
         def store(total):
-            b.grad_up[l] = total
+            b.sum_up[l] = total
 
         return store
 
     def store_down(l):
         def store(total):
-            b.grad_down[l] = total.T
+            b.sum_down[l] = total
 
         return store
 
@@ -772,13 +797,13 @@
     normed_one, normed_two, qkv, attended = (pair(n) for n in ("normed_one", "normed_two", "qkv", "attended"))
     slope, act, middle = (pair(n) for n in ("slope", "act", "middle"))
 
+    weights["qo", 0].start()
     swap_x = Swap(me, b.x_own, b.x_rows, both("swap"), 0)
     swap_x.start()
     swap_mask = Swap(me, b.mask_in, b.mask, both("swap"), 1)
     swap_mask.start()
     swap_cot = Swap(me, b.cot_own, b.cot_rows, both("swap"), 2)
     swap_x.end()
-    weights["qo", 0].start()
 
     def norm_rows(rows, l, i, out):
         out[me.slot] = layer_norm(rows, b.gain[l, i : i + 1], b.shift[l, i : i + 1]).astype(BF16)
@@ -828,7 +853,6 @@
     gather = Gather(me, normed_one[0], *both("rows"))
     gather.start()
     swap_mask.end()
-    gather.second()
     gather.relay()
     weights["qo", 0].arrived()
     swap_cot.start()
@@ -840,14 +864,10 @@
     gather_cot = Gather(me, b.g_rows, *both("cot"))
     gather_cot.start()
 
-    def cot_second():
-        gather_cot.second()
-        weights["down", 0].start()
-
     b.state[...] = forward(
         0,
         lambda: b.x_rows[...].astype(F32),
-        cot_second,
+        weights["down", 0].start,
         nothing,
         weights["qo", 1].start,
     )
@@ -940,7 +960,7 @@
     gather_g = Gather(me, b.g_rows, *both("cot"))
     gather_g.start()
     swap_out.end()
-    b.out_rows[...] = b.rows_home[...].astype(F32)[:ROWS].astype(BF16)
+    b.out_rows[...] = b.rows_home[...]
     backward(0, lambda: b.grad[...], gather_g, grads["up", 1].end, grads["qo", 1].end)
     b.grad[...] = first_back(0, lambda: b.x_rows[...].astype(F32), grads["down", 0].end)
     b.rows_away[...] = b.grad[...].astype(BF16)
@@ -952,32 +972,15 @@
             weights[name, l].sent()
     grads["up", 0].end()
     vectors_end(me, b.narrow, b.va, b.vl, *both("v1"), b.vb, b.piece, *both("v2"), b.vectors, *both("v3"))
-    for s in range(MEMBERS):
-        cols = slice(s * COLS, (s + 1) * COLS)
-        for l in range(2):
-            for ref, at, row in (
-                (b.grad_gain, 0, 0),
-                (b.grad_shift, 0, 1),
-                (b.grad_bias, 3, 2),
-                (b.grad_gain, 1, 3),
-                (b.grad_shift, 1, 4),
-                (b.grad_bias, 2, 5),
-                (b.grad_bias, 0, 16),
-                (b.grad_bias, 1, 17),
-            ):
-                ref[l, at : at + 1, cols] = b.vectors[s, row + 6 * l : row + 6 * l + 1]
-            for j in range(4):
-                to = s * HID + j * COLS
-                b.grad_up_bias[l : l + 1, to : to + COLS] = b.vectors[s, 18 + 6 * l + j : 19 + 6 * l + j]
     swap_grad.end()
 
     @pl.when(me.core == me.zlo)
     def _():
-        b.gradient[...] = b.grad[...][:ROWS]
+        b.gradient[...] = b.grad[...]
 
     @pl.when(me.core != me.zlo)
     def _():
-        b.gradient[...] = b.x_own[...].astype(F32)[:ROWS]
+        b.gradient[...] = b.x_own[...].astype(F32)
 
     grads["qo", 0].end()
 
@@ -997,7 +1000,7 @@
         [w_qkv.reshape(2, 64, 384), jnp.swapaxes(w_out, 1, 2), w_up, jnp.swapaxes(w_down, 1, 2)], axis=2
     )
     vmem = pl.BlockSpec(memory_space=pltpu.VMEM)
-    return pl.pallas_call(
+    arrays = pl.pallas_call(
         whole_kernel,
         out_shape=[jax.ShapeDtypeStruct(s, t) for s, t in OUTPUTS.values()],
         in_specs=[vmem] * len(INPUTS),
@@ -1007,6 +1010,16 @@
             collective_id=0, has_side_effects=True, vmem_limit_bytes=VMEM_BYTES
         ),
     )(x_in, cotangent, mask, shards, norm_gain, norm_shift, bias, up_bias)
+    results = list(pl.pallas_call(
+        result_kernel,
+        out_shape=[jax.ShapeDtypeStruct(s, t) for s, t in RESULTS.values()],
+        in_specs=[vmem] * len(OUTPUTS),
+        out_specs=[vmem] * len(RESULTS),
+    )(*arrays))
+    results[2] = jnp.swapaxes(results[2], 1, 2)
+    results[3] = jnp.swapaxes(results[3], 1, 2)
+    results[5] = jnp.swapaxes(results[5], 1, 2)
+    return tuple(results)
 
 
 def solution(mesh):

time: 341 us -> 322 us (0.944)
  Pallas kernels: 327 us -> 317 us
  local copies, waits for them, and re-layouts: 10.9 us -> 1.54 us
    pallas_call x1, Pallas kernels: 327 us -> 315 us  [per_device(): pl.pallas_call(whole_kernel, out_shape=[jax.ShapeDtypeStruct(s, t) for s,...]
    unnamed x27 -> x4, local copies, waits for them, and re-layouts: 5.15 us -> 0.01 us
    pallas_call x3 -> x0, local copies, waits for them, and re-layouts: 4.25 us -> none  [per_device(): pl.pallas_call(whole_kernel, out_shape=[jax.ShapeDtypeStruct(s, t) for s,...]
where the time goes in v5:
time: 322 us
  Pallas kernels  317 us (98%)
    pallas_call x1, Pallas kernels, per_device(): pl.pallas_call(whole_kernel, out_shape=[jax.ShapeDtypeStruct(s, t) for s,...  315 us

profile of v5, /device:TPU:1, one launch (start us, length us, event | category | flops | bytes accessed | tf_op | source)
XLA Modules:
  0.0 321.9 jit_solution(15287064006851461346)
XLA Ops:
  0.6 0.0 copy-start.1
  0.7 0.0 copy-start
  0.7 0.8 and_convert_fusion
  1.5 0.6 broadcast_in_dim.2.refs_2_
  2.1 0.9 copy_bitcast_fusion
  3.0 0.0 copy-done.1
  3.0 0.0 copy-done
  3.0 1.5 pad_maximum_fusion.refs_3_
  4.6 314.5 %shard_map.186 = (bf16[160,1024]{1,0:T(8,128)(2,1)}, f32[160,1024]{1,0:T(8,128)}, f32[2,64,512]{2,1,0:T(8,128)}, f32[2,64,512]{2,1,0:T(8,128)}, f32[2,64,512]{2,1,0:T(8,128)}, /*index=5*/f32[8,32,128]{2,1,0:T(8,128)}) custom-call(bf16[146,1024]{1,0:T(8,128)(2,1)} %refs_0_.1, bf16[146,1024]{1,0:T(8,128)(2,1)} %refs_1_.1, ...), custom_call_target="tpu_custom_call" | custom-call | tf_op jit(solution)/shard_map/pallas_call | solution.py:1003
  319.1 2.7 shard_map.187
  (2 shorter events, 0.0 us)
Async XLA Ops:
  0.6 2.4 copy-start.1
  0.7 2.4 copy-start

commit v6 on v5

--- a/solution.py
+++ b/solution.py
@@ -216,7 +216,10 @@
 ]
 
 
-def sum_rows(me, produce, send_bufs, land_bufs, fill=None):
+def sum_rows(me, produce, send_bufs, land_bufs, pending, fill=None):
+    for wait in pending:
+        wait()
+    pending.clear()
     s1, s2, acc, hold = send_bufs
     r1, ra, rb, ss1, rs1, ss2, rs2 = land_bufs
     sibling = me.sibling()
@@ -286,10 +289,14 @@
     for k in range(2, 6):
         along(k).wait_recv()
     total = acc[...] + rb[0].astype(F32) + rb[1].astype(F32)
-    for i in range(4):
-        to_sibling(i).wait_send()
-    for k in range(6):
-        along(k).wait_send()
+
+    def sent():
+        for i in range(4):
+            to_sibling(i).wait_send()
+        for k in range(6):
+            along(k).wait_send()
+
+    pending.append(sent)
     return total
 
 
@@ -763,7 +770,7 @@
         return [getattr(b, name + "0"), getattr(b, name + "1")]
 
     cuts = {"qo": pl.ds(0, 512), "up": pl.ds(512, 512), "down": pl.ds(1024, 512)}
-    weights, grads = {}, {}
+    weights, grads, pending = {}, {}, []
 
     def store_qo(l):
         def store(total):
@@ -824,7 +831,7 @@
         def out_product(slot):
             return dot(attended[l][slot], columns(w, 384, 128), NT)
 
-        branch = sum_rows(me, out_product, send_bufs, land[0])
+        branch = sum_rows(me, out_product, send_bufs, land[0], pending)
         middle[l][...] = state() + (branch + b.bias[l, 2:3])
         norm_rows(middle[l][...], l, 1, normed_two[l])
         gather = Gather(me, normed_two[l], *both("rows"))
@@ -845,7 +852,7 @@
         def down_product(slot):
             return dot(act[l][slot], columns(weights["down", l].full, 0, 512), NT)
 
-        total = sum_rows(me, down_product, send_bufs, land[1])
+        total = sum_rows(me, down_product, send_bufs, land[1], pending)
         gather.end()
         return middle[l][...] + (total + b.bias[l, 3:4])
 
@@ -858,7 +865,7 @@
     swap_cot.start()
     weights["up", 0].start()
     gather.run(project(0), relayed=True)
-    gather.end()
+    pending.append(gather.end)
     swap_cot.end()
     b.g_rows[me.slot] = b.cot_rows[...]
     gather_cot = Gather(me, b.g_rows, *both("cot"))
@@ -877,7 +884,7 @@
     weights["qo", 1].arrived()
     weights["up", 1].start()
     gather.run(project(1))
-    gather.end()
+    pending.append(gather.end)
     gather_cot.relay()
     b.rows_away[...] = forward(1, lambda: b.state[...], weights["down", 1].start, nothing, nothing).astype(BF16)
     swap_out = Swap(me, b.rows_away, b.rows_home, both("swap"), 3)
@@ -907,8 +914,8 @@
             narrow_sum(grad_hid, l * 6 + 2, 0, 4)
             after_down()
 
-        grad = sum_rows(me, up_back, send_bufs, land[0], fill)
-        gather_g.end()
+        grad = sum_rows(me, up_back, send_bufs, land[0], pending, fill)
+        pending.append(gather_g.end)
         back, gain_sum, shift_sum = layer_norm_back(middle[l][...], b.gain[l, 1:2], grad)
         mid = g_own() + back
         b.grad_mid[...] = mid
@@ -930,7 +937,7 @@
             b.grad_att[slot] = dot(b.g_attn[slot], columns(w, 384, 128)).astype(BF16)
 
         gather.run(att_back, fill_two)
-        gather.end()
+        pending.append(gather.end)
         attend_back(qkv[l], b.mask, b.grad_att)
 
     def first_back(l, rows, more):
@@ -948,7 +955,7 @@
             b.narrow[l * 6 : l * 6 + 1] = total[:, 0:128]
             b.narrow[l * 6 + 1 : l * 6 + 2] = total[:, 256:384]
 
-        grad = sum_rows(me, back_product, send_bufs, land[1], fill)
+        grad = sum_rows(me, back_product, send_bufs, land[1], pending, fill)
         back, gain_sum, shift_sum = layer_norm_back(rows(), b.gain[l, 0:1], grad)
         b.wide[l * 6 : l * 6 + 1] = gain_sum
         b.wide[l * 6 + 1 : l * 6 + 2] = shift_sum
@@ -983,6 +990,8 @@
         b.gradient[...] = b.x_own[...].astype(F32)
 
     grads["qo", 0].end()
+    for wait in pending:
+        wait()
 
 
 def nothing():

time: 322 us -> 321 us (level)
  no operation moved by 1% of the time
where the time goes in v6:
time: 321 us
  Pallas kernels  316 us (98%)
    pallas_call x1, Pallas kernels, per_device(): pl.pallas_call(whole_kernel, out_shape=[jax.ShapeDtypeStruct(s, t) for s,...  313 us

profile of v6, /device:TPU:1, one launch (start us, length us, event | category | flops | bytes accessed | tf_op | source)
XLA Modules:
  0.0 320.6 jit_solution(9812930509035277901)
XLA Ops:
  0.6 0.0 copy-start.1
  0.7 0.0 copy-start
  0.7 0.8 and_convert_fusion
  1.5 0.6 broadcast_in_dim.2.refs_2_
  2.1 0.9 copy_bitcast_fusion
  3.0 0.0 copy-done.1
  3.0 0.0 copy-done
  3.0 1.5 pad_maximum_fusion.refs_3_
  4.6 313.1 %shard_map.186 = (bf16[160,1024]{1,0:T(8,128)(2,1)}, f32[160,1024]{1,0:T(8,128)}, f32[2,64,512]{2,1,0:T(8,128)}, f32[2,64,512]{2,1,0:T(8,128)}, f32[2,64,512]{2,1,0:T(8,128)}, /*index=5*/f32[8,32,128]{2,1,0:T(8,128)}) custom-call(bf16[146,1024]{1,0:T(8,128)(2,1)} %refs_0_.1, bf16[146,1024]{1,0:T(8,128)(2,1)} %refs_1_.1, ...), custom_call_target="tpu_custom_call" | custom-call | tf_op jit(solution)/shard_map/pallas_call | solution.py:1012
  317.7 2.7 shard_map.187
  (2 shorter events, 0.0 us)
Async XLA Ops:
  0.6 2.4 copy-start.1
  0.7 2.4 copy-start
